TPU v7x, 32 devices: a whole 2x2x4 slice. The times are simulated.
32 devices in a mesh: groups: 2 (over y), expert: 4 (over z), dp: 2 (over x), sub: 2 (over core).
Axes of the slice: x: 2, y: 2, z: 4, core: 2. Of those that a mesh axis runs over, the one named last changes fastest.
Arguments:
- tokens: bfloat16 [2048, 2048], P(('groups', 'expert', 'dp')), parts along dimension 0, may hold values from -6 to 6
- cotangent: bfloat16 [2048, 2048], P(('groups', 'expert', 'dp')), parts along dimension 0, may hold values from -6 to 6
- route_ids: int32 [2048, 4], P(('groups', 'expert', 'dp')), parts along dimension 0, may hold values from 0 to 15, all different within a row; in each aligned block of 128 rows (0 to 127, 128 to 255, ...) at most 36 rows name the same one
- route_weights: float32 [2048, 4], P(('groups', 'expert', 'dp')), parts along dimension 0, may hold values from 0.05 to 0.5
- w_gate: bfloat16 [16, 2048, 768], P('expert', 'dp', 'sub'), may hold values from -0.125 to 0.125
- w_up: bfloat16 [16, 2048, 768], P('expert', 'dp', 'sub'), may hold values from -0.125 to 0.125
- v_down: bfloat16 [32, 768, 2048], P(('groups', 'expert'), 'sub', 'dp'), parts along dimension 0, may hold values from -0.125 to 0.125
Outputs:
- grad_down: bfloat16 [32, 768, 2048], P(('groups', 'expert'), 'sub', 'dp'), parts along dimension 0
- hyper_tokens: bfloat16 [2048, 2048], P(('groups', 'expert', 'dp'), 'sub'), parts along dimension 0
There are 2 independent parts, one for each index of `groups`. A program takes and returns all parts, laid end to end along the dimension named above; an argument that names none is the same for every part. Nothing has to cross between parts.
Inputs may be any that keep to these rules, and one draw needn't show every extreme that they name: `route_ids`: each token names 4 different experts. In the 128 rows of one token shard no expert is named by more than 36 tokens, a bound that some block reaches of them.
All inputs are finite; a program needn't handle non-finite values.
Results may differ from a plain program's by a relative error of at most 0.014.
Values may be sent and summed in bfloat16 or wider, within the bound.
No kernel may reach another device: no remote copies, remote signals or barrier semaphores. Data moves between devices by JAX's collectives and lax.ppermute only.
A program may use at most 128 MiB of HBM per device.

v0:
```python
import jax
import jax.numpy as jnp
from jax import lax
from jax.sharding import PartitionSpec as P


def slot_positions(chosen_ids, expert_count, capacity):
    flat_ids = chosen_ids.reshape(-1)
    onehot = (flat_ids[:, None] == jnp.arange(expert_count, dtype=jnp.int32)[None, :]).astype(
        jnp.int32
    )
    earlier = jnp.cumsum(onehot, axis=0) - onehot
    rank_in = jnp.sum(earlier * onehot, axis=1)
    return (flat_ids * capacity + rank_in).reshape(chosen_ids.shape)


def per_device(tokens, cotangent, route_ids, route_weights, w_gate, w_up, v_down):
    owners = lax.axis_size("expert")
    local_experts = w_gate.shape[0]
    expert_count = owners * local_experts
    token_count = route_ids.shape[0]
    chosen = route_ids.shape[1]
    model_width = tokens.shape[1]
    capacity = max(2, 9 * token_count * chosen // (8 * expert_count))
    slot_index = slot_positions(route_ids, expert_count, capacity)
    flat_slots = slot_index.reshape(-1)
    token_rows = jnp.repeat(jnp.arange(token_count, dtype=jnp.int32), chosen)
    source_rows = (
        jnp.full((expert_count * capacity,), token_count, jnp.int32).at[flat_slots].set(token_rows)
    )
    slot_scales = (
        jnp.zeros((expert_count * capacity,), jnp.float32)
        .at[flat_slots]
        .set(route_weights.reshape(-1))
    )
    padded_tokens = jnp.concatenate([tokens, jnp.zeros((1, model_width), tokens.dtype)], axis=0)
    padded_cotangent = jnp.concatenate(
        [cotangent, jnp.zeros((1, model_width), cotangent.dtype)], axis=0
    )
    send_tokens = padded_tokens[source_rows].reshape(owners, local_experts, capacity, model_width)
    send_cotangent = padded_cotangent[source_rows].reshape(
        owners, local_experts, capacity, model_width
    )
    send_scales = slot_scales.reshape(owners, local_experts, capacity)
    got_tokens, got_cotangent, got_scales = (
        lax.all_to_all(send_tokens, "expert", split_axis=0, concat_axis=2, tiled=True),
        lax.all_to_all(send_cotangent, "expert", split_axis=0, concat_axis=2, tiled=True),
        lax.all_to_all(
            send_scales.astype(jnp.bfloat16), "expert", split_axis=0, concat_axis=2, tiled=True
        ).astype(send_scales.dtype),
    )
    got_tokens = got_tokens[0]
    got_cotangent = got_cotangent[0]
    weighting = got_scales[0][:, :, None]
    full_gate, full_up, full_tangent = (
        lax.all_gather(w_gate, "dp", axis=1, tiled=True),
        lax.all_gather(w_up, "dp", axis=1, tiled=True),
        lax.all_gather(v_down, "dp", axis=2, tiled=True),
    )
    pre_gate = jnp.einsum("erd,edf->erf", got_tokens, full_gate, preferred_element_type=jnp.float32)
    pre_up = jnp.einsum("erd,edf->erf", got_tokens, full_up, preferred_element_type=jnp.float32)
    tangent = jnp.einsum(
        "erd,efd->erf", got_cotangent, full_tangent, preferred_element_type=jnp.float32
    )
    sigmoid_gate = jax.nn.sigmoid(pre_gate)
    activated = pre_gate * sigmoid_gate
    slope = sigmoid_gate * (1.0 + pre_gate * (1.0 - sigmoid_gate))
    weighted_hidden = (weighting * activated * pre_up).astype(jnp.bfloat16)
    grad_terms = jnp.einsum(
        "erf,erd->efd", weighted_hidden, got_cotangent, preferred_element_type=jnp.float32
    )
    grad_down = lax.psum_scatter(
        grad_terms.astype(jnp.bfloat16), "dp", scatter_dimension=2, tiled=True
    )
    scaled_tangent = weighting * tangent
    gate_adjoint = (scaled_tangent * pre_up * slope).astype(jnp.bfloat16)
    up_adjoint = (scaled_tangent * activated).astype(jnp.bfloat16)
    partial_value = jnp.einsum(
        "erf,edf->erd", gate_adjoint, full_gate, preferred_element_type=jnp.float32
    )
    partial_value = partial_value + jnp.einsum(
        "erf,edf->erd", up_adjoint, full_up, preferred_element_type=jnp.float32
    )
    returned = lax.all_to_all(
        partial_value[None].astype(jnp.bfloat16), "expert", split_axis=2, concat_axis=0, tiled=True
    ).astype(jnp.float32)
    pair_rows = returned.reshape(expert_count * capacity, model_width)[slot_index]
    hyper_tokens = lax.psum_scatter(
        jnp.sum(pair_rows, axis=1).astype(jnp.bfloat16), "sub", scatter_dimension=1, tiled=True
    )
    return (grad_down, hyper_tokens)


def solution(mesh):
    placed = (
        P(("groups", "expert", "dp"), None),
        P(("groups", "expert", "dp"), None),
        P(("groups", "expert", "dp"), None),
        P(("groups", "expert", "dp"), None),
        P("expert", "dp", "sub"),
        P("expert", "dp", "sub"),
        P(("groups", "expert"), "sub", "dp"),
    )
    return jax.shard_map(
        per_device,
        mesh=mesh,
        in_specs=placed,
        out_specs=(P(("groups", "expert"), "sub", "dp"), P(("groups", "expert", "dp"), "sub")),
        check_vma=False,
    )
```

profile of v0, /device:TPU:0, one launch (start us, length us, event | category | flops | bytes accessed | tf_op | source)
XLA Modules:
  0.0 455.4 jit_solution(5171316793175414946)
XLA Ops:
  7.2 0.7 all-gather.4.cloned.1.call-update
  8.0 0.7 all-gather.6.cloned.1.call-update
  8.7 0.1 copy.39
  8.8 0.1 eq.29
  8.9 0.1 eq.25
  9.0 1.2 reduce-window.6
  10.2 0.2 slice_reduce_fusion
  10.4 0.1 fusion.19
  10.5 0.1 reduce_sum.24
  10.7 0.1 mul.57
  10.8 0.1 copy.43
  10.9 0.1 reshape.124
  11.0 2.4 scatter_custom_fusion
  13.5 0.7 convert_element_type.68
  14.2 6.3 %all-to-all-start = ((bf16[4,4,36]{2,1,0:T(4,128)(2,1)}), bf16[4,4,36]{2,1,0:T(4,128)(2,1)S(1)}, u32[]{:S(2)}, u32[]{:S(2)}) async-start(bf16[4,4,36]{2,1,0:T(4,128)(2,1)} %convert_element_type.68), calls=%async_computation | async-start | bytes 8192 | tf_op jit(solution)/shard_map/all_to_all | solution.py:48
  20.5 0.1 reshape.132
  20.6 2.4 scatter_custom_fusion.1
  23.2 4.0 gather_fusion
  27.1 2.7 reshape.90
  29.8 3.2 copy.45
  33.1 5.2 %all-to-all-start.1 = ((bf16[4,4,36,2048]{3,1,2,0:T(4,128)(2,1)}), bf16[4,4,36,2048]{3,1,2,0:T(4,128)(2,1)S(1)}, u32[]{:S(2)}, u32[]{:S(2)}) async-start(bf16[4,4,36,2048]{3,1,2,0:T(4,128)(2,1)} %copy.45), calls=%async_computation.1 | async-start | bytes 4718592 | tf_op jit(solution)/shard_map/all_to_all | solution.py:46
  38.3 0.7 all-gather.8.cloned.1.call-update
  39.1 4.0 gather_fusion.1
  43.1 4.1 reshape.91
  47.2 5.0 %copy.48 = bf16[4,4,36,2048]{3,1,2,0:T(4,128)(2,1)} copy(bf16[4,4,36,2048]{3,2,1,0:T(8,128)(2,1)} %reshape.91) | data formatting | bytes 4718592 | tf_op jit(solution)/shard_map/reshape | solution.py:41
  52.2 39.4 %all-to-all-done.1 = bf16[4,4,36,2048]{3,1,2,0:T(4,128)(2,1)S(1)} async-done(((bf16[4,4,36,2048]{3,1,2,0:T(4,128)(2,1)}), bf16[4,4,36,2048]{3,1,2,0:T(4,128)(2,1)S(1)}, u32[]{:S(2)}, u32[]{:S(2)}) %all-to-all-start.1) | async-done | bytes 2359328 | tf_op jit(solution)/shard_map/all_to_all | solution.py:46
  91.6 4.7 %all-to-all-start.2 = ((bf16[4,4,36,2048]{3,1,2,0:T(4,128)(2,1)}), bf16[4,4,36,2048]{3,1,2,0:T(4,128)(2,1)}, u32[]{:S(2)}, u32[]{:S(2)}) async-start(bf16[4,4,36,2048]{3,1,2,0:T(4,128)(2,1)} %copy.48), calls=%async_computation.2 | async-start | bytes 4718592 | tf_op jit(solution)/shard_map/all_to_all | solution.py:47
  96.3 0.1 reshape.92
  96.4 7.1 %fusion.6 = f32[4,144,384]{2,1,0:T(8,128)} fusion(bf16[4,2048,384]{2,1,0:T(8,128)(2,1)} %all-gather.4.cloned.1.call-done, bf16[4,144,2048]{2,0,1:T(4,128)(2,1)S(1)} %bitcast.53), kind=kOutput, calls=%fused_computation.14 | convolution fusion | flops 905969664 | bytes 9535488 | tf_op jit(solution)/shard_map/erd,edf->erf/dot_general | solution.py:60
  103.5 71.1 %all-gather.6.cloned.1.call-done = bf16[4,2048,384]{2,1,0:T(8,128)(2,1)} async-done(((bf16[4,1024,384]{2,1,0:T(8,128)(2,1)}), bf16[4,2048,384]{2,1,0:T(8,128)(2,1)}) %all-gather.6.cloned.1.call-update) | async-done | bytes 6291472 | tf_op jit(solution)/shard_map/all_gather | solution.py:57
  174.6 7.8 %fusion.4 = f32[4,144,384]{2,1,0:T(8,128)} fusion(bf16[4,2048,384]{2,1,0:T(8,128)(2,1)} %all-gather.6.cloned.1.call-done, bf16[4,144,2048]{2,0,1:T(4,128)(2,1)} %bitcast.54), kind=kOutput, calls=%fused_computation.12 | convolution fusion | flops 905969664 | bytes 9535488 | tf_op jit(solution)/shard_map/erd,edf->erf/dot_general | solution.py:61
  182.5 74.1 %all-gather.8.cloned.1.call-done = bf16[4,384,2048]{2,1,0:T(8,128)(2,1)} async-done(((bf16[4,384,1024]{2,1,0:T(8,128)(2,1)}), bf16[4,384,2048]{2,1,0:T(8,128)(2,1)}) %all-gather.8.cloned.1.call-update) | async-done | bytes 6291472 | tf_op jit(solution)/shard_map/all_gather | solution.py:58
  256.6 7.1 %fusion.8 = f32[4,144,384]{2,1,0:T(8,128)S(1)} fusion(bf16[4,384,2048]{2,1,0:T(8,128)(2,1)} %all-gather.8.cloned.1.call-done, bf16[4,144,2048]{2,0,1:T(4,128)(2,1)} %bitcast.12, f32[4,144]{1,0:T(4,128)S(1)} %reshape.92), kind=kOutput, calls=%fused_computation.16 | convolution fusion | flops 906190848 | bytes 9537792 | tf_op jit(solution)/shard_map/erd,efd->erf/dot_general | solution.py:62
  263.8 3.5 fusion.12
  267.3 2.4 fusion
  269.7 3.2 copy.51
  272.9 4.6 %all-to-all-start.3 = ((bf16[1,4,144,2048]{3,1,0,2:T(4,128)(2,1)}), bf16[1,4,144,2048]{3,1,0,2:T(4,128)(2,1)S(1)}, u32[]{:S(2)}, u32[]{:S(2)}) async-start(bf16[1,4,144,2048]{3,1,0,2:T(4,128)(2,1)} %copy.51), calls=%async_computation.4 | async-start | bytes 4718592 | tf_op jit(solution)/shard_map/all_to_all | solution.py:84
  277.5 0.1 reshape.114
  277.6 53.7 %all-to-all-done.3 = bf16[1,4,144,2048]{3,1,0,2:T(4,128)(2,1)S(1)} async-done(((bf16[1,4,144,2048]{3,1,0,2:T(4,128)(2,1)}), bf16[1,4,144,2048]{3,1,0,2:T(4,128)(2,1)S(1)}, u32[]{:S(2)}, u32[]{:S(2)}) %all-to-all-start.3) | async-done | bytes 2359328 | tf_op jit(solution)/shard_map/all_to_all | solution.py:84
  331.3 0.7 convert_bitcast_fusion
  332.0 5.1 %copy.52 = f32[4,1,4,36,2048]{4,3,2,0,1:T(8,128)} copy(f32[4,1,4,36,2048]{4,2,3,0,1:T(4,128)S(1)} %convert_bitcast_fusion) | data formatting | bytes 9437184 | tf_op jit(solution)/shard_map/convert_element_type | solution.py:86
  337.1 5.3 %reshape.93 = f32[576,2048]{1,0:T(8,128)} reshape(f32[4,1,4,36,2048]{4,3,2,0,1:T(8,128)} %copy.52) | data formatting | bytes 9437184 | tf_op jit(solution)/shard_map/convert_element_type | solution.py:86
  342.4 7.7 %gather_fusion.2 = f32[512,2048]{1,0:T(8,128)} fusion(f32[576,2048]{1,0:T(8,128)} %reshape.93, s32[1024]{0:T(1024)S(1)} %pad_clamp_fusion), kind=kCustom, calls=%fused_computation.2 | custom fusion | bytes 8390656 | tf_op jit(solution)/shard_map/gather | solution.py:87
  350.1 5.2 %reshape.117 = f32[128,4,2048]{2,1,0:T(4,128)} reshape(f32[512,2048]{1,0:T(8,128)} %gather_fusion.2) | data formatting | bytes 8388608 | tf_op jit(solution)/shard_map/gather | solution.py:87
  355.3 5.8 %reduce_sum.25 = bf16[128,2048]{1,0:T(8,128)(2,1)} reduce(f32[128,4,2048]{2,1,0:T(4,128)} %reshape.117, f32[]{:T(128)} %constant.8.clone.1), dimensions={1}, to_apply=%region_6.7 | reduce | flops 786432 | bytes 4718596 | tf_op jit(solution)/shard_map/reduce_sum | solution.py:89
  361.1 0.3 reduce-scatter.3.cloned.1.call-start
  361.4 8.0 %convolution_convert_fusion = bf16[4,384,2048]{2,1,0:T(8,128)(2,1)} fusion(bf16[4,144,2048]{2,0,1:T(4,128)(2,1)} %bitcast.12, f32[4,144,384]{2,1,0:T(8,128)S(1)} %copy-done.2, f32[4,144]{1,0:T(4,128)S(1)} %reshape.92, f32[4,144,384]{2,1,0:T(8,128)S(1)} %copy-done.1), kind=kOutput, calls=%fused_computation.7 | convolution fusion | flops 910663680 | bytes 10422528 | tf_op jit(solution)/shard_map/erf,erd->efd/dot_general | solution.py:69
  369.5 78.9 %reduce-scatter.3.cloned.1.call-done = bf16[4,384,1024]{2,1,0:T(8,128)(2,1)} async-done(((bf16[4,384,2048]{2,1,0:T(8,128)(2,1)}), bf16[4,384,1024]{2,1,0:T(8,128)(2,1)}) %reduce-scatter.3.cloned.1.call-update) | async-done | bytes 3145744 | tf_op jit(solution)/shard_map/reduce_scatter | solution.py:72
  (48 shorter events, 0.4 us)
Async XLA Ops:
  7.2 1.5 copy-start.5
  7.2 3.6 copy-start.6
  7.2 15.9 %copy-start.3 = (bf16[128,2048]{1,0:T(8,128)(2,1)S(1)}, bf16[128,2048]{1,0:T(8,128)(2,1)}, u32[]{:S(2)}) copy-start(bf16[128,2048]{1,0:T(8,128)(2,1)} %param.7) | copy-start | bytes 1572868
  7.2 89.2 %all-gather.4.cloned.1.call-start = ((), (), s32[]{:S(2)}) async-start(), calls=%async_computation.6 | async-start | bytes 9437184 | tf_op jit(solution)/shard_map/all_gather | solution.py:56
  7.9 166.7 %all-gather.6.cloned.1.call-start = ((), (), s32[]{:S(2)}) async-start(), calls=%async_computation.7 | async-start | bytes 9437184 | tf_op jit(solution)/shard_map/all_gather | solution.py:57
  14.2 18.9 %all-to-all-start = ((bf16[4,4,36]{2,1,0:T(4,128)(2,1)}), bf16[4,4,36]{2,1,0:T(4,128)(2,1)S(1)}, u32[]{:S(2)}, u32[]{:S(2)}) async-start(bf16[4,4,36]{2,1,0:T(4,128)(2,1)} %convert_element_type.68), calls=%async_computation | async-start | bytes 8192 | tf_op jit(solution)/shard_map/all_to_all | solution.py:48
  33.1 6.0 %copy-start.4 = (bf16[128,2048]{1,0:T(8,128)(2,1)S(1)}, bf16[128,2048]{1,0:T(8,128)(2,1)}, u32[]{:S(2)}) copy-start(bf16[128,2048]{1,0:T(8,128)(2,1)} %param.8) | copy-start | bytes 1572868
  33.1 58.5 %all-to-all-start.1 = ((bf16[4,4,36,2048]{3,1,2,0:T(4,128)(2,1)}), bf16[4,4,36,2048]{3,1,2,0:T(4,128)(2,1)S(1)}, u32[]{:S(2)}, u32[]{:S(2)}) async-start(bf16[4,4,36,2048]{3,1,2,0:T(4,128)(2,1)} %copy.45), calls=%async_computation.1 | async-start | bytes 4718592 | tf_op jit(solution)/shard_map/all_to_all | solution.py:46
  38.3 218.3 %all-gather.8.cloned.1.call-start = ((), (), s32[]{:S(2)}) async-start(), calls=%async_computation.9 | async-start | bytes 9437184 | tf_op jit(solution)/shard_map/all_gather | solution.py:58
  91.6 11.9 %copy-start = (bf16[4,4,36,2048]{3,1,2,0:T(4,128)(2,1)}, bf16[4,4,36,2048]{3,1,2,0:T(4,128)(2,1)S(1)}, u32[]{:S(2)}) copy-start(bf16[4,4,36,2048]{3,1,2,0:T(4,128)(2,1)S(1)} %all-to-all-done.1) | copy-start | bytes 7077892
  91.6 90.9 %all-to-all-start.2 = ((bf16[4,4,36,2048]{3,1,2,0:T(4,128)(2,1)}), bf16[4,4,36,2048]{3,1,2,0:T(4,128)(2,1)}, u32[]{:S(2)}, u32[]{:S(2)}) async-start(bf16[4,4,36,2048]{3,1,2,0:T(4,128)(2,1)} %copy.48), calls=%async_computation.2 | async-start | bytes 4718592 | tf_op jit(solution)/shard_map/all_to_all | solution.py:47
  174.6 89.1 %slice-start = ((s8[6291456]{0:T(1024)(128)(4,1)}), s8[2097152]{0:T(1024)(128)(4,1)S(1)}, s32[]{:S(2)}) async-start(s8[6291456]{0:T(1024)(128)(4,1)} %bitcast.49), calls=%async_computation.11 | async-start | bytes 4194304
  256.6 7.1 %slice-start.1 = ((s8[6291456]{0:T(1024)(128)(4,1)}), s8[4194304]{0:T(1024)(128)(4,1)S(1)}, s32[]{:S(2)}) async-start(s8[6291456]{0:T(1024)(128)(4,1)} %bitcast.49), calls=%async_computation.12 | async-start | bytes 8388608
  256.6 7.1 %copy-start.1 = (f32[4,144,384]{2,1,0:T(8,128)S(1)}, f32[4,144,384]{2,1,0:T(8,128)}, u32[]{:S(2)}) copy-start(f32[4,144,384]{2,1,0:T(8,128)} %fusion.6) | copy-start | bytes 2654212
  256.6 10.6 %slice-start.2 = ((s8[6291456]{0:T(1024)(128)(4,1)}), s8[4194304]{0:T(1024)(128)(4,1)S(1)}, s32[]{:S(2)}) async-start(s8[6291456]{0:T(1024)(128)(4,1)} %bitcast.51), calls=%async_computation.13 | async-start | bytes 8388608
  263.8 3.5 slice-start.3
  272.9 58.4 %all-to-all-start.3 = ((bf16[1,4,144,2048]{3,1,0,2:T(4,128)(2,1)}), bf16[1,4,144,2048]{3,1,0,2:T(4,128)(2,1)S(1)}, u32[]{:S(2)}, u32[]{:S(2)}) async-start(bf16[1,4,144,2048]{3,1,0,2:T(4,128)(2,1)} %copy.51), calls=%async_computation.4 | async-start | bytes 4718592 | tf_op jit(solution)/shard_map/all_to_all | solution.py:84
  277.5 92.0 %reduce-scatter.5.cloned.1.call-start = ((), (), s32[]{:S(2)}) async-start(), calls=%async_computation.10 | async-start | bytes 786432 | tf_op jit(solution)/shard_map/reduce_scatter | solution.py:88
  355.3 6.1 %copy-start.2 = (f32[4,144,384]{2,1,0:T(8,128)S(1)}, f32[4,144,384]{2,1,0:T(8,128)}, u32[]{:S(2)}) copy-start(f32[4,144,384]{2,1,0:T(8,128)} %fusion.4) | copy-start | bytes 2654212
  361.1 87.3 %reduce-scatter.3.cloned.1.call-start = ((), (), s32[]{:S(2)}) async-start(), calls=%async_computation.8 | async-start | bytes 9437184 | tf_op jit(solution)/shard_map/reduce_scatter | solution.py:72
Sparse Core Ops, SparseCore 0:
  9.6 83.0 all-gather.3
  94.2 80.3 all-gather.5
  176.2 80.3 all-gather.7
  361.2 6.0 reduce-scatter.4
  370.2 78.1 reduce-scatter.2
where the time goes:
time: 463 us; the launch traced here: 455 us
  waiting for transfers between devices  319 us (69%)
  local copies, waits for them, and re-layouts  56.5 us (12%)
  matrix products  36 us (8%)
  starting transfers between devices  21.2 us (5%)
  between operations  14.5 us (3%)
  other arithmetic  7.85 us (2%)
    reduce_scatter x1, waiting for transfers between devices, per_device(): lax.psum_scatter(grad_terms.astype(jnp.bfloat16), 'dp', scatter_dimension...  78.9 us
    all_gather x1, waiting for transfers between devices, per_device(): lax.all_gather(v_down, 'dp', axis=2, tiled=True)  74.1 us
    all_gather x1, waiting for transfers between devices, per_device(): lax.all_gather(w_up, 'dp', axis=1, tiled=True)  71.1 us
    all_to_all x1, waiting for transfers between devices, per_device(): lax.all_to_all(partial_value[None].astype(jnp.bfloat16), 'expert', split_...  53.7 us
    all_to_all x1, waiting for transfers between devices, per_device(): lax.all_to_all(send_tokens, 'expert', split_axis=0, concat_axis=2, tiled=...  39.4 us
    gather x2, local copies, waits for them, and re-layouts, per_device(): returned.reshape(expert_count * capacity, model_width)[slot_index]  12.9 us
    convert_element_type x2, local copies, waits for them, and re-layouts, per_device(): returned = lax.all_to_all(partial_value[None].astype(jnp.bfloat16), 'expe...  10.3 us
  transfers between devices with their start and end apart: 9, of which 5 were waited for; matrix products, arithmetic and copies ran while one was open for 12% of the time, Pallas kernels for 0%

commit v1 on v0

v1 whole, which is shorter than its diff:
```python
import functools

import jax
import jax.numpy as jnp
from jax import lax
from jax.experimental import pallas as pl
from jax.experimental.pallas import tpu as pltpu
from jax.sharding import PartitionSpec as P

BF = jnp.bfloat16
F32 = jnp.float32
LANES = 128
VMEM_LIMIT = 48 * 1024 * 1024


def up_to(value, step):
    return -(-value // step) * step


def dot(a, b, contract=((1,), (0,))):
    return lax.dot_general(a, b, (contract, ((), ())), preferred_element_type=F32)


def vmem_spec(shape):
    return pl.BlockSpec(shape, lambda j: (0,) * len(shape))


def expert_spec(shape):
    return pl.BlockSpec((1,) + shape, lambda j: (j,) + (0,) * len(shape))


def route_tables(payload, token_rows, chosen, first_expert, local_experts, tables):
    shards = payload.shape[0]
    width = token_rows // LANES
    per_row = payload.shape[2] // LANES

    def entry(index):
        pieces = []
        for shard in range(shards):
            for piece in range(width):
                row, column = divmod(index * width + piece, per_row)
                pieces.append(
                    payload[shard, token_rows:, :].astype(F32)[
                        row : row + 1, column * LANES : (column + 1) * LANES
                    ]
                )
        return jnp.concatenate(pieces, axis=1)

    ids = [entry(k) for k in range(chosen)]
    weights = [
        entry(chosen + k) + entry(2 * chosen + k) + entry(3 * chosen + k) for k in range(chosen)
    ]
    total = shards * token_rows
    masks, scales = [], []
    for local in range(local_experts):
        wanted = (first_expert + local).astype(F32)
        hits = [(one == wanted).astype(F32) for one in ids]
        masks.append(sum(hits))
        scales.append(sum(hit * weight for hit, weight in zip(hits, weights)))
    pad = [jnp.zeros((8 - local_experts, total), F32)] if local_experts < 8 else []
    mask = jnp.concatenate(masks + pad, axis=0)
    before = lax.broadcasted_iota(jnp.int32, (total, total), 0) < lax.broadcasted_iota(
        jnp.int32, (total, total), 1
    )
    rank = dot(mask.astype(BF), before.astype(F32).astype(BF))
    tables[0:8, :] = jnp.where(mask > 0.5, rank, -1.0)
    tables[8:16, :] = jnp.concatenate(scales + pad, axis=0)


def one_hot(tables, local, slots):
    rank = tables[pl.ds(local, 1), :].astype(jnp.int32)
    total = rank.shape[1]
    return lax.broadcasted_iota(jnp.int32, (slots, total), 0) == rank


def forward_kernel(
    token_rows, chosen, capacity, place, mine, other, gate, up, down, sums, cot_rows, tables,
    token_scratch, sum_scratch,
):
    local = pl.program_id(0)
    shards = mine.shape[0]
    quarter = mine.shape[2] // 2
    slots = token_scratch.shape[0]

    @pl.when(local == 0)
    def _():
        route_tables(mine, token_rows, chosen, place[1], pl.num_programs(0), tables)

    hot = one_hot(tables, local, slots).astype(F32).astype(BF)
    for source, which in ((mine, place[0]), (other, 1 - place[0])):
        rows = source[:, 0:token_rows, :].reshape(shards * token_rows, 2 * quarter)
        picked = dot(hot, rows).astype(BF)
        columns = pl.ds(pl.multiple_of(which * quarter, LANES), quarter)
        token_scratch[:, columns] = picked[:, :quarter]
        cot_rows[0, :, columns] = picked[:, quarter:]
    here = pl.ds(pl.multiple_of(local * capacity, 8), capacity)
    sum_scratch[0, here, :] = dot(token_scratch[...], gate[0])[:capacity]
    sum_scratch[1, here, :] = dot(token_scratch[...], up[0])[:capacity]
    sum_scratch[2, here, :] = dot(cot_rows[0], down[0], ((1,), (1,)))[:capacity]

    @pl.when(local == pl.num_programs(0) - 1)
    def _():
        sums[...] = sum_scratch[...].astype(BF)


def backward_kernel(capacity, place, tables, *refs):
    *sums, gate, up, hidden, keep, send, full, total = refs
    local = pl.program_id(0)
    rows = sums[0].shape[1]
    slots = hidden.shape[1]
    quarter = keep.shape[1]

    @pl.when(local == 0)
    def _():
        full[:, 0:rows, :] = sum(one[...].astype(F32) for one in sums)
        full[:, rows:, :] = jnp.zeros((3, full.shape[1] - rows, full.shape[2]), F32)
        total[...] = jnp.zeros_like(total)

    hot = one_hot(tables, local, slots).astype(F32)
    scale = jnp.sum(hot * tables[pl.ds(8 + local, 1), :], axis=1, keepdims=True)
    here = pl.ds(pl.multiple_of(local * capacity, 8), slots)
    pre_gate, pre_up, tangent = full[0, here, :], full[1, here, :], full[2, here, :]
    sigmoid_gate = jax.nn.sigmoid(pre_gate)
    act = pre_gate * sigmoid_gate
    slope = sigmoid_gate * (1.0 + pre_gate * (1.0 - sigmoid_gate))
    hidden[0] = (scale * act * pre_up).astype(BF)
    scaled = scale * tangent
    gate_adjoint = (scaled * pre_up * slope).astype(BF)
    up_adjoint = (scaled * act).astype(BF)
    hot = hot.astype(BF)
    gate_tokens = dot(hot, gate_adjoint, ((0,), (0,))).astype(BF)
    up_tokens = dot(hot, up_adjoint, ((0,), (0,))).astype(BF)
    total[...] += dot(gate_tokens, gate[0], ((1,), (1,))) + dot(up_tokens, up[0], ((1,), (1,)))

    @pl.when(local == pl.num_programs(0) - 1)
    def _():
        for out, which in ((keep, place[0]), (send, 1 - place[0])):
            out[...] = total[:, pl.ds(pl.multiple_of(which * quarter, LANES), quarter)].astype(BF)


def grad_kernel(*refs):
    *inputs, out = refs
    half = len(inputs) // 2
    hidden = jnp.concatenate([one[0] for one in inputs[:half]], axis=0)
    cot_rows = jnp.concatenate([one[0] for one in inputs[half:]], axis=0)
    out[0] = dot(hidden, cot_rows, ((0,), (0,))).astype(BF)


def params():
    return pltpu.CompilerParams(
        vmem_limit_bytes=VMEM_LIMIT, dimension_semantics=("arbitrary",)
    )


SMEM = pl.BlockSpec(memory_space=pltpu.SMEM)


def forward(place, mine, other, gate, up, down, token_rows, chosen, capacity):
    local_experts, depth, hidden = gate.shape
    slots = up_to(capacity, 16)
    rows = local_experts * capacity
    tokens = mine.shape[0] * token_rows
    return pl.pallas_call(
        functools.partial(forward_kernel, token_rows, chosen, capacity),
        grid=(local_experts,),
        in_specs=[
            SMEM,
            vmem_spec(mine.shape),
            vmem_spec(other.shape),
            expert_spec((depth, hidden)),
            expert_spec((depth, hidden)),
            expert_spec((hidden, depth)),
        ],
        out_specs=[
            vmem_spec((3, rows, hidden)),
            expert_spec((slots, depth)),
            vmem_spec((16, tokens)),
        ],
        out_shape=[
            jax.ShapeDtypeStruct((3, rows, hidden), BF),
            jax.ShapeDtypeStruct((local_experts, slots, depth), BF),
            jax.ShapeDtypeStruct((16, tokens), F32),
        ],
        scratch_shapes=[pltpu.VMEM((slots, depth), BF), pltpu.VMEM((3, rows, hidden), F32)],
        compiler_params=params(),
        cost_estimate=pl.CostEstimate(
            flops=2 * local_experts * slots * depth * (3 * hidden + 2 * tokens),
            bytes_accessed=2 * (3 * gate.size + 2 * mine.size + 3 * rows * hidden),
            transcendentals=0,
        ),
    )(place, mine, other, gate, up, down)


def backward(place, tables, sums, gate, up, capacity):
    local_experts, depth, hidden = gate.shape
    slots = up_to(capacity, 16)
    tokens = tables.shape[1]
    return pl.pallas_call(
        functools.partial(backward_kernel, capacity),
        grid=(local_experts,),
        in_specs=[SMEM, vmem_spec(tables.shape)]
        + [vmem_spec(one.shape) for one in sums]
        + [expert_spec((depth, hidden))] * 2,
        out_specs=[
            expert_spec((slots, hidden)),
            vmem_spec((tokens, depth // 2)),
            vmem_spec((tokens, depth // 2)),
        ],
        out_shape=[
            jax.ShapeDtypeStruct((local_experts, slots, hidden), BF),
            jax.ShapeDtypeStruct((tokens, depth // 2), BF),
            jax.ShapeDtypeStruct((tokens, depth // 2), BF),
        ],
        scratch_shapes=[
            pltpu.VMEM((3, sums[0].shape[1] + slots - capacity + 8, hidden), F32),
            pltpu.VMEM((tokens, depth), F32),
        ],
        compiler_params=params(),
        cost_estimate=pl.CostEstimate(
            flops=4 * local_experts * tokens * hidden * (depth + slots),
            bytes_accessed=2 * (2 * gate.size + 6 * sums[0].size),
            transcendentals=sums[0].size,
        ),
    )(place, tables, *sums, gate, up)


def grads(hiddens, cots):
    local_experts, slots, hidden = hiddens[0].shape
    depth = cots[0].shape[2]
    return pl.pallas_call(
        grad_kernel,
        grid=(local_experts,),
        in_specs=[expert_spec((slots, hidden))] * len(hiddens)
        + [expert_spec((slots, depth))] * len(cots),
        out_specs=expert_spec((hidden, depth)),
        out_shape=jax.ShapeDtypeStruct((local_experts, hidden, depth), BF),
        compiler_params=params(),
        cost_estimate=pl.CostEstimate(
            flops=2 * local_experts * slots * len(cots) * hidden * depth,
            bytes_accessed=2 * local_experts * (hidden * depth + len(cots) * slots * depth),
            transcendentals=0,
        ),
    )(*hiddens, *cots)


def shift(array, axis, by):
    size = lax.axis_size(axis)
    return lax.ppermute(array, axis, [(i, (i + by) % size) for i in range(size)])


def per_device(tokens, cotangent, route_ids, route_weights, w_gate, w_up, v_down):
    owners, wide, cores = (lax.axis_size(a) for a in ("expert", "dp", "sub"))
    owner, dp, sub = (lax.axis_index(a) for a in ("expert", "dp", "sub"))
    token_rows, chosen = route_ids.shape
    local_experts = w_gate.shape[0]
    expert_count = owners * local_experts
    most = max(2, 9 * token_rows * chosen // (8 * expert_count))
    capacity = up_to(wide * most, 8)
    quarter = tokens.shape[1] // (wide * cores)
    place = jnp.stack([sub, owner * local_experts]).astype(jnp.int32)

    parts, rest = [], route_weights
    for _ in range(3):
        part = lax.reduce_precision(rest, 8, 7)
        parts.append(part)
        rest = rest - part
    routing = jnp.concatenate([route_ids.astype(F32)] + parts, axis=1).astype(BF).T
    routing = routing.reshape(-1)
    routing = jnp.pad(routing, (0, -routing.shape[0] % (4 * quarter))).reshape(-1, 2 * quarter)

    def payload(to):
        start = (to * cores + sub) * quarter
        body = jnp.concatenate(
            [lax.dynamic_slice_in_dim(a, start, quarter, 1) for a in (tokens, cotangent)], axis=1
        )
        return jnp.concatenate([body, routing], axis=0)[None]

    mine = jnp.zeros((wide, token_rows + routing.shape[0], 2 * quarter), BF)
    mine = lax.dynamic_update_slice_in_dim(mine, payload(dp), dp, 0)
    for by in range(1, wide):
        got = shift(payload((dp + by) % wide), "dp", by)
        mine = lax.dynamic_update_slice_in_dim(mine, got, (dp - by) % wide, 0)

    order = sorted(range(owners), key=lambda by: min(by, owners - by))
    blocks = [mine if by == 0 else shift(mine, "expert", by) for by in order]
    total, hiddens, cots = None, [], []
    for by, block in zip(order, blocks):
        other = shift(block, "sub", 1)
        sums, cot_rows, tables = forward(
            place, block, other, w_gate, w_up, v_down, token_rows, chosen, capacity
        )
        everyone = [sums] + [shift(sums, "dp", step) for step in range(1, wide)]
        hidden, keep, send = backward(place, tables, everyone, w_gate, w_up, capacity)
        hiddens.append(hidden)
        cots.append(cot_rows)
        rows = keep.astype(F32) + shift(send, "sub", 1).astype(F32)
        if by:
            rows = shift(rows.astype(BF), "expert", -by).astype(F32)
        total = rows if total is None else total + rows
    grad_down = grads(hiddens, cots)

    total = total.astype(BF).reshape(wide, token_rows, quarter)
    pieces = jnp.zeros_like(total)
    pieces = lax.dynamic_update_slice_in_dim(
        pieces, lax.dynamic_slice_in_dim(total, dp, 1, 0), dp, 0
    )
    for by in range(1, wide):
        got = shift(lax.dynamic_slice_in_dim(total, (dp + by) % wide, 1, 0), "dp", by)
        pieces = lax.dynamic_update_slice_in_dim(pieces, got, (dp - by) % wide, 0)
    span = wide // cores
    stay = lax.dynamic_slice_in_dim(pieces, sub * span, span, 0)
    come = shift(lax.dynamic_slice_in_dim(pieces, (1 - sub) * span, span, 0), "sub", 1)
    columns = []
    for index in range(span):
        columns.append(jnp.where(sub == 0, stay[index], come[index]))
        columns.append(jnp.where(sub == 0, come[index], stay[index]))
    return (grad_down, jnp.concatenate(columns, axis=1))


def solution(mesh):
    placed = (
        P(("groups", "expert", "dp"), None),
        P(("groups", "expert", "dp"), None),
        P(("groups", "expert", "dp"), None),
        P(("groups", "expert", "dp"), None),
        P("expert", "dp", "sub"),
        P("expert", "dp", "sub"),
        P(("groups", "expert"), "sub", "dp"),
    )
    return jax.shard_map(
        per_device,
        mesh=mesh,
        in_specs=placed,
        out_specs=(P(("groups", "expert"), "sub", "dp"), P(("groups", "expert", "dp"), "sub")),
        check_vma=False,
    )
```

time: 463 us -> 183 us (0.40)
  the two profiles are of different devices: /device:TPU:0 before, /device:TPU:15 now
where the time goes in v1:
time: 183 us; the launch traced here: 182 us
  waiting for transfers between devices  59.1 us (32%)
  Pallas kernels  49.6 us (27%)
  starting transfers between devices  47.4 us (26%)
  local copies, waits for them, and re-layouts  16.7 us (9%)
  other arithmetic  7.78 us (4%)
    ppermute x21, waiting for transfers between devices, shift(): lax.ppermute(array, axis, [(i, (i + by) % size) for i in range(size)])  59.1 us
    ppermute x21, starting transfers between devices, shift(): lax.ppermute(array, axis, [(i, (i + by) % size) for i in range(size)])  47.4 us
    pallas_call x4, Pallas kernels, forward(): pl.pallas_call(functools.partial(forward_kernel, token_rows, chosen, capa...  23.1 us
    pallas_call x4, Pallas kernels, backward(): pl.pallas_call(functools.partial(backward_kernel, capacity), grid=(local_...  22.9 us
    ppermute x7, local copies, waits for them, and re-layouts, shift(): lax.ppermute(array, axis, [(i, (i + by) % size) for i in range(size)])  7.09 us
    unnamed x38, local copies, waits for them, and re-layouts  5.34 us
  transfers between devices with their start and end apart: 21, of which 9 were waited for; matrix products, arithmetic and copies ran while one was open for 5% of the time, Pallas kernels for 27%

profile of v1, /device:TPU:15, one launch (start us, length us, event | category | flops | bytes accessed | tf_op | source)
XLA Modules:
  0.0 181.6 jit_solution(15104775976868168310)
XLA Ops:
  0.7 0.8 reduce-precision_convert_fusion.1
  2.3 1.1 constant_dynamic-slice_fusion.2
  4.5 7.5 %collective-permute-done = bf16[1,130,1024]{2,1,0:T(8,128)(2,1)} collective-permute-done((bf16[1,130,1024]{2,1,0:T(8,128)(2,1)}, bf16[1,130,1024]{2,1,0:T(8,128)(2,1)}, u32[]{:S(2)}, u32[]{:S(2)}) %collective-permute-start) | collective-permute-done | bytes 266272 | tf_op jit(solution)/shard_map/ppermute | solution.py:248
  12.0 1.0 constant_dynamic-update-slice_fusion.1.mine
  13.0 1.4 copy.9
  14.4 0.8 copy-done.1
  15.3 2.3 %collective-permute-start.9 = (bf16[2,130,1024]{2,0,1:T(2,128)(2,1)}, bf16[2,130,1024]{2,0,1:T(2,128)(2,1)}, u32[]{:S(2)}, u32[]{:S(2)}) collective-permute-start(bf16[2,130,1024]{2,0,1:T(2,128)(2,1)} %copy.9), channel_id=1, source_target_pairs={{0,8},{4,12},{8,0},{12,4},{1,9},{5,13},{9,1},{13,5},{2,10},{6,14},... | collective-permute-start | bytes 1597448 | tf_op jit(solution)/shard_map/ppermute | solution.py:248
  17.7 2.2 %collective-permute-start.3 = (bf16[2,130,1024]{2,0,1:T(2,128)(2,1)}, bf16[2,130,1024]{2,0,1:T(2,128)(2,1)}, u32[]{:S(2)}, u32[]{:S(2)}) collective-permute-start(bf16[2,130,1024]{2,0,1:T(2,128)(2,1)} %copy.9), channel_id=1, source_target_pairs={{0,4},{4,8},{8,12},{12,0},{1,5},{5,9},{9,13},{13,1},{2,6},{6,10},{... | collective-permute-start | bytes 1597448 | tf_op jit(solution)/shard_map/ppermute | solution.py:248
  19.8 2.4 %collective-permute-start.1 = (bf16[2,130,1024]{2,0,1:T(2,128)(2,1)}, bf16[2,130,1024]{2,0,1:T(2,128)(2,1)}, u32[]{:S(2)}, u32[]{:S(2)}) collective-permute-start(bf16[2,130,1024]{2,0,1:T(2,128)(2,1)} %copy.9), channel_id=1, source_target_pairs={{0,1},{1,0},{2,3},{3,2},{4,5},{5,4},{6,7},{7,6},{8,9},{9,8},{10,11... | collective-permute-start | bytes 1597448 | tf_op jit(solution)/shard_map/ppermute | solution.py:248
  22.2 5.3 %collective-permute-done.6 = bf16[2,130,1024]{2,0,1:T(2,128)(2,1)} collective-permute-done((bf16[2,130,1024]{2,0,1:T(2,128)(2,1)}, bf16[2,130,1024]{2,0,1:T(2,128)(2,1)}, u32[]{:S(2)}, u32[]{:S(2)}) %collective-permute-start.6) | collective-permute-done | bytes 532512 | tf_op jit(solution)/shard_map/ppermute | solution.py:248
  27.5 27.4 %collective-permute-start.7 = (bf16[2,130,1024]{2,0,1:T(2,128)(2,1)}, bf16[2,130,1024]{2,0,1:T(2,128)(2,1)}, u32[]{:S(2)}, u32[]{:S(2)}) collective-permute-start(bf16[2,130,1024]{2,0,1:T(2,128)(2,1)} %collective-permute-done.6), channel_id=1, source_target_pairs={{0,1},{1,0},{2,3},{3,2},{4,5},{5,4},{6,7},{7,6},{8,9},{9,8},{10,11... | collective-permute-start | bytes 1597448 | tf_op jit(solution)/shard_map/ppermute | solution.py:248
  54.9 8.4 %collective-permute-done.3 = bf16[2,130,1024]{2,0,1:T(2,128)(2,1)} collective-permute-done((bf16[2,130,1024]{2,0,1:T(2,128)(2,1)}, bf16[2,130,1024]{2,0,1:T(2,128)(2,1)}, u32[]{:S(2)}, u32[]{:S(2)}) %collective-permute-start.3) | collective-permute-done | bytes 532512 | tf_op jit(solution)/shard_map/ppermute | solution.py:248
  63.3 1.3 collective-permute-start.4
  64.6 1.2 copy.10.other
  65.8 1.0 copy-done.2
  66.9 5.8 %shard_map.86 = (bf16[3,288,384]{2,1,0:T(8,128)(2,1)S(1)}, bf16[4,80,1024]{2,1,0:T(8,128)(2,1)S(1)}, f32[16,256]{1,0:T(8,128)S(1)}) custom-call(s32[2]{0:T(128)S(1)} %pad_add_fusion.place, bf16[2,130,1024]{2,1,0:T(8,128)(2,1)S(1)} %copy-done.2, bf16[2,130,1024]{2,1,0:T(8,128)(2,1)S(1)} %copy.10.other, bf16[4,1024,384]{2,1,0:T(8,128)(2,1)S(1)} %copy-done, ...), custom_call_target="tpu_custom_call" | custom-call | flops 1090519040 | bytes 11165696 | tf_op jit(solution)/shard_map/pallas_call | solution.py:163
  73.0 1.2 copy.15.mine
  74.2 1.2 copy.16.other
  75.3 5.8 %shard_map.90 = (bf16[3,288,384]{2,1,0:T(8,128)(2,1)S(1)}, bf16[4,80,1024]{2,1,0:T(8,128)(2,1)S(1)}, f32[16,256]{1,0:T(8,128)S(1)}) custom-call(s32[2]{0:T(128)S(1)} %pad_add_fusion.place, bf16[2,130,1024]{2,1,0:T(8,128)(2,1)S(1)} %copy.15.mine, bf16[2,130,1024]{2,1,0:T(8,128)(2,1)S(1)} %copy.16.other, bf16[4,1024,384]{2,1,0:T(8,128)(2,1)S(1)} %copy-done, ...), custom_call_target="tpu_custom_call" | custom-call | flops 1090519040 | bytes 11165696 | tf_op jit(solution)/shard_map/pallas_call | solution.py:163
  81.2 1.3 collective-permute-start.8
  82.4 1.2 copy.18.mine
  83.6 1.2 copy.19.other
  84.8 5.8 %shard_map.92 = (bf16[3,288,384]{2,1,0:T(8,128)(2,1)S(1)}, bf16[4,80,1024]{2,1,0:T(8,128)(2,1)S(1)}, f32[16,256]{1,0:T(8,128)S(1)}) custom-call(s32[2]{0:T(128)S(1)} %pad_add_fusion.place, bf16[2,130,1024]{2,1,0:T(8,128)(2,1)S(1)} %copy.18.mine, bf16[2,130,1024]{2,1,0:T(8,128)(2,1)S(1)} %copy.19.other, bf16[4,1024,384]{2,1,0:T(8,128)(2,1)S(1)} %copy-done, ...), custom_call_target="tpu_custom_call" | custom-call | flops 1090519040 | bytes 11165696 | tf_op jit(solution)/shard_map/pallas_call | solution.py:163
  90.9 1.2 copy.12.mine
  92.2 5.8 %shard_map.88 = (bf16[3,288,384]{2,1,0:T(8,128)(2,1)S(1)}, bf16[4,80,1024]{2,1,0:T(8,128)(2,1)S(1)}, f32[16,256]{1,0:T(8,128)S(1)}) custom-call(s32[2]{0:T(128)S(1)} %pad_add_fusion.place, bf16[2,130,1024]{2,1,0:T(8,128)(2,1)S(1)} %copy.12.mine, bf16[2,130,1024]{2,1,0:T(8,128)(2,1)S(1)} %copy.13.other, bf16[4,1024,384]{2,1,0:T(8,128)(2,1)S(1)} %copy-done, ...), custom_call_target="tpu_custom_call" | custom-call | flops 1090519040 | bytes 11165696 | tf_op jit(solution)/shard_map/pallas_call | solution.py:163
  98.0 0.8 copy-done.9
  98.9 1.2 collective-permute-start.5
  100.1 6.2 %shard_map.87 = (bf16[4,80,384]{2,1,0:T(8,128)(2,1)S(1)}, bf16[256,512]{1,0:T(8,128)(2,1)S(1)}, bf16[256,512]{1,0:T(8,128)(2,1)}) custom-call(s32[2]{0:T(128)S(1)} %pad_add_fusion.place, f32[16,256]{1,0:T(8,128)S(1)} %get-tuple-element.26.tables, bf16[3,288,384]{2,1,0:T(8,128)(2,1)S(1)} %get-tuple-element.27.refs_0_, ...), custom_call_target="tpu_custom_call" | custom-call | flops 1736441856 | bytes 10272768 | tf_op jit(solution)/shard_map/pallas_call | solution.py:198
  107.0 1.1 collective-permute-start.12
  108.2 5.5 %shard_map.91 = (bf16[4,80,384]{2,1,0:T(8,128)(2,1)S(1)}, bf16[256,512]{1,0:T(8,128)(2,1)S(1)}, bf16[256,512]{1,0:T(8,128)(2,1)S(1)}) custom-call(s32[2]{0:T(128)S(1)} %pad_add_fusion.place, f32[16,256]{1,0:T(8,128)S(1)} %get-tuple-element.32.tables, bf16[3,288,384]{2,1,0:T(8,128)(2,1)S(1)} %get-tuple-element.33.refs_0_, ...), custom_call_target="tpu_custom_call" | custom-call | flops 1736441856 | bytes 10272768 | tf_op jit(solution)/shard_map/pallas_call | solution.py:198
  113.8 3.9 %collective-permute-done.11.refs_1_ = bf16[3,288,384]{2,1,0:T(8,128)(2,1)S(1)} collective-permute-done((bf16[3,288,384]{2,1,0:T(8,128)(2,1)S(1)}, bf16[3,288,384]{2,1,0:T(8,128)(2,1)S(1)}, u32[]{:S(2)}, u32[]{:S(2)}) %collective-permute-start.11) | collective-permute-done | bytes 663584 | tf_op jit(solution)/shard_map/ppermute | solution.py:248
  117.7 5.5 %shard_map.93 = (bf16[4,80,384]{2,1,0:T(8,128)(2,1)S(1)}, bf16[256,512]{1,0:T(8,128)(2,1)S(1)}, bf16[256,512]{1,0:T(8,128)(2,1)S(1)}) custom-call(s32[2]{0:T(128)S(1)} %pad_add_fusion.place, f32[16,256]{1,0:T(8,128)S(1)} %get-tuple-element.35.tables, bf16[3,288,384]{2,1,0:T(8,128)(2,1)S(1)} %get-tuple-element.36.refs_0_, ...), custom_call_target="tpu_custom_call" | custom-call | flops 1736441856 | bytes 10272768 | tf_op jit(solution)/shard_map/pallas_call | solution.py:198
  123.3 1.2 collective-permute-start.17
  124.5 7.4 %collective-permute-done.5.refs_1_ = bf16[3,288,384]{2,1,0:T(8,128)(2,1)S(1)} collective-permute-done((bf16[3,288,384]{2,1,0:T(8,128)(2,1)S(1)}, bf16[3,288,384]{2,1,0:T(8,128)(2,1)S(1)}, u32[]{:S(2)}, u32[]{:S(2)}) %collective-permute-start.5) | collective-permute-done | bytes 663584 | tf_op jit(solution)/shard_map/ppermute | solution.py:248
  131.9 5.6 %shard_map.89 = (bf16[4,80,384]{2,1,0:T(8,128)(2,1)S(1)}, bf16[256,512]{1,0:T(8,128)(2,1)S(1)}, bf16[256,512]{1,0:T(8,128)(2,1)S(1)}) custom-call(s32[2]{0:T(128)S(1)} %pad_add_fusion.place, f32[16,256]{1,0:T(8,128)S(1)} %get-tuple-element.29.tables, bf16[3,288,384]{2,1,0:T(8,128)(2,1)S(1)} %get-tuple-element.30.refs_0_, ...), custom_call_target="tpu_custom_call" | custom-call | flops 1736441856 | bytes 10272768 | tf_op jit(solution)/shard_map/pallas_call | solution.py:198
  137.6 0.8 collective-permute-start.13
  138.5 0.8 add_convert_fusion.2
  139.2 2.2 %collective-permute-start.16 = (bf16[256,512]{1,0:T(8,128)(2,1)}, bf16[256,512]{1,0:T(8,128)(2,1)}, u32[]{:S(2)}, u32[]{:S(2)}) collective-permute-start(bf16[256,512]{1,0:T(8,128)(2,1)} %add_convert_fusion.2), channel_id=1, source_target_pairs={{0,4},{4,8},{8,12},{12,0},{1,5},{5,9},{9,13},{13,1},{2,6},{6,10},{... | collective-permute-start | bytes 786440 | tf_op jit(solution)/shard_map/ppermute | solution.py:248
  144.2 14.4 %collective-permute-done.16 = bf16[256,512]{1,0:T(8,128)(2,1)} collective-permute-done((bf16[256,512]{1,0:T(8,128)(2,1)}, bf16[256,512]{1,0:T(8,128)(2,1)}, u32[]{:S(2)}, u32[]{:S(2)}) %collective-permute-start.16) | collective-permute-done | bytes 262176 | tf_op jit(solution)/shard_map/ppermute | solution.py:248
  158.6 5.8 %collective-permute-done.18 = bf16[256,512]{1,0:T(8,128)(2,1)} collective-permute-done((bf16[256,512]{1,0:T(8,128)(2,1)}, bf16[256,512]{1,0:T(8,128)(2,1)}, u32[]{:S(2)}, u32[]{:S(2)}) %collective-permute-start.18) | collective-permute-done | bytes 262176 | tf_op jit(solution)/shard_map/ppermute | solution.py:248
  164.3 1.9 %collective-permute-done.14 = bf16[256,512]{1,0:T(8,128)(2,1)} collective-permute-done((bf16[256,512]{1,0:T(8,128)(2,1)}, bf16[256,512]{1,0:T(8,128)(2,1)}, u32[]{:S(2)}, u32[]{:S(2)}) %collective-permute-start.14) | collective-permute-done | bytes 262176 | tf_op jit(solution)/shard_map/ppermute | solution.py:248
  166.2 1.4 add_convert_fusion
  168.5 4.6 %collective-permute-done.19 = bf16[1,128,512]{2,1,0:T(8,128)(2,1)S(1)} collective-permute-done((bf16[1,128,512]{2,1,0:T(8,128)(2,1)}, bf16[1,128,512]{2,1,0:T(8,128)(2,1)S(1)}, u32[]{:S(2)}, u32[]{:S(2)}) %collective-permute-start.19) | collective-permute-done | bytes 131104 | tf_op jit(solution)/shard_map/ppermute | solution.py:248
  173.1 1.4 collective-permute-start.20
  174.5 0.9 copy-done.16
  175.5 0.9 copy-done.18
  176.4 3.6 %shard_map.94 = bf16[4,384,1024]{2,1,0:T(8,128)(2,1)} custom-call(bf16[4,80,384]{2,1,0:T(8,128)(2,1)S(1)} %copy-done.12, bf16[4,80,384]{2,1,0:T(8,128)(2,1)S(1)} %copy-done.18, bf16[4,80,384]{2,1,0:T(8,128)(2,1)S(1)} %copy-done.14, bf16[4,80,384]{2,1,0:T(8,128)(2,1)S(1)} %copy-done.16, bf16[4,80,1024]{2,1,0:T(8,128)(2,1)S(1)} %copy-done.4, ...), custom_call_target="tpu_custom_call" | custom-call | flops 1006632960 | bytes 5767168 | tf_op jit(solution)/shard_map/pallas_call | solution.py:230
  180.0 0.9 select_bitcast_fusion.1
  (69 shorter events, 8.2 us)
Async XLA Ops:
  0.6 65.2 %copy-start = (bf16[4,1024,384]{2,1,0:T(8,128)(2,1)S(1)}, bf16[4,1024,384]{2,1,0:T(8,128)(2,1)}, u32[]{:S(2)}) copy-start(bf16[4,1024,384]{2,1,0:T(8,128)(2,1)} %refs_2_.7) | copy-start | bytes 9437188
  4.2 7.8 %collective-permute-start = (bf16[1,130,1024]{2,1,0:T(8,128)(2,1)}, bf16[1,130,1024]{2,1,0:T(8,128)(2,1)}, u32[]{:S(2)}, u32[]{:S(2)}) collective-permute-start(bf16[1,130,1024]{2,1,0:T(8,128)(2,1)} %fusion.2), channel_id=1, source_target_pairs={{0,2},{2,0},{1,3},{3,1},{4,6},{6,4},{5,7},{7,5},{8,10},{10,8},{9,1... | collective-permute-start | bytes 798728 | tf_op jit(solution)/shard_map/ppermute | solution.py:248
  14.4 0.8 copy-start.1
  15.2 12.4 %collective-permute-start.6 = (bf16[2,130,1024]{2,0,1:T(2,128)(2,1)}, bf16[2,130,1024]{2,0,1:T(2,128)(2,1)}, u32[]{:S(2)}, u32[]{:S(2)}) collective-permute-start(bf16[2,130,1024]{2,0,1:T(2,128)(2,1)} %copy.9), channel_id=1, source_target_pairs={{0,12},{4,0},{8,4},{12,8},{1,13},{5,1},{9,5},{13,9},{2,14},{6,2},{... | collective-permute-start | bytes 1597448 | tf_op jit(solution)/shard_map/ppermute | solution.py:248
  15.3 39.6 %collective-permute-start.9 = (bf16[2,130,1024]{2,0,1:T(2,128)(2,1)}, bf16[2,130,1024]{2,0,1:T(2,128)(2,1)}, u32[]{:S(2)}, u32[]{:S(2)}) collective-permute-start(bf16[2,130,1024]{2,0,1:T(2,128)(2,1)} %copy.9), channel_id=1, source_target_pairs={{0,8},{4,12},{8,0},{12,4},{1,9},{5,13},{9,1},{13,5},{2,10},{6,14},... | collective-permute-start | bytes 1597448 | tf_op jit(solution)/shard_map/ppermute | solution.py:248
  17.7 45.6 %collective-permute-start.3 = (bf16[2,130,1024]{2,0,1:T(2,128)(2,1)}, bf16[2,130,1024]{2,0,1:T(2,128)(2,1)}, u32[]{:S(2)}, u32[]{:S(2)}) collective-permute-start(bf16[2,130,1024]{2,0,1:T(2,128)(2,1)} %copy.9), channel_id=1, source_target_pairs={{0,4},{4,8},{8,12},{12,0},{1,5},{5,9},{9,13},{13,1},{2,6},{6,10},{... | collective-permute-start | bytes 1597448 | tf_op jit(solution)/shard_map/ppermute | solution.py:248
  19.8 44.8 %collective-permute-start.1 = (bf16[2,130,1024]{2,0,1:T(2,128)(2,1)}, bf16[2,130,1024]{2,0,1:T(2,128)(2,1)}, u32[]{:S(2)}, u32[]{:S(2)}) collective-permute-start(bf16[2,130,1024]{2,0,1:T(2,128)(2,1)} %copy.9), channel_id=1, source_target_pairs={{0,1},{1,0},{2,3},{3,2},{4,5},{5,4},{6,7},{7,6},{8,9},{9,8},{10,11... | collective-permute-start | bytes 1597448 | tf_op jit(solution)/shard_map/ppermute | solution.py:248
  27.5 46.6 %collective-permute-start.7 = (bf16[2,130,1024]{2,0,1:T(2,128)(2,1)}, bf16[2,130,1024]{2,0,1:T(2,128)(2,1)}, u32[]{:S(2)}, u32[]{:S(2)}) collective-permute-start(bf16[2,130,1024]{2,0,1:T(2,128)(2,1)} %collective-permute-done.6), channel_id=1, source_target_pairs={{0,1},{1,0},{2,3},{3,2},{4,5},{5,4},{6,7},{7,6},{8,9},{9,8},{10,11... | collective-permute-start | bytes 1597448 | tf_op jit(solution)/shard_map/ppermute | solution.py:248
  54.9 28.7 %collective-permute-start.10 = (bf16[2,130,1024]{2,0,1:T(2,128)(2,1)}, bf16[2,130,1024]{2,0,1:T(2,128)(2,1)}, u32[]{:S(2)}, u32[]{:S(2)}) collective-permute-start(bf16[2,130,1024]{2,0,1:T(2,128)(2,1)} %collective-permute-done.9), channel_id=1, source_target_pairs={{0,1},{1,0},{2,3},{3,2},{4,5},{5,4},{6,7},{7,6},{8,9},{9,8},{10,11... | collective-permute-start | bytes 1597448 | tf_op jit(solution)/shard_map/ppermute | solution.py:248
  63.3 28.8 %collective-permute-start.4 = (bf16[2,130,1024]{2,0,1:T(2,128)(2,1)}, bf16[2,130,1024]{2,0,1:T(2,128)(2,1)S(1)}, u32[]{:S(2)}, u32[]{:S(2)}) collective-permute-start(bf16[2,130,1024]{2,0,1:T(2,128)(2,1)} %collective-permute-done.3), channel_id=1, source_target_pairs={{0,1},{1,0},{2,3},{3,2},{4,5},{5,4},{6,7},{7,6},{8,9},{9,8},{10,11... | collective-permute-start | bytes 1597448 | tf_op jit(solution)/shard_map/ppermute | solution.py:248
  65.8 1.1 copy-start.2
  72.7 1.5 copy-start.3
  72.7 27.4 %collective-permute-start.2 = (bf16[3,288,384]{2,1,0:T(8,128)(2,1)S(1)}, bf16[3,288,384]{2,1,0:T(8,128)(2,1)S(1)}, u32[]{:S(2)}, u32[]{:S(2)}) collective-permute-start(bf16[3,288,384]{2,1,0:T(8,128)(2,1)S(1)} %get-tuple-element.27.refs_0_), channel_id=1, source_target_pairs={{0,2},{2,0},{1,3},{3,1},{4,6},{6,4},{5,7},{7,5},{8,10},{10,8},{9,1... | collective-permute-start | bytes 1990664 | tf_op jit(solution)/shard_map/ppermute | solution.py:248
  81.1 2.5 %copy-start.5 = (bf16[4,80,1024]{2,1,0:T(8,128)(2,1)}, bf16[4,80,1024]{2,1,0:T(8,128)(2,1)S(1)}, u32[]{:S(2)}) copy-start(bf16[4,80,1024]{2,1,0:T(8,128)(2,1)S(1)} %get-tuple-element.40.refs_6_) | copy-start | bytes 1966084
  81.2 27.0 %collective-permute-start.8 = (bf16[3,288,384]{2,1,0:T(8,128)(2,1)S(1)}, bf16[3,288,384]{2,1,0:T(8,128)(2,1)S(1)}, u32[]{:S(2)}, u32[]{:S(2)}) collective-permute-start(bf16[3,288,384]{2,1,0:T(8,128)(2,1)S(1)} %get-tuple-element.33.refs_0_), channel_id=1, source_target_pairs={{0,2},{2,0},{1,3},{3,1},{4,6},{6,4},{5,7},{7,5},{8,10},{10,8},{9,1... | collective-permute-start | bytes 1990664 | tf_op jit(solution)/shard_map/ppermute | solution.py:248
  90.6 1.5 copy-start.7
  90.6 27.1 %collective-permute-start.11 = (bf16[3,288,384]{2,1,0:T(8,128)(2,1)S(1)}, bf16[3,288,384]{2,1,0:T(8,128)(2,1)S(1)}, u32[]{:S(2)}, u32[]{:S(2)}) collective-permute-start(bf16[3,288,384]{2,1,0:T(8,128)(2,1)S(1)} %get-tuple-element.36.refs_0_), channel_id=1, source_target_pairs={{0,2},{2,0},{1,3},{3,1},{4,6},{6,4},{5,7},{7,5},{8,10},{10,8},{9,1... | collective-permute-start | bytes 1990664 | tf_op jit(solution)/shard_map/ppermute | solution.py:248
  98.0 0.8 copy-start.9
  98.9 33.1 %collective-permute-start.5 = (bf16[3,288,384]{2,1,0:T(8,128)(2,1)S(1)}, bf16[3,288,384]{2,1,0:T(8,128)(2,1)S(1)}, u32[]{:S(2)}, u32[]{:S(2)}) collective-permute-start(bf16[3,288,384]{2,1,0:T(8,128)(2,1)S(1)} %get-tuple-element.30.refs_0_), channel_id=1, source_target_pairs={{0,2},{2,0},{1,3},{3,1},{4,6},{6,4},{5,7},{7,5},{8,10},{10,8},{9,1... | collective-permute-start | bytes 1990664 | tf_op jit(solution)/shard_map/ppermute | solution.py:248
  106.3 0.7 copy-start.11
  107.0 37.1 %collective-permute-start.12 = (bf16[256,512]{1,0:T(8,128)(2,1)}, bf16[256,512]{1,0:T(8,128)(2,1)}, u32[]{:S(2)}, u32[]{:S(2)}) collective-permute-start(bf16[256,512]{1,0:T(8,128)(2,1)} %get-tuple-element.43), channel_id=1, source_target_pairs={{0,1},{1,0},{2,3},{3,2},{4,5},{5,4},{6,7},{7,6},{8,9},{9,8},{10,11... | collective-permute-start | bytes 786440 | tf_op jit(solution)/shard_map/ppermute | solution.py:248
  113.7 9.6 %copy-start.13 = (bf16[4,80,384]{2,1,0:T(8,128)(2,1)}, bf16[4,80,384]{2,1,0:T(8,128)(2,1)S(1)}, u32[]{:S(2)}) copy-start(bf16[4,80,384]{2,1,0:T(8,128)(2,1)S(1)} %get-tuple-element.34.refs_2_) | copy-start | bytes 737284
  113.7 24.7 %collective-permute-start.15 = (bf16[256,512]{1,0:T(8,128)(2,1)S(1)}, bf16[256,512]{1,0:T(8,128)(2,1)S(1)}, u32[]{:S(2)}, u32[]{:S(2)}) collective-permute-start(bf16[256,512]{1,0:T(8,128)(2,1)S(1)} %get-tuple-element.47), channel_id=1, source_target_pairs={{0,1},{1,0},{2,3},{3,2},{4,5},{5,4},{6,7},{7,6},{8,9},{9,8},{10,11... | collective-permute-start | bytes 786440 | tf_op jit(solution)/shard_map/ppermute | solution.py:248
  123.3 14.2 %copy-start.15 = (bf16[4,80,384]{2,1,0:T(8,128)(2,1)}, bf16[4,80,384]{2,1,0:T(8,128)(2,1)S(1)}, u32[]{:S(2)}) copy-start(bf16[4,80,384]{2,1,0:T(8,128)(2,1)S(1)} %get-tuple-element.37.refs_3_) | copy-start | bytes 737284
  123.3 18.2 %collective-permute-start.17 = (bf16[256,512]{1,0:T(8,128)(2,1)S(1)}, bf16[256,512]{1,0:T(8,128)(2,1)S(1)}, u32[]{:S(2)}, u32[]{:S(2)}) collective-permute-start(bf16[256,512]{1,0:T(8,128)(2,1)S(1)} %get-tuple-element.49), channel_id=1, source_target_pairs={{0,1},{1,0},{2,3},{3,2},{4,5},{5,4},{6,7},{7,6},{8,9},{9,8},{10,11... | collective-permute-start | bytes 786440 | tf_op jit(solution)/shard_map/ppermute | solution.py:248
  137.5 6.2 %copy-start.17 = (bf16[4,80,384]{2,1,0:T(8,128)(2,1)}, bf16[4,80,384]{2,1,0:T(8,128)(2,1)S(1)}, u32[]{:S(2)}) copy-start(bf16[4,80,384]{2,1,0:T(8,128)(2,1)S(1)} %get-tuple-element.31.refs_1_) | copy-start | bytes 737284
  137.5 37.0 %copy-start.4 = (bf16[4,80,1024]{2,1,0:T(8,128)(2,1)S(1)}, bf16[4,80,1024]{2,1,0:T(8,128)(2,1)}, u32[]{:S(2)}) copy-start(bf16[4,80,1024]{2,1,0:T(8,128)(2,1)} %copy-done.3) | copy-start | bytes 1966084
  137.6 36.9 %copy-start.6 = (bf16[4,80,1024]{2,1,0:T(8,128)(2,1)S(1)}, bf16[4,80,1024]{2,1,0:T(8,128)(2,1)}, u32[]{:S(2)}) copy-start(bf16[4,80,1024]{2,1,0:T(8,128)(2,1)} %copy-done.5) | copy-start | bytes 1966084
  137.6 36.9 %copy-start.8 = (bf16[4,80,1024]{2,1,0:T(8,128)(2,1)S(1)}, bf16[4,80,1024]{2,1,0:T(8,128)(2,1)}, u32[]{:S(2)}) copy-start(bf16[4,80,1024]{2,1,0:T(8,128)(2,1)} %copy-done.7) | copy-start | bytes 1966084
  137.6 36.9 %copy-start.10 = (bf16[4,80,1024]{2,1,0:T(8,128)(2,1)S(1)}, bf16[4,80,1024]{2,1,0:T(8,128)(2,1)}, u32[]{:S(2)}) copy-start(bf16[4,80,1024]{2,1,0:T(8,128)(2,1)} %copy-done.9) | copy-start | bytes 1966084
  137.6 36.9 %copy-start.12 = (bf16[4,80,384]{2,1,0:T(8,128)(2,1)S(1)}, bf16[4,80,384]{2,1,0:T(8,128)(2,1)}, u32[]{:S(2)}) copy-start(bf16[4,80,384]{2,1,0:T(8,128)(2,1)} %copy-done.11) | copy-start | bytes 737284
  137.6 36.9 %copy-start.14 = (bf16[4,80,384]{2,1,0:T(8,128)(2,1)S(1)}, bf16[4,80,384]{2,1,0:T(8,128)(2,1)}, u32[]{:S(2)}) copy-start(bf16[4,80,384]{2,1,0:T(8,128)(2,1)} %copy-done.13) | copy-start | bytes 737284
  137.6 5.3 %collective-permute-start.13 = (bf16[256,512]{1,0:T(8,128)(2,1)S(1)}, bf16[256,512]{1,0:T(8,128)(2,1)S(1)}, u32[]{:S(2)}, u32[]{:S(2)}) collective-permute-start(bf16[256,512]{1,0:T(8,128)(2,1)S(1)} %get-tuple-element.45), channel_id=1, source_target_pairs={{0,1},{1,0},{2,3},{3,2},{4,5},{5,4},{6,7},{7,6},{8,9},{9,8},{10,11... | collective-permute-start | bytes 786440 | tf_op jit(solution)/shard_map/ppermute | solution.py:248
  139.2 19.3 %collective-permute-start.16 = (bf16[256,512]{1,0:T(8,128)(2,1)}, bf16[256,512]{1,0:T(8,128)(2,1)}, u32[]{:S(2)}, u32[]{:S(2)}) collective-permute-start(bf16[256,512]{1,0:T(8,128)(2,1)} %add_convert_fusion.2), channel_id=1, source_target_pairs={{0,4},{4,8},{8,12},{12,0},{1,5},{5,9},{9,13},{13,1},{2,6},{6,10},{... | collective-permute-start | bytes 786440 | tf_op jit(solution)/shard_map/ppermute | solution.py:248
  142.2 22.1 %collective-permute-start.18 = (bf16[256,512]{1,0:T(8,128)(2,1)}, bf16[256,512]{1,0:T(8,128)(2,1)}, u32[]{:S(2)}, u32[]{:S(2)}) collective-permute-start(bf16[256,512]{1,0:T(8,128)(2,1)} %add_convert_fusion.1), channel_id=1, source_target_pairs={{0,8},{4,12},{8,0},{12,4},{1,9},{5,13},{9,1},{13,5},{2,10},{6,14},... | collective-permute-start | bytes 786440 | tf_op jit(solution)/shard_map/ppermute | solution.py:248
  143.7 22.5 %collective-permute-start.14 = (bf16[256,512]{1,0:T(8,128)(2,1)}, bf16[256,512]{1,0:T(8,128)(2,1)}, u32[]{:S(2)}, u32[]{:S(2)}) collective-permute-start(bf16[256,512]{1,0:T(8,128)(2,1)} %add_convert_fusion.3), channel_id=1, source_target_pairs={{0,12},{4,0},{8,4},{12,8},{1,13},{5,1},{9,5},{13,9},{2,14},{6,2},{... | collective-permute-start | bytes 786440 | tf_op jit(solution)/shard_map/ppermute | solution.py:248
  168.3 4.8 %collective-permute-start.19 = (bf16[1,128,512]{2,1,0:T(8,128)(2,1)}, bf16[1,128,512]{2,1,0:T(8,128)(2,1)S(1)}, u32[]{:S(2)}, u32[]{:S(2)}) collective-permute-start(bf16[1,128,512]{2,1,0:T(8,128)(2,1)} %get-tuple-element.56), channel_id=1, source_target_pairs={{0,2},{2,0},{1,3},{3,1},{4,6},{6,4},{5,7},{7,5},{8,10},{10,8},{9,1... | collective-permute-start | bytes 393224 | tf_op jit(solution)/shard_map/ppermute | solution.py:248
  173.1 6.9 %collective-permute-start.20 = (bf16[1,128,512]{2,1,0:T(8,128)(2,1)S(1)}, bf16[1,128,512]{2,1,0:T(8,128)(2,1)}, u32[]{:S(2)}, u32[]{:S(2)}) collective-permute-start(bf16[1,128,512]{2,1,0:T(8,128)(2,1)S(1)} %constant_dynamic-slice_fusion), channel_id=1, source_target_pairs={{0,1},{1,0},{2,3},{3,2},{4,5},{5,4},{6,7},{7,6},{8,9},{9,8},{10,11... | collective-permute-start | bytes 393224 | tf_op jit(solution)/shard_map/ppermute | solution.py:248
  174.5 0.9 copy-start.16
  175.5 0.9 copy-start.18

commit v2 on v0

v2 whole, which is shorter than its diff:
```python
import functools

import jax
import jax.numpy as jnp
from jax import lax
from jax.experimental import pallas as pl
from jax.experimental.pallas import tpu as pltpu
from jax.sharding import PartitionSpec as P

BF = jnp.bfloat16
F32 = jnp.float32
LANES = 128


def up_to(value, step):
    return -(-value // step) * step


def dot(a, b, contract=((1,), (0,))):
    return lax.dot_general(a, b, (contract, ((), ())), preferred_element_type=F32)


def vmem_spec(shape):
    return pl.BlockSpec(shape, lambda j: (0,) * len(shape))


def expert_spec(shape):
    return pl.BlockSpec((1,) + shape, lambda j: (j,) + (0,) * len(shape))


def pack_kernel(place, tokens, cotangent, route_ids, route_weights, *refs):
    *outs, ids, weights, sems = refs
    chosen, rows = ids.shape
    quarter = outs[0].shape[1] // 2
    wide = len(outs) - 1
    dp, sub = place[2], place[0]
    copies = [
        pltpu.make_async_copy(route_ids, ids, sems.at[0]),
        pltpu.make_async_copy(route_weights, weights, sems.at[1]),
    ]
    wanted = [((dp + by) % wide, sub) for by in range(1, wide)] + [(dp, sub), (dp, 1 - sub)]
    for out, (half, which) in zip(outs, wanted):
        columns = pl.ds(pl.multiple_of((half * 2 + which) * quarter, LANES), quarter)
        for source, at in ((tokens, 0), (cotangent, quarter)):
            target = out.at[0:rows, at : at + quarter]
            copies.append(
                pltpu.make_async_copy(source.at[:, columns], target, sems.at[len(copies)])
            )
    for copy in copies:
        copy.start()
    copies[0].wait()
    copies[1].wait()
    parts, rest = [ids[...].astype(F32)], weights[...]
    for _ in range(3):
        part = rest.astype(BF).astype(F32)
        parts.append(part)
        rest = rest - part
    table = jnp.concatenate(parts, axis=0)
    per_row = 2 * quarter // rows
    lines = [
        jnp.concatenate([table[i : i + 1] for i in range(start, start + per_row)], axis=1)
        for start in range(0, 4 * chosen, per_row)
    ]
    lines.append(jnp.zeros((ROUTE_ROWS - len(lines), 2 * quarter), F32))
    lines = jnp.concatenate(lines, axis=0).astype(BF)
    for out in outs:
        out[rows:, :] = lines
    for copy in copies[2:]:
        copy.wait()


def pack(place, tokens, cotangent, route_ids, route_weights, wide, quarter):
    rows, chosen = route_ids.shape
    shape = (rows + ROUTE_ROWS, 2 * quarter)
    return pl.pallas_call(
        pack_kernel,
        in_specs=[SMEM] + [pl.BlockSpec(memory_space=pltpu.HBM)] * 4,
        out_specs=[WHOLE] * (wide + 1),
        out_shape=[jax.ShapeDtypeStruct(shape, BF)] * (wide + 1),
        scratch_shapes=[
            pltpu.VMEM((chosen, rows), jnp.int32),
            pltpu.VMEM((chosen, rows), F32),
            pltpu.SemaphoreType.DMA((2 * wide + 4,)),
        ],
        compiler_params=pltpu.CompilerParams(vmem_limit_bytes=LIMIT),
        cost_estimate=PACK_COST,
    )(place, tokens, cotangent, route_ids.T, route_weights.T)


def route_tables(payloads, token_rows, chosen, first_expert, dp, local_experts, tables):
    shards = len(payloads)
    per_row = payloads[0].shape[1] // token_rows
    lines = [payload[token_rows:, :].astype(F32) for payload in payloads]

    def entry(index):
        row, column = divmod(index, per_row)
        at = slice(column * token_rows, (column + 1) * token_rows)
        return jnp.concatenate([line[row : row + 1, at] for line in lines], axis=1)

    ids = [entry(k) for k in range(chosen)]
    weights = [
        entry(chosen + k) + entry(2 * chosen + k) + entry(3 * chosen + k) for k in range(chosen)
    ]
    total = shards * token_rows
    masks, scales = [], []
    for local in range(local_experts):
        wanted = (first_expert + local).astype(F32)
        hits = [(one == wanted).astype(F32) for one in ids]
        masks.append(sum(hits))
        scales.append(sum(hit * weight for hit, weight in zip(hits, weights)))
    pad = [jnp.zeros((8 - local_experts, total), F32)] if local_experts < 8 else []
    mask = jnp.concatenate(masks + pad, axis=0)

    def number(axis):
        index = lax.broadcasted_iota(jnp.int32, (total, total), axis)
        part = sum((index >= i * token_rows).astype(jnp.int32) for i in range(1, shards + 1))
        shard = dp - part
        return index + (jnp.where(shard < 0, shard + shards, shard) - part) * token_rows

    rank = dot(mask.astype(BF), (number(0) < number(1)).astype(F32).astype(BF))
    tables[0:8, :] = jnp.where(mask > 0.5, rank, -1.0)
    tables[8:16, :] = jnp.concatenate(scales + pad, axis=0)


def one_hot(tables, local, slots):
    rank = tables[pl.ds(local, 1), :].astype(jnp.int32)
    total = rank.shape[1]
    return lax.broadcasted_iota(jnp.int32, (slots, total), 0) == rank


def forward_kernel(shards, token_rows, chosen, capacity, streamed, place, *refs):
    mine, other, refs = refs[:shards], refs[shards : 2 * shards], refs[2 * shards :]
    gate, up, down, _, sums, cot_rows, tables, token_scratch, sum_scratch = refs
    quarter = mine[0].shape[1] // 2
    experts = sums.shape[1] // capacity
    slots = cot_rows.shape[1]

    def routing():
        route_tables(mine, token_rows, chosen, place[1], place[2], experts, tables)

    def finish():
        sums[...] = sum_scratch[...].astype(BF)

    def one_expert(local, at):
        hot = one_hot(tables, local, slots).astype(F32).astype(BF)
        for source, which in ((mine, place[0]), (other, 1 - place[0])):
            rows = jnp.concatenate([one[0:token_rows, :] for one in source], axis=0)
            columns = pl.ds(pl.multiple_of(which * quarter, LANES), quarter)
            picked = dot(hot, rows).astype(BF)
            token_scratch[:, columns] = picked[:, :quarter]
            cot_rows[at, :, columns] = picked[:, quarter:]
        start = pl.multiple_of(local * capacity, 8) if streamed else local * capacity
        here = pl.ds(start, capacity)
        sum_scratch[0, here, :] = dot(token_scratch[...], gate[at])[:capacity]
        sum_scratch[1, here, :] = dot(token_scratch[...], up[at])[:capacity]
        sum_scratch[2, here, :] = dot(cot_rows[at], down[at], ((1,), (1,)))[:capacity]

    if streamed:
        local = pl.program_id(0)
        pl.when(local == 0)(routing)
        one_expert(local, 0)
        pl.when(local == experts - 1)(finish)
    else:
        routing()
        for local in range(experts):
            one_expert(local, local)
        finish()


def backward_kernel(capacity, parts, wide, place, *refs):
    tables, refs = refs[:parts], refs[parts:]
    sums, refs = refs[: parts * wide], refs[parts * wide :]
    gate, up, _, hidden, keep, send, full, total = refs
    rows = sums[0].shape[1]
    experts = hidden.shape[0]
    slots = hidden.shape[1] // parts
    quarter = keep.shape[1]
    for part in range(parts):
        here = sums[part * wide : (part + 1) * wide]
        full[part, :, 0:rows, :] = sum(one[...].astype(F32) for one in here)
        full[part, :, rows:, :] = jnp.zeros((3, full.shape[2] - rows, full.shape[3]), F32)
    for local in range(experts):
        gate_tokens, up_tokens = [], []
        for part in range(parts):
            hot = one_hot(tables[part], local, slots).astype(F32)
            scale = jnp.sum(hot * tables[part][8 + local : 9 + local, :], axis=1, keepdims=True)
            here = slice(local * capacity, local * capacity + slots)
            pre_gate, pre_up, tangent = (full[part, i, here, :] for i in range(3))
            sigmoid_gate = jax.nn.sigmoid(pre_gate)
            act = pre_gate * sigmoid_gate
            slope = sigmoid_gate * (1.0 + pre_gate * (1.0 - sigmoid_gate))
            hidden[local, part * slots : (part + 1) * slots, :] = (scale * act * pre_up).astype(BF)
            scaled = scale * tangent
            gate_adjoint = (scaled * pre_up * slope).astype(BF)
            up_adjoint = (scaled * act).astype(BF)
            hot = hot.astype(BF)
            gate_tokens.append(dot(hot, gate_adjoint, ((0,), (0,))).astype(BF))
            up_tokens.append(dot(hot, up_adjoint, ((0,), (0,))).astype(BF))
        gate_tokens = jnp.concatenate(gate_tokens, axis=0)
        up_tokens = jnp.concatenate(up_tokens, axis=0)
        term = dot(gate_tokens, gate[local], ((1,), (1,)))
        term = term + dot(up_tokens, up[local], ((1,), (1,)))
        total[...] = term if local == 0 else total[...] + term
    for out, which in ((keep, place[0]), (send, 1 - place[0])):
        out[...] = total[:, pl.ds(pl.multiple_of(which * quarter, LANES), quarter)].astype(BF)


def grad_kernel(half, *refs):
    *inputs, out, done = refs
    done[...] = jnp.zeros_like(done)
    local = pl.program_id(0)
    hidden = jnp.concatenate([one[local] for one in inputs[:half]], axis=0)
    cot_rows = jnp.concatenate([one[local] for one in inputs[half:]], axis=0)
    out[0] = dot(hidden, cot_rows, ((0,), (0,))).astype(BF)


SMEM = pl.BlockSpec(memory_space=pltpu.SMEM)
ANY = pl.BlockSpec(memory_space=pl.ANY)
WHOLE = pl.BlockSpec(memory_space=pltpu.VMEM)
LIMIT = 12 * 1024 * 1024
STREAM_LIMIT = 60 * 1024 * 1024
ROUTE_ROWS = 16
PACK_COST = pl.CostEstimate(flops=1, bytes_accessed=32 * 1024 * 1024, transcendentals=0)
NO_COST = pl.CostEstimate(flops=1, bytes_accessed=1, transcendentals=0)


def forward(
    place, mine, other, gate, up, down, token_rows, chosen, most, previous, streamed=False
):
    local_experts, depth, hidden = gate.shape
    shards = len(mine)
    capacity = up_to(shards * most, 8)
    slots = up_to(capacity, 16)
    rows = local_experts * capacity
    tokens = shards * token_rows
    weights = [WHOLE] * 3
    if streamed:
        weights = [expert_spec((depth, hidden))] * 2 + [expert_spec((hidden, depth))]
    return pl.pallas_call(
        functools.partial(forward_kernel, shards, token_rows, chosen, capacity, streamed),
        grid=(local_experts,) if streamed else (),
        in_specs=[SMEM] + [WHOLE] * (2 * shards) + weights + [ANY],
        out_specs=[WHOLE, expert_spec((slots, depth)) if streamed else WHOLE, WHOLE],
        out_shape=[
            jax.ShapeDtypeStruct((3, rows, hidden), BF),
            jax.ShapeDtypeStruct((local_experts, slots, depth), BF),
            jax.ShapeDtypeStruct((16, tokens), F32),
        ],
        scratch_shapes=[pltpu.VMEM((slots, depth), BF), pltpu.VMEM((3, rows, hidden), F32)],
        compiler_params=pltpu.CompilerParams(vmem_limit_bytes=STREAM_LIMIT if streamed else LIMIT),
        cost_estimate=NO_COST,
    )(place, *mine, *other, gate, up, down, previous)


def backward(place, tables, sums, gate, up, previous):
    local_experts, depth, hidden = gate.shape
    parts, wide = len(tables), len(sums[0])
    rows = sums[0][0].shape[1]
    capacity = rows // local_experts
    slots = up_to(capacity, 16)
    tokens = parts * tables[0].shape[1]
    flat = [one for part in sums for one in part]
    return pl.pallas_call(
        functools.partial(backward_kernel, capacity, parts, wide),
        in_specs=[SMEM] + [WHOLE] * (parts + len(flat) + 2) + [ANY],
        out_specs=[WHOLE] * 3,
        out_shape=[
            jax.ShapeDtypeStruct((local_experts, parts * slots, hidden), BF),
            jax.ShapeDtypeStruct((tokens, depth // 2), BF),
            jax.ShapeDtypeStruct((tokens, depth // 2), BF),
        ],
        scratch_shapes=[
            pltpu.VMEM((parts, 3, rows + slots - capacity + 8, hidden), F32),
            pltpu.VMEM((tokens, depth), F32),
        ],
        compiler_params=pltpu.CompilerParams(vmem_limit_bytes=LIMIT),
        cost_estimate=NO_COST,
    )(place, *tables, *flat, gate, up, previous)


def grads(hiddens, cots):
    local_experts, _, hidden = hiddens[0].shape
    depth = cots[0].shape[2]
    slots = sum(one.shape[1] for one in cots)
    return pl.pallas_call(
        functools.partial(grad_kernel, len(hiddens)),
        grid=(local_experts,),
        in_specs=[WHOLE] * (len(hiddens) + len(cots)),
        out_specs=[expert_spec((hidden, depth)), vmem_spec((8, LANES))],
        out_shape=[
            jax.ShapeDtypeStruct((local_experts, hidden, depth), BF),
            jax.ShapeDtypeStruct((8, LANES), F32),
        ],
        compiler_params=pltpu.CompilerParams(vmem_limit_bytes=LIMIT),
        cost_estimate=NO_COST,
    )(*hiddens, *cots)


def small(kernel, shapes, *arrays):
    return pl.pallas_call(
        kernel,
        in_specs=[SMEM] + [WHOLE] * (len(arrays) - 1),
        out_specs=[WHOLE] * len(shapes),
        out_shape=[jax.ShapeDtypeStruct(shape, BF) for shape in shapes],
        compiler_params=pltpu.CompilerParams(vmem_limit_bytes=LIMIT),
        cost_estimate=NO_COST,
    )(*arrays)


def sum_kernel(inputs, place, *refs):
    total = sum(one[...].astype(F32) for one in refs[:inputs]).astype(BF)
    rows = refs[inputs].shape[0]
    for index, out in enumerate(refs[inputs:]):
        out[...] = total[index * rows : (index + 1) * rows]


def turned_kernel(inputs, place, *refs):
    total = sum(one[...].astype(F32) for one in refs[:inputs]).astype(BF)
    first, second = refs[inputs:]
    rows = first.shape[0]
    straight = place[2] == place[0]

    @pl.when(straight)
    def _():
        first[...] = total[:rows]
        second[...] = total[rows:]

    @pl.when(jnp.logical_not(straight))
    def _():
        first[...] = total[rows:]
        second[...] = total[:rows]


def choose_kernel(place, one, two, stay, send):
    straight = place[2] == place[0]

    @pl.when(straight)
    def _():
        stay[...] = one[...]
        send[...] = two[...]

    @pl.when(jnp.logical_not(straight))
    def _():
        stay[...] = two[...]
        send[...] = one[...]


def final_kernel(place, stay, come, *refs):
    *far, out = refs
    quarter = stay.shape[1]

    def far_sum(flip):
        return [
            sum(far[start + (q + flip) % 2][...].astype(F32) for start in range(0, len(far), 2))
            for q in range(2)
        ]

    for sub in range(2):
        for dp in range(2):

            @pl.when((place[0] == sub) & (place[2] == dp))
            def _():
                own = [stay[...], come[...]] if sub == 0 else [come[...], stay[...]]
                for q, extra in enumerate(far_sum(dp)):
                    out[:, q * quarter : (q + 1) * quarter] = (own[q].astype(F32) + extra).astype(BF)


def shift(array, axis, by):
    size = lax.axis_size(axis)
    return lax.ppermute(array, axis, [(i, (i + by) % size) for i in range(size)])


def after(array, *done):
    return lax.optimization_barrier((array,) + done)[0]


def per_device(tokens, cotangent, route_ids, route_weights, w_gate, w_up, v_down):
    owners, wide, cores = (lax.axis_size(a) for a in ("expert", "dp", "sub"))
    owner, dp, sub = (lax.axis_index(a) for a in ("expert", "dp", "sub"))
    token_rows, chosen = route_ids.shape
    local_experts = w_gate.shape[0]
    expert_count = owners * local_experts
    most = max(2, 9 * token_rows * chosen // (8 * expert_count))
    quarter = tokens.shape[1] // (wide * cores)
    place = jnp.stack([sub, owner * local_experts, dp]).astype(jnp.int32)

    *sends, own, own_other = pack(
        place, tokens, cotangent, route_ids, route_weights, wide, quarter
    )

    def ahead(mine, other, previous, streamed=False):
        return forward(
            place, mine, other, w_gate, w_up, v_down, token_rows, chosen, most, previous, streamed
        )

    received = [shift(one, "dp", by) for by, one in enumerate(sends, 1)]
    parts = [ahead([own], [own_other], place)]
    blocks, swapped = [[own] + received], [[]]
    for _ in range(1, owners):
        blocks.append([shift(one, "expert", 1) for one in blocks[-1]])
    blocks.append([])
    swapped.append([shift(blocks[1][0], "sub", 1)])
    for one in received:
        other = shift(after(one, parts[0][2]), "sub", 1)
        previous = after(parts[-1][2], swapped[1][0], *blocks[1][1:])
        parts.append(ahead([one], [other], previous))
    home_sums = [[part[0]] for part in parts]
    arrived = []
    for index in range(wide):
        for step in range(1, wide):
            got = shift(parts[index][0], "dp", -step)
            home_sums[(index - step) % wide].append(got)
            arrived.append(got)
    hiddens, cots = [], [part[1] for part in parts]
    waiting = ([part[2] for part in parts], home_sums)
    last = parts[-1][2]
    swapped[1] += [
        shift(after(one, last, *arrived[: wide - 1]), "sub", 1) for one in blocks[1][1:]
    ]
    gate_for_sums = arrived[wide - 1 :]

    def behind(waiting, previous, crossing_after=()):
        hidden, keep, send = backward(place, *waiting, w_gate, w_up, previous)
        hiddens.append(hidden)
        send = after(send, *crossing_after)
        return hidden, (keep, shift(send, "sub", 1))

    direct = wide == cores
    near, far = [], []

    def sent_back(halves, by):
        if by < 2 or not direct:
            (rows,) = small(
                functools.partial(sum_kernel, 2), [halves[0].shape], place, *halves
            )
            near.append(shift(rows, "expert", -by) if by else rows)
            return [rows]
        pieces = small(
            functools.partial(turned_kernel, 2), [(token_rows, quarter)] * 2, place, *halves
        )
        return pieces

    def sent_straight(pieces, by):
        for way, piece in enumerate(pieces):
            pairs = []
            for index in range(owners * wide * cores):
                place_of, from_dp, from_sub = (
                    index // (wide * cores),
                    index // cores % wide,
                    index % cores,
                )
                to = (place_of - by) % owners * wide + (from_sub + way) % wide
                pairs.append((index, to * cores + from_dp))
            far.append(lax.ppermute(piece, ("expert", "dp", "sub"), pairs))

    def gathered(rows):
        pieces = jnp.zeros((wide, token_rows, quarter), BF)
        for by in range(wide):
            one = rows[by * token_rows : (by + 1) * token_rows].astype(BF)
            one = after(shift(one, "dp", -by), last) if by else one
            pieces = lax.dynamic_update_slice_in_dim(pieces, one[None], (dp + by) % wide, 0)
        span = wide // cores
        stay = lax.dynamic_slice_in_dim(pieces, sub * span, span, 0)
        come = shift(lax.dynamic_slice_in_dim(pieces, (1 - sub) * span, span, 0), "sub", 1)
        columns = []
        for index in range(span):
            columns.append(jnp.where(sub == 0, stay[index], come[index]))
            columns.append(jnp.where(sub == 0, come[index], stay[index]))
        return jnp.concatenate(columns, axis=1)

    for by in range(1, owners):
        previous = after(last, *blocks[2][:1]) if by == 1 else last
        sums, cot_rows, tables = ahead(blocks[by], swapped[by], previous)
        cots.append(cot_rows)
        swapped.append([shift(after(one, tables), "sub", 1) for one in blocks[by + 1]])
        send = after(sums, *gate_for_sums, *swapped[by + 1][:1])
        gate_for_sums = [shift(send, "dp", step) for step in range(1, wide)]
        last, halves = behind(waiting, tables, swapped[by + 1])
        pieces = sent_back(halves, by - 1)
        if direct and by - 1 >= 2:
            sent_straight(pieces, by - 1)
        waiting = ([tables], [[sums] + gate_for_sums])
    last, halves = behind(waiting, after(last, *near[-1:], *pieces), far)
    pieces = sent_back(halves, owners - 1)
    if direct and owners > 2:
        hiddens[-1], *pieces = lax.optimization_barrier((last, *pieces))
        sent_straight(pieces, owners - 1)
    grad_down, done = grads(hiddens, cots)
    if not direct or owners < 3:
        return (grad_down, gathered(sum((one.astype(F32) for one in near[1:]), near[0])))
    keep, send = small(
        functools.partial(sum_kernel, len(near)), [(token_rows, quarter)] * 2, place, *near
    )
    got = after(shift(send, "dp", -1), last)
    stay, send = small(choose_kernel, [keep.shape] * 2, place, keep, got)
    come = shift(send, "sub", 1)
    far = [after(one, done) for one in far]
    (out,) = small(
        final_kernel, [(token_rows, cores * quarter)], place, stay, come, *far
    )
    return (grad_down, out)


def solution(mesh):
    placed = (
        P(("groups", "expert", "dp"), None),
        P(("groups", "expert", "dp"), None),
        P(("groups", "expert", "dp"), None),
        P(("groups", "expert", "dp"), None),
        P("expert", "dp", "sub"),
        P("expert", "dp", "sub"),
        P(("groups", "expert"), "sub", "dp"),
    )
    return jax.shard_map(
        per_device,
        mesh=mesh,
        in_specs=placed,
        out_specs=(P(("groups", "expert"), "sub", "dp"), P(("groups", "expert", "dp"), "sub")),
        check_vma=False,
    )
```

time: 463 us -> 127 us (0.27); the launches traced: 455 us -> 127 us
  waiting for transfers between devices: 319 us -> 51 us
  local copies, waits for them, and re-layouts: 56.5 us -> 9.12 us
  Pallas kernels: 0 us -> 42.3 us
  matrix products: 36 us -> 0 us
  between operations: 14.5 us -> 0.87 us
  other arithmetic: 7.85 us -> 0.08 us
    all_gather x3 -> x0, waiting for transfers between devices: 145 us -> none  [the longest x1 74.1 us: per_device(): lax.all_gather(v_down, 'dp', axis=2, tiled=True)]
    all_to_all x4 -> x0, waiting for transfers between devices: 93.1 us -> none  [the longest x1 53.7 us: per_device(): lax.all_to_all(partial_value[None].astype(jnp.bfloat16), 'expert', split_...]
    reduce_scatter x2 -> x0, waiting for transfers between devices: 78.9 us -> none  [the longest x1 78.9 us: per_device(): lax.psum_scatter(grad_terms.astype(jnp.bfloat16), 'dp', scatter_dimension...]
    ppermute x0 -> x30, waiting for transfers between devices: none -> 51 us  [the longest x26 44.7 us: shift(): lax.ppermute(array, axis, [(i, (i + by) % size) for i in range(size)])]
    pallas_call x0 -> x18, Pallas kernels: none -> 42.3 us  [the longest x5 18 us: forward(): pl.pallas_call(functools.partial(forward_kernel, shards, token_rows, chos...]
    dot_general x6 -> x0, matrix products: 36 us -> none  [the longest x1 8.03 us: per_device(): jnp.einsum('erf,erd->efd', weighted_hidden, got_cotangent, preferred_elem...]
    ppermute x0 -> x30, starting transfers between devices: none -> 23.5 us  [the longest x26 17.2 us: shift(): lax.ppermute(array, axis, [(i, (i + by) % size) for i in range(size)])]
    gather x4 -> x0, local copies, waits for them, and re-layouts: 20.9 us -> none  [the longest x2 12.9 us: per_device(): returned.reshape(expert_count * capacity, model_width)[slot_index]]
  transfers between devices with their start and end apart: 9 -> 30, of which waited for: 5 -> 13; matrix products, arithmetic and copies ran while one was open for 12% -> 0% of each run, Pallas kernels for 0% -> 31%
where the time goes in v2:
time: 127 us
  waiting for transfers between devices  51 us (40%)
  Pallas kernels  42.3 us (33%)
  starting transfers between devices  23.5 us (19%)
  local copies, waits for them, and re-layouts  9.12 us (7%)
    ppermute x26, waiting for transfers between devices, shift(): lax.ppermute(array, axis, [(i, (i + by) % size) for i in range(size)])  44.7 us
    pallas_call x5, Pallas kernels, forward(): pl.pallas_call(functools.partial(forward_kernel, shards, token_rows, chos...  18 us
    ppermute x26, starting transfers between devices, shift(): lax.ppermute(array, axis, [(i, (i + by) % size) for i in range(size)])  17.2 us
    pallas_call x4, Pallas kernels, backward(): pl.pallas_call(functools.partial(backward_kernel, capacity, parts, wide),...  14.9 us
    unnamed x20, local copies, waits for them, and re-layouts  9.12 us
    ppermute x4, starting transfers between devices, sent_straight(): far.append(lax.ppermute(piece, ('expert', 'dp', 'sub'), pairs))  6.35 us
    ppermute x4, waiting for transfers between devices, sent_straight(): far.append(lax.ppermute(piece, ('expert', 'dp', 'sub'), pairs))  6.3 us
    pallas_call x7, Pallas kernels, small(): pl.pallas_call(kernel, in_specs=[SMEM] + [WHOLE] * (len(arrays) - 1), out...  5.07 us
  transfers between devices with their start and end apart: 30, of which 13 were waited for; matrix products, arithmetic and copies ran while one was open for 0% of the time, Pallas kernels for 31%

profile of v2, /device:TPU:0, one launch (start us, length us, event | category | flops | bytes accessed | tf_op | source)
XLA Modules:
  0.0 126.9 jit_solution(14072261763080865152)
XLA Ops:
  0.7 1.0 copy-done.6
  1.8 1.0 copy-done.7
  2.8 0.7 copy-done.8
  3.5 0.7 copy-done.9
  4.2 0.8 shard_map.86
  4.9 3.0 %collective-permute-start = (bf16[144,1024]{1,0:T(8,128)(2,1)S(1)}, bf16[144,1024]{1,0:T(8,128)(2,1)S(1)}, u32[]{:S(2)}, u32[]{:S(2)}) collective-permute-start(bf16[144,1024]{1,0:T(8,128)(2,1)S(1)} %get-tuple-element.68), channel_id=1, source_target_pairs={{0,2},{2,0},{1,3},{3,1},{4,6},{6,4},{5,7},{7,5},{8,10},{10,8},{9,1... | collective-permute-start | bytes 884744 | tf_op jit(solution)/shard_map/ppermute | solution.py:370
  7.9 1.6 %collective-permute-start.2 = (bf16[144,1024]{1,0:T(8,128)(2,1)S(1)}, bf16[144,1024]{1,0:T(8,128)(2,1)S(1)}, u32[]{:S(2)}, u32[]{:S(2)}) collective-permute-start(bf16[144,1024]{1,0:T(8,128)(2,1)S(1)} %get-tuple-element.65.refs_0_), channel_id=1, source_target_pairs={{0,4},{4,8},{8,12},{12,0},{1,5},{5,9},{9,13},{13,1},{2,6},{6,10},{... | collective-permute-start | bytes 884744 | tf_op jit(solution)/shard_map/ppermute | solution.py:370
  9.5 1.9 %copy-done = bf16[4,1024,384]{2,1,0:T(8,128)(2,1)S(1)} copy-done((bf16[4,1024,384]{2,1,0:T(8,128)(2,1)S(1)}, bf16[4,1024,384]{2,1,0:T(8,128)(2,1)}, u32[]{:S(2)}) %copy-start) | copy-done | bytes 3145752
  11.4 1.9 %copy-done.2 = bf16[4,1024,384]{2,1,0:T(8,128)(2,1)S(1)} copy-done((bf16[4,1024,384]{2,1,0:T(8,128)(2,1)S(1)}, bf16[4,1024,384]{2,1,0:T(8,128)(2,1)}, u32[]{:S(2)}) %copy-start.2) | copy-done | bytes 3145752
  13.3 1.9 %copy-done.4 = bf16[4,384,1024]{2,1,0:T(8,128)(2,1)S(1)} copy-done((bf16[4,384,1024]{2,1,0:T(8,128)(2,1)S(1)}, bf16[4,384,1024]{2,1,0:T(8,128)(2,1)}, u32[]{:S(2)}) %copy-start.4) | copy-done | bytes 3145752
  15.2 3.3 %shard_map.87 = (bf16[3,160,384]{2,1,0:T(8,128)(2,1)S(1)}, bf16[4,48,1024]{2,1,0:T(8,128)(2,1)S(1)}, f32[16,128]{1,0:T(8,128)S(1)}) custom-call(s32[3]{0:T(128)S(1)} %pad_add_fusion.place.refs_5_, bf16[144,1024]{1,0:T(8,128)(2,1)S(1)} %get-tuple-element.65.refs_0_, bf16[144,1024]{1,0:T(8,128)(2,1)S(1)} %get-tuple-element.66.refs_1_, ...), custom_call_target="tpu_custom_call" | custom-call | flops 1 | bytes 1 | tf_op jit(solution)/shard_map/pallas_call | solution.py:239
  18.5 0.6 collective-permute-start.6
  19.1 1.6 %collective-permute-start.4 = (bf16[144,1024]{1,0:T(8,128)(2,1)S(1)}, bf16[144,1024]{1,0:T(8,128)(2,1)S(1)}, u32[]{:S(2)}, u32[]{:S(2)}) collective-permute-start(bf16[144,1024]{1,0:T(8,128)(2,1)S(1)} %collective-permute-done.refs_0_), channel_id=1, source_target_pairs={{0,4},{4,8},{8,12},{12,0},{1,5},{5,9},{9,13},{13,1},{2,6},{6,10},{... | collective-permute-start | bytes 884744 | tf_op jit(solution)/shard_map/ppermute | solution.py:370
  21.2 1.6 %collective-permute-start.8 = (bf16[144,1024]{1,0:T(8,128)(2,1)S(1)}, bf16[144,1024]{1,0:T(8,128)(2,1)S(1)}, u32[]{:S(2)}, u32[]{:S(2)}) collective-permute-start(bf16[144,1024]{1,0:T(8,128)(2,1)S(1)} %collective-permute-done.2.refs_0_), channel_id=1, source_target_pairs={{0,4},{4,8},{8,12},{12,0},{1,5},{5,9},{9,13},{13,1},{2,6},{6,10},{... | collective-permute-start | bytes 884744 | tf_op jit(solution)/shard_map/ppermute | solution.py:370
  22.7 8.1 %collective-permute-done.4.refs_1_ = bf16[144,1024]{1,0:T(8,128)(2,1)S(1)} collective-permute-done((bf16[144,1024]{1,0:T(8,128)(2,1)S(1)}, bf16[144,1024]{1,0:T(8,128)(2,1)S(1)}, u32[]{:S(2)}, u32[]{:S(2)}) %collective-permute-start.4) | collective-permute-done | bytes 294944 | tf_op jit(solution)/shard_map/ppermute | solution.py:370
  30.8 3.3 %shard_map.88 = (bf16[3,160,384]{2,1,0:T(8,128)(2,1)S(1)}, bf16[4,48,1024]{2,1,0:T(8,128)(2,1)S(1)}, f32[16,128]{1,0:T(8,128)S(1)}) custom-call(s32[3]{0:T(128)S(1)} %pad_add_fusion.place.refs_5_, bf16[144,1024]{1,0:T(8,128)(2,1)S(1)} %collective-permute-done.refs_0_, bf16[144,1024]{1,0:T(8,128)(2,1)S(1)} %collective-permute-done.1.refs_1_, ...), custom_call_target="tpu_custom_call" | custom-call | flops 1 | bytes 1 | tf_op jit(solution)/shard_map/pallas_call | solution.py:239
  34.2 1.6 %collective-permute-start.5 = (bf16[3,160,384]{2,1,0:T(8,128)(2,1)S(1)}, bf16[3,160,384]{2,1,0:T(8,128)(2,1)S(1)}, u32[]{:S(2)}, u32[]{:S(2)}) collective-permute-start(bf16[3,160,384]{2,1,0:T(8,128)(2,1)S(1)} %get-tuple-element.73.refs_4_), channel_id=1, source_target_pairs={{0,2},{2,0},{1,3},{3,1},{4,6},{6,4},{5,7},{7,5},{8,10},{10,8},{9,1... | collective-permute-start | bytes 1105928 | tf_op jit(solution)/shard_map/ppermute | solution.py:370
  35.8 3.8 %shard_map.89 = (bf16[3,288,384]{2,1,0:T(8,128)(2,1)S(1)}, bf16[4,80,1024]{2,1,0:T(8,128)(2,1)S(1)}, f32[16,256]{1,0:T(8,128)S(1)}) custom-call(s32[3]{0:T(128)S(1)} %pad_add_fusion.place.refs_5_, bf16[144,1024]{1,0:T(8,128)(2,1)S(1)} %collective-permute-done.2.refs_0_, bf16[144,1024]{1,0:T(8,128)(2,1)S(1)} %collective-permute-done.4.refs_1_, ...), custom_call_target="tpu_custom_call" | custom-call | flops 1 | bytes 1 | tf_op jit(solution)/shard_map/pallas_call | solution.py:239
  39.8 5.4 %collective-permute-done.5.refs_3_ = bf16[3,160,384]{2,1,0:T(8,128)(2,1)S(1)} collective-permute-done((bf16[3,160,384]{2,1,0:T(8,128)(2,1)S(1)}, bf16[3,160,384]{2,1,0:T(8,128)(2,1)S(1)}, u32[]{:S(2)}, u32[]{:S(2)}) %collective-permute-start.5) | collective-permute-done | bytes 368672 | tf_op jit(solution)/shard_map/ppermute | solution.py:370
  45.2 1.5 %collective-permute-start.10 = (bf16[3,288,384]{2,1,0:T(8,128)(2,1)S(1)}, bf16[3,288,384]{2,1,0:T(8,128)(2,1)S(1)}, u32[]{:S(2)}, u32[]{:S(2)}) collective-permute-start(bf16[3,288,384]{2,1,0:T(8,128)(2,1)S(1)} %get-tuple-element.80.refs_1_), channel_id=1, source_target_pairs={{0,2},{2,0},{1,3},{3,1},{4,6},{6,4},{5,7},{7,5},{8,10},{10,8},{9,1... | collective-permute-start | bytes 1990664 | tf_op jit(solution)/shard_map/ppermute | solution.py:370
  46.7 4.2 %collective-permute-done.11.refs_1_ = bf16[144,1024]{1,0:T(8,128)(2,1)S(1)} collective-permute-done((bf16[144,1024]{1,0:T(8,128)(2,1)S(1)}, bf16[144,1024]{1,0:T(8,128)(2,1)S(1)}, u32[]{:S(2)}, u32[]{:S(2)}) %collective-permute-start.11) | collective-permute-done | bytes 294944 | tf_op jit(solution)/shard_map/ppermute | solution.py:370
  50.9 3.7 %shard_map.90 = (bf16[4,96,384]{2,1,0:T(8,128)(2,1)S(1)}, bf16[256,512]{1,0:T(8,128)(2,1)S(1)}, bf16[256,512]{1,0:T(8,128)(2,1)S(1)}) custom-call(s32[3]{0:T(128)S(1)} %pad_add_fusion.place.refs_5_, f32[16,128]{1,0:T(8,128)S(1)} %get-tuple-element.70.refs_5_.refs_0_, f32[16,128]{1,0:T(8,128)S(1)} %get-tuple-element.75.refs_7_.refs_1_, ...), custom_call_target="tpu_custom_call" | custom-call | flops 1 | bytes 1 | tf_op jit(solution)/shard_map/pallas_call | solution.py:263
  54.6 3.8 %shard_map.91 = (bf16[3,288,384]{2,1,0:T(8,128)(2,1)S(1)}, bf16[4,80,1024]{2,1,0:T(8,128)(2,1)S(1)}, f32[16,256]{1,0:T(8,128)S(1)}) custom-call(s32[3]{0:T(128)S(1)} %pad_add_fusion.place.refs_5_, bf16[144,1024]{1,0:T(8,128)(2,1)S(1)} %collective-permute-done.8.refs_0_, bf16[144,1024]{1,0:T(8,128)(2,1)S(1)} %collective-permute-done.11.refs_1_, ...), custom_call_target="tpu_custom_call" | custom-call | flops 1 | bytes 1 | tf_op jit(solution)/shard_map/pallas_call | solution.py:239
  58.4 3.7 %collective-permute-done.13.refs_0_ = bf16[144,1024]{1,0:T(8,128)(2,1)S(1)} collective-permute-done((bf16[144,1024]{1,0:T(8,128)(2,1)S(1)}, bf16[144,1024]{1,0:T(8,128)(2,1)S(1)}, u32[]{:S(2)}, u32[]{:S(2)}) %collective-permute-start.13) | collective-permute-done | bytes 294944 | tf_op jit(solution)/shard_map/ppermute | solution.py:370
  62.1 1.6 %collective-permute-done.14.refs_2_ = bf16[144,1024]{1,0:T(8,128)(2,1)S(1)} collective-permute-done((bf16[144,1024]{1,0:T(8,128)(2,1)S(1)}, bf16[144,1024]{1,0:T(8,128)(2,1)S(1)}, u32[]{:S(2)}, u32[]{:S(2)}) %collective-permute-start.14) | collective-permute-done | bytes 294944 | tf_op jit(solution)/shard_map/ppermute | solution.py:370
  63.7 1.5 %collective-permute-start.15 = (bf16[3,288,384]{2,1,0:T(8,128)(2,1)S(1)}, bf16[3,288,384]{2,1,0:T(8,128)(2,1)S(1)}, u32[]{:S(2)}, u32[]{:S(2)}) collective-permute-start(bf16[3,288,384]{2,1,0:T(8,128)(2,1)S(1)} %get-tuple-element.86.refs_1_), channel_id=1, source_target_pairs={{0,2},{2,0},{1,3},{3,1},{4,6},{6,4},{5,7},{7,5},{8,10},{10,8},{9,1... | collective-permute-start | bytes 1990664 | tf_op jit(solution)/shard_map/ppermute | solution.py:370
  65.2 10.6 %collective-permute-done.16.refs_1_ = bf16[144,1024]{1,0:T(8,128)(2,1)S(1)} collective-permute-done((bf16[144,1024]{1,0:T(8,128)(2,1)S(1)}, bf16[144,1024]{1,0:T(8,128)(2,1)S(1)}, u32[]{:S(2)}, u32[]{:S(2)}) %collective-permute-start.16) | collective-permute-done | bytes 294944 | tf_op jit(solution)/shard_map/ppermute | solution.py:370
  75.7 3.7 %shard_map.92 = (bf16[4,80,384]{2,1,0:T(8,128)(2,1)S(1)}, bf16[256,512]{1,0:T(8,128)(2,1)S(1)}, bf16[256,512]{1,0:T(8,128)(2,1)S(1)}) custom-call(s32[3]{0:T(128)S(1)} %pad_add_fusion.place.refs_5_, f32[16,256]{1,0:T(8,128)S(1)} %get-tuple-element.76.refs_8_.refs_0_, bf16[3,288,384]{2,1,0:T(8,128)(2,1)S(1)} %get-tuple-element.80.refs_1_, ...), custom_call_target="tpu_custom_call" | custom-call | flops 1 | bytes 1 | tf_op jit(solution)/shard_map/pallas_call | solution.py:263
  79.5 3.8 %shard_map.93 = (bf16[3,288,384]{2,1,0:T(8,128)(2,1)S(1)}, bf16[4,80,1024]{2,1,0:T(8,128)(2,1)S(1)}, f32[16,256]{1,0:T(8,128)S(1)}) custom-call(s32[3]{0:T(128)S(1)} %pad_add_fusion.place.refs_5_, bf16[144,1024]{1,0:T(8,128)(2,1)S(1)} %collective-permute-done.13.refs_0_, bf16[144,1024]{1,0:T(8,128)(2,1)S(1)} %collective-permute-done.16.refs_1_, ...), custom_call_target="tpu_custom_call" | custom-call | flops 1 | bytes 1 | tf_op jit(solution)/shard_map/pallas_call | solution.py:239
  83.4 0.6 collective-permute-start.18
  84.2 3.7 %shard_map.94 = (bf16[4,80,384]{2,1,0:T(8,128)(2,1)S(1)}, bf16[256,512]{1,0:T(8,128)(2,1)S(1)}, bf16[256,512]{1,0:T(8,128)(2,1)S(1)}) custom-call(s32[3]{0:T(128)S(1)} %pad_add_fusion.place.refs_5_, f32[16,256]{1,0:T(8,128)S(1)} %get-tuple-element.82.refs_5_.refs_0_, bf16[3,288,384]{2,1,0:T(8,128)(2,1)S(1)} %get-tuple-element.86.refs_1_, ...), custom_call_target="tpu_custom_call" | custom-call | flops 1 | bytes 1 | tf_op jit(solution)/shard_map/pallas_call | solution.py:263
  88.3 0.6 shard_map.95
  89.6 0.7 shard_map.96
  90.3 3.7 %collective-permute-start.23 = (bf16[128,512]{1,0:T(8,128)(2,1)S(1)}, bf16[128,512]{1,0:T(8,128)(2,1)S(1)}, u32[]{:S(2)}, u32[]{:S(2)}) collective-permute-start(bf16[128,512]{1,0:T(8,128)(2,1)S(1)} %get-tuple-element.98), channel_id=1, source_target_pairs={{0,10},{1,8},{2,11},{3,9},{4,14},{5,12},{6,15},{7,13},{8,2},{9,0},... | collective-permute-start | bytes 393224 | tf_op jit(solution)/shard_map/ppermute | solution.py:454
  94.0 3.8 %collective-permute-done.20.refs_1_ = bf16[256,512]{1,0:T(8,128)(2,1)S(1)} collective-permute-done((bf16[256,512]{1,0:T(8,128)(2,1)S(1)}, bf16[256,512]{1,0:T(8,128)(2,1)S(1)}, u32[]{:S(2)}, u32[]{:S(2)}) %collective-permute-start.20) | collective-permute-done | bytes 262176 | tf_op jit(solution)/shard_map/ppermute | solution.py:370
  97.8 2.9 %collective-permute-done.18.refs_2_ = bf16[3,288,384]{2,1,0:T(8,128)(2,1)S(1)} collective-permute-done((bf16[3,288,384]{2,1,0:T(8,128)(2,1)S(1)}, bf16[3,288,384]{2,1,0:T(8,128)(2,1)S(1)}, u32[]{:S(2)}, u32[]{:S(2)}) %collective-permute-start.18) | collective-permute-done | bytes 663584 | tf_op jit(solution)/shard_map/ppermute | solution.py:370
  100.8 3.8 %shard_map.97 = (bf16[4,80,384]{2,1,0:T(8,128)(2,1)S(1)}, bf16[256,512]{1,0:T(8,128)(2,1)S(1)}, bf16[256,512]{1,0:T(8,128)(2,1)S(1)}) custom-call(s32[3]{0:T(128)S(1)} %pad_add_fusion.place.refs_5_, f32[16,256]{1,0:T(8,128)S(1)} %get-tuple-element.88.refs_5_.refs_0_, bf16[3,288,384]{2,1,0:T(8,128)(2,1)S(1)} %get-tuple-element.91.refs_1_, ...), custom_call_target="tpu_custom_call" | custom-call | flops 1 | bytes 1 | tf_op jit(solution)/shard_map/pallas_call | solution.py:263
  104.5 1.9 %collective-permute-done.23.refs_1_ = bf16[128,512]{1,0:T(8,128)(2,1)S(1)} collective-permute-done((bf16[128,512]{1,0:T(8,128)(2,1)S(1)}, bf16[128,512]{1,0:T(8,128)(2,1)S(1)}, u32[]{:S(2)}, u32[]{:S(2)}) %collective-permute-start.23) | collective-permute-done | bytes 131104 | tf_op jit(solution)/shard_map/ppermute | solution.py:454
  107.2 0.6 shard_map.101
  107.8 1.6 %collective-permute-start.26 = (bf16[128,512]{1,0:T(8,128)(2,1)S(1)}, bf16[128,512]{1,0:T(8,128)(2,1)S(1)}, u32[]{:S(2)}, u32[]{:S(2)}) collective-permute-start(bf16[128,512]{1,0:T(8,128)(2,1)S(1)} %get-tuple-element.117), channel_id=1, source_target_pairs={{0,2},{2,0},{1,3},{3,1},{4,6},{6,4},{5,7},{7,5},{8,10},{10,8},{9,1... | collective-permute-start | bytes 393224 | tf_op jit(solution)/shard_map/ppermute | solution.py:370
  109.5 4.1 %collective-permute-done.26.two = bf16[128,512]{1,0:T(8,128)(2,1)S(1)} collective-permute-done((bf16[128,512]{1,0:T(8,128)(2,1)S(1)}, bf16[128,512]{1,0:T(8,128)(2,1)S(1)}, u32[]{:S(2)}, u32[]{:S(2)}) %collective-permute-start.26) | collective-permute-done | bytes 131104 | tf_op jit(solution)/shard_map/ppermute | solution.py:370
  113.6 0.7 shard_map.98
  114.3 1.6 %collective-permute-start.28 = (bf16[128,512]{1,0:T(8,128)(2,1)S(1)}, bf16[128,512]{1,0:T(8,128)(2,1)S(1)}, u32[]{:S(2)}, u32[]{:S(2)}) collective-permute-start(bf16[128,512]{1,0:T(8,128)(2,1)S(1)} %get-tuple-element.124), channel_id=1, source_target_pairs={{0,4},{1,6},{2,5},{3,7},{4,8},{5,10},{6,9},{7,11},{8,12},{9,14},{1... | collective-permute-start | bytes 393224 | tf_op jit(solution)/shard_map/ppermute | solution.py:454
  115.9 1.0 collective-permute-start.29
  117.6 3.6 %shard_map.99 = (bf16[4,384,1024]{2,1,0:T(8,128)(2,1)}, f32[8,128]{1,0:T(8,128)}) custom-call(bf16[4,96,384]{2,1,0:T(8,128)(2,1)S(1)} %get-tuple-element.77.refs_7_.refs_0_, bf16[4,80,384]{2,1,0:T(8,128)(2,1)S(1)} %get-tuple-element.83.refs_7_.refs_1_, bf16[4,80,384]{2,1,0:T(8,128)(2,1)S(1)} %get-tuple-element.99.refs_5_.refs_2_, ...), custom_call_target="tpu_custom_call" | custom-call | flops 1 | bytes 1 | tf_op jit(solution)/shard_map/pallas_call | solution.py:285
  121.1 2.1 %collective-permute-done.28.refs_2_ = bf16[128,512]{1,0:T(8,128)(2,1)S(1)} collective-permute-done((bf16[128,512]{1,0:T(8,128)(2,1)S(1)}, bf16[128,512]{1,0:T(8,128)(2,1)S(1)}, u32[]{:S(2)}, u32[]{:S(2)}) %collective-permute-start.28) | collective-permute-done | bytes 131104 | tf_op jit(solution)/shard_map/ppermute | solution.py:454
  123.2 2.3 %collective-permute-done.29.refs_3_ = bf16[128,512]{1,0:T(8,128)(2,1)S(1)} collective-permute-done((bf16[128,512]{1,0:T(8,128)(2,1)S(1)}, bf16[128,512]{1,0:T(8,128)(2,1)S(1)}, u32[]{:S(2)}, u32[]{:S(2)}) %collective-permute-start.29) | collective-permute-done | bytes 131104 | tf_op jit(solution)/shard_map/ppermute | solution.py:454
  125.6 1.4 %shard_map.103 = bf16[128,1024]{1,0:T(8,128)(2,1)} custom-call(s32[3]{0:T(128)S(1)} %pad_add_fusion.place.refs_5_, bf16[128,512]{1,0:T(8,128)(2,1)S(1)} %get-tuple-element.119.stay, bf16[128,512]{1,0:T(8,128)(2,1)S(1)} %collective-permute-done.27.come, bf16[128,512]{1,0:T(8,128)(2,1)S(1)} %collective-permute-done.22.refs_0_, ...), custom_call_target="tpu_custom_call" | custom-call | flops 1 | bytes 1 | tf_op jit(solution)/shard_map/pallas_call | solution.py:300
  (51 shorter events, 3.7 us)
Async XLA Ops:
  0.7 1.0 copy-start.6
  1.8 1.0 copy-start.7
  2.8 0.7 copy-start.8
  3.5 0.7 copy-start.9
  4.9 14.1 %collective-permute-start = (bf16[144,1024]{1,0:T(8,128)(2,1)S(1)}, bf16[144,1024]{1,0:T(8,128)(2,1)S(1)}, u32[]{:S(2)}, u32[]{:S(2)}) collective-permute-start(bf16[144,1024]{1,0:T(8,128)(2,1)S(1)} %get-tuple-element.68), channel_id=1, source_target_pairs={{0,2},{2,0},{1,3},{3,1},{4,6},{6,4},{5,7},{7,5},{8,10},{10,8},{9,1... | collective-permute-start | bytes 884744 | tf_op jit(solution)/shard_map/ppermute | solution.py:370
  7.9 12.7 %collective-permute-start.2 = (bf16[144,1024]{1,0:T(8,128)(2,1)S(1)}, bf16[144,1024]{1,0:T(8,128)(2,1)S(1)}, u32[]{:S(2)}, u32[]{:S(2)}) collective-permute-start(bf16[144,1024]{1,0:T(8,128)(2,1)S(1)} %get-tuple-element.65.refs_0_), channel_id=1, source_target_pairs={{0,4},{4,8},{8,12},{12,0},{1,5},{5,9},{9,13},{13,1},{2,6},{6,10},{... | collective-permute-start | bytes 884744 | tf_op jit(solution)/shard_map/ppermute | solution.py:370
  9.5 1.9 %copy-start = (bf16[4,1024,384]{2,1,0:T(8,128)(2,1)S(1)}, bf16[4,1024,384]{2,1,0:T(8,128)(2,1)}, u32[]{:S(2)}) copy-start(bf16[4,1024,384]{2,1,0:T(8,128)(2,1)} %refs_3_.9) | copy-start | bytes 9437188
  11.4 1.9 %copy-start.2 = (bf16[4,1024,384]{2,1,0:T(8,128)(2,1)S(1)}, bf16[4,1024,384]{2,1,0:T(8,128)(2,1)}, u32[]{:S(2)}) copy-start(bf16[4,1024,384]{2,1,0:T(8,128)(2,1)} %refs_4_.15) | copy-start | bytes 9437188
  13.3 1.9 %copy-start.4 = (bf16[4,384,1024]{2,1,0:T(8,128)(2,1)S(1)}, bf16[4,384,1024]{2,1,0:T(8,128)(2,1)}, u32[]{:S(2)}) copy-start(bf16[4,384,1024]{2,1,0:T(8,128)(2,1)} %refs_6_.7) | copy-start | bytes 9437188
  15.2 15.6 %copy-start.1 = (bf16[4,1024,384]{2,1,0:T(8,128)(2,1)S(1)}, bf16[4,1024,384]{2,1,0:T(8,128)(2,1)}, u32[]{:S(2)}) copy-start(bf16[4,1024,384]{2,1,0:T(8,128)(2,1)} %refs_3_.9) | copy-start | bytes 9437188
  15.2 15.6 %copy-start.3 = (bf16[4,1024,384]{2,1,0:T(8,128)(2,1)S(1)}, bf16[4,1024,384]{2,1,0:T(8,128)(2,1)}, u32[]{:S(2)}) copy-start(bf16[4,1024,384]{2,1,0:T(8,128)(2,1)} %refs_4_.15) | copy-start | bytes 9437188
  15.2 15.6 %copy-start.5 = (bf16[4,384,1024]{2,1,0:T(8,128)(2,1)S(1)}, bf16[4,384,1024]{2,1,0:T(8,128)(2,1)}, u32[]{:S(2)}) copy-start(bf16[4,384,1024]{2,1,0:T(8,128)(2,1)} %refs_6_.7) | copy-start | bytes 9437188
  18.5 15.7 %collective-permute-start.6 = (bf16[3,160,384]{2,1,0:T(8,128)(2,1)S(1)}, bf16[3,160,384]{2,1,0:T(8,128)(2,1)S(1)}, u32[]{:S(2)}, u32[]{:S(2)}) collective-permute-start(bf16[3,160,384]{2,1,0:T(8,128)(2,1)S(1)} %get-tuple-element.72.refs_2_), channel_id=1, source_target_pairs={{0,2},{2,0},{1,3},{3,1},{4,6},{6,4},{5,7},{7,5},{8,10},{10,8},{9,1... | collective-permute-start | bytes 1105928 | tf_op jit(solution)/shard_map/ppermute | solution.py:370
  19.1 11.7 %collective-permute-start.4 = (bf16[144,1024]{1,0:T(8,128)(2,1)S(1)}, bf16[144,1024]{1,0:T(8,128)(2,1)S(1)}, u32[]{:S(2)}, u32[]{:S(2)}) collective-permute-start(bf16[144,1024]{1,0:T(8,128)(2,1)S(1)} %collective-permute-done.refs_0_), channel_id=1, source_target_pairs={{0,4},{4,8},{8,12},{12,0},{1,5},{5,9},{9,13},{13,1},{2,6},{6,10},{... | collective-permute-start | bytes 884744 | tf_op jit(solution)/shard_map/ppermute | solution.py:370
  20.7 10.2 %collective-permute-start.3 = (bf16[144,1024]{1,0:T(8,128)(2,1)S(1)}, bf16[144,1024]{1,0:T(8,128)(2,1)S(1)}, u32[]{:S(2)}, u32[]{:S(2)}) collective-permute-start(bf16[144,1024]{1,0:T(8,128)(2,1)S(1)} %collective-permute-done.2.refs_0_), channel_id=1, source_target_pairs={{0,1},{1,0},{2,3},{3,2},{4,5},{5,4},{6,7},{7,6},{8,9},{9,8},{10,11... | collective-permute-start | bytes 884744 | tf_op jit(solution)/shard_map/ppermute | solution.py:370
  20.7 10.2 %collective-permute-start.1 = (bf16[144,1024]{1,0:T(8,128)(2,1)S(1)}, bf16[144,1024]{1,0:T(8,128)(2,1)S(1)}, u32[]{:S(2)}, u32[]{:S(2)}) collective-permute-start(bf16[144,1024]{1,0:T(8,128)(2,1)S(1)} %collective-permute-done.refs_0_), channel_id=1, source_target_pairs={{0,1},{1,0},{2,3},{3,2},{4,5},{5,4},{6,7},{7,6},{8,9},{9,8},{10,11... | collective-permute-start | bytes 884744 | tf_op jit(solution)/shard_map/ppermute | solution.py:370
  21.2 14.6 %collective-permute-start.8 = (bf16[144,1024]{1,0:T(8,128)(2,1)S(1)}, bf16[144,1024]{1,0:T(8,128)(2,1)S(1)}, u32[]{:S(2)}, u32[]{:S(2)}) collective-permute-start(bf16[144,1024]{1,0:T(8,128)(2,1)S(1)} %collective-permute-done.2.refs_0_), channel_id=1, source_target_pairs={{0,4},{4,8},{8,12},{12,0},{1,5},{5,9},{9,13},{13,1},{2,6},{6,10},{... | collective-permute-start | bytes 884744 | tf_op jit(solution)/shard_map/ppermute | solution.py:370
  34.1 1.6 %collective-permute-start.7 = (bf16[144,1024]{1,0:T(8,128)(2,1)S(1)}, bf16[144,1024]{1,0:T(8,128)(2,1)S(1)}, u32[]{:S(2)}, u32[]{:S(2)}) collective-permute-start(bf16[144,1024]{1,0:T(8,128)(2,1)S(1)} %collective-permute-done.4.refs_1_), channel_id=1, source_target_pairs={{0,1},{1,0},{2,3},{3,2},{4,5},{5,4},{6,7},{7,6},{8,9},{9,8},{10,11... | collective-permute-start | bytes 884744 | tf_op jit(solution)/shard_map/ppermute | solution.py:370
  34.2 11.0 %collective-permute-start.5 = (bf16[3,160,384]{2,1,0:T(8,128)(2,1)S(1)}, bf16[3,160,384]{2,1,0:T(8,128)(2,1)S(1)}, u32[]{:S(2)}, u32[]{:S(2)}) collective-permute-start(bf16[3,160,384]{2,1,0:T(8,128)(2,1)S(1)} %get-tuple-element.73.refs_4_), channel_id=1, source_target_pairs={{0,2},{2,0},{1,3},{3,1},{4,6},{6,4},{5,7},{7,5},{8,10},{10,8},{9,1... | collective-permute-start | bytes 1105928 | tf_op jit(solution)/shard_map/ppermute | solution.py:370
  39.6 5.6 %collective-permute-start.9 = (bf16[144,1024]{1,0:T(8,128)(2,1)S(1)}, bf16[144,1024]{1,0:T(8,128)(2,1)S(1)}, u32[]{:S(2)}, u32[]{:S(2)}) collective-permute-start(bf16[144,1024]{1,0:T(8,128)(2,1)S(1)} %collective-permute-done.8.refs_0_), channel_id=1, source_target_pairs={{0,1},{1,0},{2,3},{3,2},{4,5},{5,4},{6,7},{7,6},{8,9},{9,8},{10,11... | collective-permute-start | bytes 884744 | tf_op jit(solution)/shard_map/ppermute | solution.py:370
  39.8 11.1 %collective-permute-start.11 = (bf16[144,1024]{1,0:T(8,128)(2,1)S(1)}, bf16[144,1024]{1,0:T(8,128)(2,1)S(1)}, u32[]{:S(2)}, u32[]{:S(2)}) collective-permute-start(bf16[144,1024]{1,0:T(8,128)(2,1)S(1)} %collective-permute-done.4.refs_1_), channel_id=1, source_target_pairs={{0,4},{4,8},{8,12},{12,0},{1,5},{5,9},{9,13},{13,1},{2,6},{6,10},{... | collective-permute-start | bytes 884744 | tf_op jit(solution)/shard_map/ppermute | solution.py:370
  45.2 18.5 %collective-permute-start.10 = (bf16[3,288,384]{2,1,0:T(8,128)(2,1)S(1)}, bf16[3,288,384]{2,1,0:T(8,128)(2,1)S(1)}, u32[]{:S(2)}, u32[]{:S(2)}) collective-permute-start(bf16[3,288,384]{2,1,0:T(8,128)(2,1)S(1)} %get-tuple-element.80.refs_1_), channel_id=1, source_target_pairs={{0,2},{2,0},{1,3},{3,1},{4,6},{6,4},{5,7},{7,5},{8,10},{10,8},{9,1... | collective-permute-start | bytes 1990664 | tf_op jit(solution)/shard_map/ppermute | solution.py:370
  50.9 3.7 %collective-permute-start.12 = (bf16[144,1024]{1,0:T(8,128)(2,1)S(1)}, bf16[144,1024]{1,0:T(8,128)(2,1)S(1)}, u32[]{:S(2)}, u32[]{:S(2)}) collective-permute-start(bf16[144,1024]{1,0:T(8,128)(2,1)S(1)} %collective-permute-done.11.refs_1_), channel_id=1, source_target_pairs={{0,1},{1,0},{2,3},{3,2},{4,5},{5,4},{6,7},{7,6},{8,9},{9,8},{10,11... | collective-permute-start | bytes 884744 | tf_op jit(solution)/shard_map/ppermute | solution.py:370
  50.9 11.2 %collective-permute-start.13 = (bf16[144,1024]{1,0:T(8,128)(2,1)S(1)}, bf16[144,1024]{1,0:T(8,128)(2,1)S(1)}, u32[]{:S(2)}, u32[]{:S(2)}) collective-permute-start(bf16[144,1024]{1,0:T(8,128)(2,1)S(1)} %collective-permute-done.8.refs_0_), channel_id=1, source_target_pairs={{0,4},{4,8},{8,12},{12,0},{1,5},{5,9},{9,13},{13,1},{2,6},{6,10},{... | collective-permute-start | bytes 884744 | tf_op jit(solution)/shard_map/ppermute | solution.py:370
  62.1 1.6 %collective-permute-start.14 = (bf16[144,1024]{1,0:T(8,128)(2,1)S(1)}, bf16[144,1024]{1,0:T(8,128)(2,1)S(1)}, u32[]{:S(2)}, u32[]{:S(2)}) collective-permute-start(bf16[144,1024]{1,0:T(8,128)(2,1)S(1)} %collective-permute-done.13.refs_0_), channel_id=1, source_target_pairs={{0,1},{1,0},{2,3},{3,2},{4,5},{5,4},{6,7},{7,6},{8,9},{9,8},{10,11... | collective-permute-start | bytes 884744 | tf_op jit(solution)/shard_map/ppermute | solution.py:370
  63.7 19.7 %collective-permute-start.15 = (bf16[3,288,384]{2,1,0:T(8,128)(2,1)S(1)}, bf16[3,288,384]{2,1,0:T(8,128)(2,1)S(1)}, u32[]{:S(2)}, u32[]{:S(2)}) collective-permute-start(bf16[3,288,384]{2,1,0:T(8,128)(2,1)S(1)} %get-tuple-element.86.refs_1_), channel_id=1, source_target_pairs={{0,2},{2,0},{1,3},{3,1},{4,6},{6,4},{5,7},{7,5},{8,10},{10,8},{9,1... | collective-permute-start | bytes 1990664 | tf_op jit(solution)/shard_map/ppermute | solution.py:370
  65.2 10.6 %collective-permute-start.16 = (bf16[144,1024]{1,0:T(8,128)(2,1)S(1)}, bf16[144,1024]{1,0:T(8,128)(2,1)S(1)}, u32[]{:S(2)}, u32[]{:S(2)}) collective-permute-start(bf16[144,1024]{1,0:T(8,128)(2,1)S(1)} %collective-permute-done.11.refs_1_), channel_id=1, source_target_pairs={{0,4},{4,8},{8,12},{12,0},{1,5},{5,9},{9,13},{13,1},{2,6},{6,10},{... | collective-permute-start | bytes 884744 | tf_op jit(solution)/shard_map/ppermute | solution.py:370
  75.7 3.8 %collective-permute-start.17 = (bf16[144,1024]{1,0:T(8,128)(2,1)S(1)}, bf16[144,1024]{1,0:T(8,128)(2,1)S(1)}, u32[]{:S(2)}, u32[]{:S(2)}) collective-permute-start(bf16[144,1024]{1,0:T(8,128)(2,1)S(1)} %collective-permute-done.16.refs_1_), channel_id=1, source_target_pairs={{0,1},{1,0},{2,3},{3,2},{4,5},{5,4},{6,7},{7,6},{8,9},{9,8},{10,11... | collective-permute-start | bytes 884744 | tf_op jit(solution)/shard_map/ppermute | solution.py:370
  83.4 17.4 %collective-permute-start.18 = (bf16[3,288,384]{2,1,0:T(8,128)(2,1)S(1)}, bf16[3,288,384]{2,1,0:T(8,128)(2,1)S(1)}, u32[]{:S(2)}, u32[]{:S(2)}) collective-permute-start(bf16[3,288,384]{2,1,0:T(8,128)(2,1)S(1)} %get-tuple-element.91.refs_1_), channel_id=1, source_target_pairs={{0,2},{2,0},{1,3},{3,1},{4,6},{6,4},{5,7},{7,5},{8,10},{10,8},{9,1... | collective-permute-start | bytes 1990664 | tf_op jit(solution)/shard_map/ppermute | solution.py:370
  84.0 4.3 %collective-permute-start.19 = (bf16[256,512]{1,0:T(8,128)(2,1)S(1)}, bf16[256,512]{1,0:T(8,128)(2,1)S(1)}, u32[]{:S(2)}, u32[]{:S(2)}) collective-permute-start(bf16[256,512]{1,0:T(8,128)(2,1)S(1)} %get-tuple-element.94), channel_id=1, source_target_pairs={{0,1},{1,0},{2,3},{3,2},{4,5},{5,4},{6,7},{7,6},{8,9},{9,8},{10,11... | collective-permute-start | bytes 786440 | tf_op jit(solution)/shard_map/ppermute | solution.py:370
  88.0 1.6 %collective-permute-start.21 = (bf16[256,512]{1,0:T(8,128)(2,1)S(1)}, bf16[256,512]{1,0:T(8,128)(2,1)S(1)}, u32[]{:S(2)}, u32[]{:S(2)}) collective-permute-start(bf16[256,512]{1,0:T(8,128)(2,1)S(1)} %get-tuple-element.96), channel_id=1, source_target_pairs={{0,1},{1,0},{2,3},{3,2},{4,5},{5,4},{6,7},{7,6},{8,9},{9,8},{10,11... | collective-permute-start | bytes 786440 | tf_op jit(solution)/shard_map/ppermute | solution.py:370
  88.9 8.9 %collective-permute-start.20 = (bf16[256,512]{1,0:T(8,128)(2,1)S(1)}, bf16[256,512]{1,0:T(8,128)(2,1)S(1)}, u32[]{:S(2)}, u32[]{:S(2)}) collective-permute-start(bf16[256,512]{1,0:T(8,128)(2,1)S(1)} %shard_map.95), channel_id=1, source_target_pairs={{0,12},{4,0},{8,4},{12,8},{1,13},{5,1},{9,5},{13,9},{2,14},{6,2},{... | collective-permute-start | bytes 786440 | tf_op jit(solution)/shard_map/ppermute | solution.py:370
  89.0 17.6 %collective-permute-start.25 = (bf16[256,512]{1,0:T(8,128)(2,1)S(1)}, bf16[256,512]{1,0:T(8,128)(2,1)S(1)}, u32[]{:S(2)}, u32[]{:S(2)}) collective-permute-start(bf16[256,512]{1,0:T(8,128)(2,1)S(1)} %get-tuple-element.115), channel_id=1, source_target_pairs={{0,1},{1,0},{2,3},{3,2},{4,5},{5,4},{6,7},{7,6},{8,9},{9,8},{10,11... | collective-permute-start | bytes 786440 | tf_op jit(solution)/shard_map/ppermute | solution.py:370
  90.2 14.3 %collective-permute-start.22 = (bf16[128,512]{1,0:T(8,128)(2,1)S(1)}, bf16[128,512]{1,0:T(8,128)(2,1)S(1)}, u32[]{:S(2)}, u32[]{:S(2)}) collective-permute-start(bf16[128,512]{1,0:T(8,128)(2,1)S(1)} %get-tuple-element.97), channel_id=1, source_target_pairs={{0,8},{1,10},{2,9},{3,11},{4,12},{5,14},{6,13},{7,15},{8,0},{9,2},... | collective-permute-start | bytes 393224 | tf_op jit(solution)/shard_map/ppermute | solution.py:454
  90.3 16.1 %collective-permute-start.23 = (bf16[128,512]{1,0:T(8,128)(2,1)S(1)}, bf16[128,512]{1,0:T(8,128)(2,1)S(1)}, u32[]{:S(2)}, u32[]{:S(2)}) collective-permute-start(bf16[128,512]{1,0:T(8,128)(2,1)S(1)} %get-tuple-element.98), channel_id=1, source_target_pairs={{0,10},{1,8},{2,11},{3,9},{4,14},{5,12},{6,15},{7,13},{8,2},{9,0},... | collective-permute-start | bytes 393224 | tf_op jit(solution)/shard_map/ppermute | solution.py:454
  106.4 7.2 %collective-permute-start.24 = (bf16[256,512]{1,0:T(8,128)(2,1)S(1)}, bf16[256,512]{1,0:T(8,128)(2,1)S(1)}, u32[]{:S(2)}, u32[]{:S(2)}) collective-permute-start(bf16[256,512]{1,0:T(8,128)(2,1)S(1)} %get-tuple-element.103), channel_id=1, source_target_pairs={{0,1},{1,0},{2,3},{3,2},{4,5},{5,4},{6,7},{7,6},{8,9},{9,8},{10,11... | collective-permute-start | bytes 786440 | tf_op jit(solution)/shard_map/ppermute | solution.py:370
  107.8 5.8 %collective-permute-start.26 = (bf16[128,512]{1,0:T(8,128)(2,1)S(1)}, bf16[128,512]{1,0:T(8,128)(2,1)S(1)}, u32[]{:S(2)}, u32[]{:S(2)}) collective-permute-start(bf16[128,512]{1,0:T(8,128)(2,1)S(1)} %get-tuple-element.117), channel_id=1, source_target_pairs={{0,2},{2,0},{1,3},{3,1},{4,6},{6,4},{5,7},{7,5},{8,10},{10,8},{9,1... | collective-permute-start | bytes 393224 | tf_op jit(solution)/shard_map/ppermute | solution.py:370
  114.3 9.0 %collective-permute-start.28 = (bf16[128,512]{1,0:T(8,128)(2,1)S(1)}, bf16[128,512]{1,0:T(8,128)(2,1)S(1)}, u32[]{:S(2)}, u32[]{:S(2)}) collective-permute-start(bf16[128,512]{1,0:T(8,128)(2,1)S(1)} %get-tuple-element.124), channel_id=1, source_target_pairs={{0,4},{1,6},{2,5},{3,7},{4,8},{5,10},{6,9},{7,11},{8,12},{9,14},{1... | collective-permute-start | bytes 393224 | tf_op jit(solution)/shard_map/ppermute | solution.py:454
  115.9 9.7 %collective-permute-start.29 = (bf16[128,512]{1,0:T(8,128)(2,1)S(1)}, bf16[128,512]{1,0:T(8,128)(2,1)S(1)}, u32[]{:S(2)}, u32[]{:S(2)}) collective-permute-start(bf16[128,512]{1,0:T(8,128)(2,1)S(1)} %get-tuple-element.126), channel_id=1, source_target_pairs={{0,6},{1,4},{2,7},{3,5},{4,10},{5,8},{6,11},{7,9},{8,14},{9,12},{1... | collective-permute-start | bytes 393224 | tf_op jit(solution)/shard_map/ppermute | solution.py:454
  117.4 8.1 %collective-permute-start.27 = (bf16[128,512]{1,0:T(8,128)(2,1)S(1)}, bf16[128,512]{1,0:T(8,128)(2,1)S(1)}, u32[]{:S(2)}, u32[]{:S(2)}) collective-permute-start(bf16[128,512]{1,0:T(8,128)(2,1)S(1)} %get-tuple-element.120), channel_id=1, source_target_pairs={{0,1},{1,0},{2,3},{3,2},{4,5},{5,4},{6,7},{7,6},{8,9},{9,8},{10,11... | collective-permute-start | bytes 393224 | tf_op jit(solution)/shard_map/ppermute | solution.py:370

commit v3 on v2

--- a/solution.py
+++ b/solution.py
@@ -402,7 +402,7 @@
     swapped.append([shift(blocks[1][0], "sub", 1)])
     for one in received:
         other = shift(after(one, parts[0][2]), "sub", 1)
-        previous = after(parts[-1][2], swapped[1][0], *blocks[1][1:])
+        previous = after(parts[-1][2], swapped[1][0])
         parts.append(ahead([one], [other], previous))
     home_sums = [[part[0]] for part in parts]
     arrived = []
@@ -469,29 +469,34 @@
         return jnp.concatenate(columns, axis=1)
 
     for by in range(1, owners):
-        previous = after(last, *blocks[2][:1]) if by == 1 else last
-        sums, cot_rows, tables = ahead(blocks[by], swapped[by], previous)
+        sums, cot_rows, tables = ahead(blocks[by], swapped[by], last)
         cots.append(cot_rows)
-        swapped.append([shift(after(one, tables), "sub", 1) for one in blocks[by + 1]])
-        send = after(sums, *gate_for_sums, *swapped[by + 1][:1])
+        send = after(sums, *gate_for_sums)
         gate_for_sums = [shift(send, "dp", step) for step in range(1, wide)]
-        last, halves = behind(waiting, tables, swapped[by + 1])
+        last, halves = behind(waiting, tables)
         pieces = sent_back(halves, by - 1)
         if direct and by - 1 >= 2:
             sent_straight(pieces, by - 1)
         waiting = ([tables], [[sums] + gate_for_sums])
-    last, halves = behind(waiting, after(last, *near[-1:], *pieces), far)
+        swapped.append([])
+        for one in blocks[by + 1]:
+            one = after(one, last, *blocks[by + 1], *swapped[-1])
+            swapped[-1].append(shift(one, "sub", 1))
+    if not direct or owners < 3:
+        last, halves = behind(waiting, after(last, *pieces))
+        sent_back(halves, owners - 1)
+        grad_down, _ = grads(hiddens, cots)
+        return (grad_down, gathered(sum((one.astype(F32) for one in near[1:]), near[0])))
+    last, halves = behind(waiting, after(last, *pieces), far)
     pieces = sent_back(halves, owners - 1)
-    if direct and owners > 2:
-        hiddens[-1], *pieces = lax.optimization_barrier((last, *pieces))
-        sent_straight(pieces, owners - 1)
+    keep, send = small(
+        functools.partial(sum_kernel, len(near)), [(token_rows, quarter)] * 2, place,
+        *near[:-1], after(near[-1], last),
+    )
+    got = shift(send, "dp", -1)
+    hiddens[-1], *pieces = lax.optimization_barrier((last, *pieces))
+    sent_straight(pieces, owners - 1)
     grad_down, done = grads(hiddens, cots)
-    if not direct or owners < 3:
-        return (grad_down, gathered(sum((one.astype(F32) for one in near[1:]), near[0])))
-    keep, send = small(
-        functools.partial(sum_kernel, len(near)), [(token_rows, quarter)] * 2, place, *near
-    )
-    got = after(shift(send, "dp", -1), last)
     stay, send = small(choose_kernel, [keep.shape] * 2, place, keep, got)
     come = shift(send, "sub", 1)
     far = [after(one, done) for one in far]

time: 127 us -> 115 us (0.906)
  waiting for transfers between devices: 51 us -> 39.4 us
    ppermute x26, waiting for transfers between devices: 44.7 us -> 36.9 us  [shift(): lax.ppermute(array, axis, [(i, (i + by) % size) for i in range(size)])]
    ppermute x4, waiting for transfers between devices: 6.3 us -> 2.49 us  [sent_straight(): far.append(lax.ppermute(piece, ('expert', 'dp', 'sub'), pairs))]
  transfers between devices with their start and end apart: 30 -> 30, of which waited for: 13 -> 15; matrix products, arithmetic and copies ran while one was open for 0% -> 0% of each run, Pallas kernels for 31% -> 35%
where the time goes in v3:
time: 115 us
  Pallas kernels  42.3 us (37%)
  waiting for transfers between devices  39.4 us (34%)
  starting transfers between devices  22.8 us (20%)
  local copies, waits for them, and re-layouts  9.12 us (8%)
    ppermute x26, waiting for transfers between devices, shift(): lax.ppermute(array, axis, [(i, (i + by) % size) for i in range(size)])  36.9 us
    pallas_call x5, Pallas kernels, forward(): pl.pallas_call(functools.partial(forward_kernel, shards, token_rows, chos...  18 us
    ppermute x26, starting transfers between devices, shift(): lax.ppermute(array, axis, [(i, (i + by) % size) for i in range(size)])  17.1 us
    pallas_call x4, Pallas kernels, backward(): pl.pallas_call(functools.partial(backward_kernel, capacity, parts, wide),...  14.9 us
    unnamed x20, local copies, waits for them, and re-layouts  9.12 us
    ppermute x4, starting transfers between devices, sent_straight(): far.append(lax.ppermute(piece, ('expert', 'dp', 'sub'), pairs))  5.65 us
    pallas_call x7, Pallas kernels, small(): pl.pallas_call(kernel, in_specs=[SMEM] + [WHOLE] * (len(arrays) - 1), out...  5.07 us
    pallas_call x1, Pallas kernels, grads(): pl.pallas_call(functools.partial(grad_kernel, len(hiddens)), grid=(local_...  3.61 us
  transfers between devices with their start and end apart: 30, of which 15 were waited for; matrix products, arithmetic and copies ran while one was open for 0% of the time, Pallas kernels for 35%

profile of v3, /device:TPU:0, one launch (start us, length us, event | category | flops | bytes accessed | tf_op | source)
XLA Modules:
  0.0 114.6 jit_solution(6447862856921879109)
XLA Ops:
  0.7 1.0 copy-done.6
  1.8 1.0 copy-done.7
  2.8 0.7 copy-done.8
  3.5 0.7 copy-done.9
  4.2 0.8 shard_map.86
  4.9 3.1 %collective-permute-start.2 = (bf16[144,1024]{1,0:T(8,128)(2,1)S(1)}, bf16[144,1024]{1,0:T(8,128)(2,1)S(1)}, u32[]{:S(2)}, u32[]{:S(2)}) collective-permute-start(bf16[144,1024]{1,0:T(8,128)(2,1)S(1)} %get-tuple-element.62.refs_0_), channel_id=1, source_target_pairs={{0,4},{4,8},{8,12},{12,0},{1,5},{5,9},{9,13},{13,1},{2,6},{6,10},{... | collective-permute-start | bytes 884744 | tf_op jit(solution)/shard_map/ppermute | solution.py:370
  8.0 1.5 %collective-permute-start = (bf16[144,1024]{1,0:T(8,128)(2,1)S(1)}, bf16[144,1024]{1,0:T(8,128)(2,1)S(1)}, u32[]{:S(2)}, u32[]{:S(2)}) collective-permute-start(bf16[144,1024]{1,0:T(8,128)(2,1)S(1)} %get-tuple-element.65), channel_id=1, source_target_pairs={{0,2},{2,0},{1,3},{3,1},{4,6},{6,4},{5,7},{7,5},{8,10},{10,8},{9,1... | collective-permute-start | bytes 884744 | tf_op jit(solution)/shard_map/ppermute | solution.py:370
  9.5 1.9 %copy-done = bf16[4,1024,384]{2,1,0:T(8,128)(2,1)S(1)} copy-done((bf16[4,1024,384]{2,1,0:T(8,128)(2,1)S(1)}, bf16[4,1024,384]{2,1,0:T(8,128)(2,1)}, u32[]{:S(2)}) %copy-start) | copy-done | bytes 3145752
  11.4 1.9 %copy-done.2 = bf16[4,1024,384]{2,1,0:T(8,128)(2,1)S(1)} copy-done((bf16[4,1024,384]{2,1,0:T(8,128)(2,1)S(1)}, bf16[4,1024,384]{2,1,0:T(8,128)(2,1)}, u32[]{:S(2)}) %copy-start.2) | copy-done | bytes 3145752
  13.3 1.9 %copy-done.4 = bf16[4,384,1024]{2,1,0:T(8,128)(2,1)S(1)} copy-done((bf16[4,384,1024]{2,1,0:T(8,128)(2,1)S(1)}, bf16[4,384,1024]{2,1,0:T(8,128)(2,1)}, u32[]{:S(2)}) %copy-start.4) | copy-done | bytes 3145752
  15.2 3.3 %shard_map.87 = (bf16[3,160,384]{2,1,0:T(8,128)(2,1)S(1)}, bf16[4,48,1024]{2,1,0:T(8,128)(2,1)S(1)}, f32[16,128]{1,0:T(8,128)S(1)}) custom-call(s32[3]{0:T(128)S(1)} %pad_add_fusion.place.refs_5_, bf16[144,1024]{1,0:T(8,128)(2,1)S(1)} %get-tuple-element.62.refs_0_, bf16[144,1024]{1,0:T(8,128)(2,1)S(1)} %get-tuple-element.63.refs_1_, ...), custom_call_target="tpu_custom_call" | custom-call | flops 1 | bytes 1 | tf_op jit(solution)/shard_map/pallas_call | solution.py:239
  19.6 1.6 %collective-permute-start.6 = (bf16[144,1024]{1,0:T(8,128)(2,1)S(1)}, bf16[144,1024]{1,0:T(8,128)(2,1)S(1)}, u32[]{:S(2)}, u32[]{:S(2)}) collective-permute-start(bf16[144,1024]{1,0:T(8,128)(2,1)S(1)} %collective-permute-done.refs_0_), channel_id=1, source_target_pairs={{0,4},{4,8},{8,12},{12,0},{1,5},{5,9},{9,13},{13,1},{2,6},{6,10},{... | collective-permute-start | bytes 884744 | tf_op jit(solution)/shard_map/ppermute | solution.py:370
  21.2 3.3 %shard_map.88 = (bf16[3,160,384]{2,1,0:T(8,128)(2,1)S(1)}, bf16[4,48,1024]{2,1,0:T(8,128)(2,1)S(1)}, f32[16,128]{1,0:T(8,128)S(1)}) custom-call(s32[3]{0:T(128)S(1)} %pad_add_fusion.place.refs_5_, bf16[144,1024]{1,0:T(8,128)(2,1)S(1)} %collective-permute-done.refs_0_, bf16[144,1024]{1,0:T(8,128)(2,1)S(1)} %collective-permute-done.1.refs_1_, ...), custom_call_target="tpu_custom_call" | custom-call | flops 1 | bytes 1 | tf_op jit(solution)/shard_map/pallas_call | solution.py:239
  24.4 1.6 %collective-permute-start.4 = (bf16[3,160,384]{2,1,0:T(8,128)(2,1)S(1)}, bf16[3,160,384]{2,1,0:T(8,128)(2,1)S(1)}, u32[]{:S(2)}, u32[]{:S(2)}) collective-permute-start(bf16[3,160,384]{2,1,0:T(8,128)(2,1)S(1)} %get-tuple-element.70.refs_4_), channel_id=1, source_target_pairs={{0,2},{2,0},{1,3},{3,1},{4,6},{6,4},{5,7},{7,5},{8,10},{10,8},{9,1... | collective-permute-start | bytes 1105928 | tf_op jit(solution)/shard_map/ppermute | solution.py:370
  26.0 3.4 %collective-permute-done.5.refs_5_ = bf16[3,160,384]{2,1,0:T(8,128)(2,1)S(1)} collective-permute-done((bf16[3,160,384]{2,1,0:T(8,128)(2,1)S(1)}, bf16[3,160,384]{2,1,0:T(8,128)(2,1)S(1)}, u32[]{:S(2)}, u32[]{:S(2)}) %collective-permute-start.5) | collective-permute-done | bytes 368672 | tf_op jit(solution)/shard_map/ppermute | solution.py:370
  29.4 1.0 collective-permute-done.6.refs_1_
  30.9 1.6 %collective-permute-start.10 = (bf16[144,1024]{1,0:T(8,128)(2,1)S(1)}, bf16[144,1024]{1,0:T(8,128)(2,1)S(1)}, u32[]{:S(2)}, u32[]{:S(2)}) collective-permute-start(bf16[144,1024]{1,0:T(8,128)(2,1)S(1)} %collective-permute-done.6.refs_1_), channel_id=1, source_target_pairs={{0,4},{4,8},{8,12},{12,0},{1,5},{5,9},{9,13},{13,1},{2,6},{6,10},{... | collective-permute-start | bytes 884744 | tf_op jit(solution)/shard_map/ppermute | solution.py:370
  32.5 3.8 %shard_map.89 = (bf16[3,288,384]{2,1,0:T(8,128)(2,1)S(1)}, bf16[4,80,1024]{2,1,0:T(8,128)(2,1)S(1)}, f32[16,256]{1,0:T(8,128)S(1)}) custom-call(s32[3]{0:T(128)S(1)} %pad_add_fusion.place.refs_5_, bf16[144,1024]{1,0:T(8,128)(2,1)S(1)} %collective-permute-done.2.refs_0_, bf16[144,1024]{1,0:T(8,128)(2,1)S(1)} %collective-permute-done.6.refs_1_, ...), custom_call_target="tpu_custom_call" | custom-call | flops 1 | bytes 1 | tf_op jit(solution)/shard_map/pallas_call | solution.py:239
  36.4 1.0 collective-permute-start.8
  37.3 3.7 %shard_map.90 = (bf16[4,96,384]{2,1,0:T(8,128)(2,1)S(1)}, bf16[256,512]{1,0:T(8,128)(2,1)S(1)}, bf16[256,512]{1,0:T(8,128)(2,1)S(1)}) custom-call(s32[3]{0:T(128)S(1)} %pad_add_fusion.place.refs_5_, f32[16,128]{1,0:T(8,128)S(1)} %get-tuple-element.67.refs_5_.refs_0_, f32[16,128]{1,0:T(8,128)S(1)} %get-tuple-element.68.refs_7_.refs_1_, ...), custom_call_target="tpu_custom_call" | custom-call | flops 1 | bytes 1 | tf_op jit(solution)/shard_map/pallas_call | solution.py:263
  41.0 0.9 collective-permute-done.9.refs_0_
  42.0 5.9 %collective-permute-done.10.refs_1_ = bf16[144,1024]{1,0:T(8,128)(2,1)S(1)} collective-permute-done((bf16[144,1024]{1,0:T(8,128)(2,1)S(1)}, bf16[144,1024]{1,0:T(8,128)(2,1)S(1)}, u32[]{:S(2)}, u32[]{:S(2)}) %collective-permute-start.10) | collective-permute-done | bytes 294944 | tf_op jit(solution)/shard_map/ppermute | solution.py:370
  47.9 1.6 %collective-permute-done.11.refs_2_ = bf16[144,1024]{1,0:T(8,128)(2,1)S(1)} collective-permute-done((bf16[144,1024]{1,0:T(8,128)(2,1)S(1)}, bf16[144,1024]{1,0:T(8,128)(2,1)S(1)}, u32[]{:S(2)}, u32[]{:S(2)}) %collective-permute-start.11) | collective-permute-done | bytes 294944 | tf_op jit(solution)/shard_map/ppermute | solution.py:370
  50.0 1.1 collective-permute-done.12.refs_3_
  51.1 3.8 %shard_map.91 = (bf16[3,288,384]{2,1,0:T(8,128)(2,1)S(1)}, bf16[4,80,1024]{2,1,0:T(8,128)(2,1)S(1)}, f32[16,256]{1,0:T(8,128)S(1)}) custom-call(s32[3]{0:T(128)S(1)} %pad_add_fusion.place.refs_5_, bf16[144,1024]{1,0:T(8,128)(2,1)S(1)} %collective-permute-done.9.refs_0_, bf16[144,1024]{1,0:T(8,128)(2,1)S(1)} %collective-permute-done.10.refs_1_, ...), custom_call_target="tpu_custom_call" | custom-call | flops 1 | bytes 1 | tf_op jit(solution)/shard_map/pallas_call | solution.py:239
  54.9 1.6 %collective-permute-start.13 = (bf16[3,288,384]{2,1,0:T(8,128)(2,1)S(1)}, bf16[3,288,384]{2,1,0:T(8,128)(2,1)S(1)}, u32[]{:S(2)}, u32[]{:S(2)}) collective-permute-start(bf16[3,288,384]{2,1,0:T(8,128)(2,1)S(1)} %get-tuple-element.81.refs_1_), channel_id=1, source_target_pairs={{0,2},{2,0},{1,3},{3,1},{4,6},{6,4},{5,7},{7,5},{8,10},{10,8},{9,1... | collective-permute-start | bytes 1990664 | tf_op jit(solution)/shard_map/ppermute | solution.py:370
  56.4 3.7 %shard_map.92 = (bf16[4,80,384]{2,1,0:T(8,128)(2,1)S(1)}, bf16[256,512]{1,0:T(8,128)(2,1)S(1)}, bf16[256,512]{1,0:T(8,128)(2,1)S(1)}) custom-call(s32[3]{0:T(128)S(1)} %pad_add_fusion.place.refs_5_, f32[16,256]{1,0:T(8,128)S(1)} %get-tuple-element.72.refs_8_.refs_0_, bf16[3,288,384]{2,1,0:T(8,128)(2,1)S(1)} %get-tuple-element.75.refs_1_, ...), custom_call_target="tpu_custom_call" | custom-call | flops 1 | bytes 1 | tf_op jit(solution)/shard_map/pallas_call | solution.py:263
  60.2 1.1 collective-permute-done.14.refs_0_
  61.3 5.7 %collective-permute-done.15.refs_1_ = bf16[144,1024]{1,0:T(8,128)(2,1)S(1)} collective-permute-done((bf16[144,1024]{1,0:T(8,128)(2,1)S(1)}, bf16[144,1024]{1,0:T(8,128)(2,1)S(1)}, u32[]{:S(2)}, u32[]{:S(2)}) %collective-permute-start.15) | collective-permute-done | bytes 294944 | tf_op jit(solution)/shard_map/ppermute | solution.py:370
  67.0 1.6 %collective-permute-done.16.refs_2_ = bf16[144,1024]{1,0:T(8,128)(2,1)S(1)} collective-permute-done((bf16[144,1024]{1,0:T(8,128)(2,1)S(1)}, bf16[144,1024]{1,0:T(8,128)(2,1)S(1)}, u32[]{:S(2)}, u32[]{:S(2)}) %collective-permute-start.16) | collective-permute-done | bytes 294944 | tf_op jit(solution)/shard_map/ppermute | solution.py:370
  68.7 1.4 %collective-permute-done.17.refs_3_ = bf16[144,1024]{1,0:T(8,128)(2,1)S(1)} collective-permute-done((bf16[144,1024]{1,0:T(8,128)(2,1)S(1)}, bf16[144,1024]{1,0:T(8,128)(2,1)S(1)}, u32[]{:S(2)}, u32[]{:S(2)}) %collective-permute-start.17) | collective-permute-done | bytes 294944 | tf_op jit(solution)/shard_map/ppermute | solution.py:370
  70.2 3.8 %shard_map.93 = (bf16[3,288,384]{2,1,0:T(8,128)(2,1)S(1)}, bf16[4,80,1024]{2,1,0:T(8,128)(2,1)S(1)}, f32[16,256]{1,0:T(8,128)S(1)}) custom-call(s32[3]{0:T(128)S(1)} %pad_add_fusion.place.refs_5_, bf16[144,1024]{1,0:T(8,128)(2,1)S(1)} %collective-permute-done.14.refs_0_, bf16[144,1024]{1,0:T(8,128)(2,1)S(1)} %collective-permute-done.15.refs_1_, ...), custom_call_target="tpu_custom_call" | custom-call | flops 1 | bytes 1 | tf_op jit(solution)/shard_map/pallas_call | solution.py:239
  74.0 1.6 %collective-permute-start.18 = (bf16[3,288,384]{2,1,0:T(8,128)(2,1)S(1)}, bf16[3,288,384]{2,1,0:T(8,128)(2,1)S(1)}, u32[]{:S(2)}, u32[]{:S(2)}) collective-permute-start(bf16[3,288,384]{2,1,0:T(8,128)(2,1)S(1)} %get-tuple-element.87.refs_1_), channel_id=1, source_target_pairs={{0,2},{2,0},{1,3},{3,1},{4,6},{6,4},{5,7},{7,5},{8,10},{10,8},{9,1... | collective-permute-start | bytes 1990664 | tf_op jit(solution)/shard_map/ppermute | solution.py:370
  75.6 3.8 %shard_map.94 = (bf16[4,80,384]{2,1,0:T(8,128)(2,1)S(1)}, bf16[256,512]{1,0:T(8,128)(2,1)S(1)}, bf16[256,512]{1,0:T(8,128)(2,1)S(1)}) custom-call(s32[3]{0:T(128)S(1)} %pad_add_fusion.place.refs_5_, f32[16,256]{1,0:T(8,128)S(1)} %get-tuple-element.78.refs_5_.refs_0_, bf16[3,288,384]{2,1,0:T(8,128)(2,1)S(1)} %get-tuple-element.81.refs_1_, ...), custom_call_target="tpu_custom_call" | custom-call | flops 1 | bytes 1 | tf_op jit(solution)/shard_map/pallas_call | solution.py:263
  79.9 1.0 collective-permute-done.19.refs_1_
  80.9 0.7 shard_map.95
  82.1 3.1 %collective-permute-start.21 = (bf16[128,512]{1,0:T(8,128)(2,1)S(1)}, bf16[128,512]{1,0:T(8,128)(2,1)S(1)}, u32[]{:S(2)}, u32[]{:S(2)}) collective-permute-start(bf16[128,512]{1,0:T(8,128)(2,1)S(1)} %get-tuple-element.91), channel_id=1, source_target_pairs={{0,10},{1,8},{2,11},{3,9},{4,14},{5,12},{6,15},{7,13},{8,2},{9,0},... | collective-permute-start | bytes 393224 | tf_op jit(solution)/shard_map/ppermute | solution.py:454
  86.3 6.9 %collective-permute-done.18.refs_2_ = bf16[3,288,384]{2,1,0:T(8,128)(2,1)S(1)} collective-permute-done((bf16[3,288,384]{2,1,0:T(8,128)(2,1)S(1)}, bf16[3,288,384]{2,1,0:T(8,128)(2,1)S(1)}, u32[]{:S(2)}, u32[]{:S(2)}) %collective-permute-start.18) | collective-permute-done | bytes 663584 | tf_op jit(solution)/shard_map/ppermute | solution.py:370
  93.2 3.8 %shard_map.96 = (bf16[4,80,384]{2,1,0:T(8,128)(2,1)S(1)}, bf16[256,512]{1,0:T(8,128)(2,1)S(1)}, bf16[256,512]{1,0:T(8,128)(2,1)S(1)}) custom-call(s32[3]{0:T(128)S(1)} %pad_add_fusion.place.refs_5_, f32[16,256]{1,0:T(8,128)S(1)} %get-tuple-element.84.refs_5_.refs_0_, bf16[3,288,384]{2,1,0:T(8,128)(2,1)S(1)} %get-tuple-element.87.refs_1_, ...), custom_call_target="tpu_custom_call" | custom-call | flops 1 | bytes 1 | tf_op jit(solution)/shard_map/pallas_call | solution.py:263
  97.0 0.6 shard_map.99.refs_0_
  97.7 2.7 %collective-permute-done.25.refs_1_ = bf16[256,512]{1,0:T(8,128)(2,1)S(1)} collective-permute-done((bf16[256,512]{1,0:T(8,128)(2,1)S(1)}, bf16[256,512]{1,0:T(8,128)(2,1)S(1)}, u32[]{:S(2)}, u32[]{:S(2)}) %collective-permute-start.25) | collective-permute-done | bytes 262176 | tf_op jit(solution)/shard_map/ppermute | solution.py:370
  101.2 0.7 shard_map.97
  101.8 0.9 collective-permute-start.28
  102.7 1.1 collective-permute-start.29
  103.9 2.6 %collective-permute-done.26.two = bf16[128,512]{1,0:T(8,128)(2,1)S(1)} collective-permute-done((bf16[128,512]{1,0:T(8,128)(2,1)S(1)}, bf16[128,512]{1,0:T(8,128)(2,1)S(1)}, u32[]{:S(2)}, u32[]{:S(2)}) %collective-permute-start.26) | collective-permute-done | bytes 131104 | tf_op jit(solution)/shard_map/ppermute | solution.py:370
  107.1 3.6 %shard_map.98 = (bf16[4,384,1024]{2,1,0:T(8,128)(2,1)}, f32[8,128]{1,0:T(8,128)}) custom-call(bf16[4,96,384]{2,1,0:T(8,128)(2,1)S(1)} %get-tuple-element.73.refs_7_.refs_0_, bf16[4,80,384]{2,1,0:T(8,128)(2,1)S(1)} %get-tuple-element.79.refs_7_.refs_1_, bf16[4,80,384]{2,1,0:T(8,128)(2,1)S(1)} %get-tuple-element.92.refs_5_.refs_2_, ...), custom_call_target="tpu_custom_call" | custom-call | flops 1 | bytes 1 | tf_op jit(solution)/shard_map/pallas_call | solution.py:285
  110.7 2.5 %collective-permute-done.29.refs_3_ = bf16[128,512]{1,0:T(8,128)(2,1)S(1)} collective-permute-done((bf16[128,512]{1,0:T(8,128)(2,1)S(1)}, bf16[128,512]{1,0:T(8,128)(2,1)S(1)}, u32[]{:S(2)}, u32[]{:S(2)}) %collective-permute-start.29) | collective-permute-done | bytes 131104 | tf_op jit(solution)/shard_map/ppermute | solution.py:454
  113.2 1.4 %shard_map.103 = bf16[128,1024]{1,0:T(8,128)(2,1)} custom-call(s32[3]{0:T(128)S(1)} %pad_add_fusion.place.refs_5_, bf16[128,512]{1,0:T(8,128)(2,1)S(1)} %get-tuple-element.113.stay, bf16[128,512]{1,0:T(8,128)(2,1)S(1)} %collective-permute-done.27.come, bf16[128,512]{1,0:T(8,128)(2,1)S(1)} %collective-permute-done.20.refs_0_, ...), custom_call_target="tpu_custom_call" | custom-call | flops 1 | bytes 1 | tf_op jit(solution)/shard_map/pallas_call | solution.py:300
  (51 shorter events, 6.2 us)
Async XLA Ops:
  0.7 1.0 copy-start.6
  1.8 1.0 copy-start.7
  2.8 0.7 copy-start.8
  3.5 0.7 copy-start.9
  4.9 14.1 %collective-permute-start.2 = (bf16[144,1024]{1,0:T(8,128)(2,1)S(1)}, bf16[144,1024]{1,0:T(8,128)(2,1)S(1)}, u32[]{:S(2)}, u32[]{:S(2)}) collective-permute-start(bf16[144,1024]{1,0:T(8,128)(2,1)S(1)} %get-tuple-element.62.refs_0_), channel_id=1, source_target_pairs={{0,4},{4,8},{8,12},{12,0},{1,5},{5,9},{9,13},{13,1},{2,6},{6,10},{... | collective-permute-start | bytes 884744 | tf_op jit(solution)/shard_map/ppermute | solution.py:370
  8.0 11.0 %collective-permute-start = (bf16[144,1024]{1,0:T(8,128)(2,1)S(1)}, bf16[144,1024]{1,0:T(8,128)(2,1)S(1)}, u32[]{:S(2)}, u32[]{:S(2)}) collective-permute-start(bf16[144,1024]{1,0:T(8,128)(2,1)S(1)} %get-tuple-element.65), channel_id=1, source_target_pairs={{0,2},{2,0},{1,3},{3,1},{4,6},{6,4},{5,7},{7,5},{8,10},{10,8},{9,1... | collective-permute-start | bytes 884744 | tf_op jit(solution)/shard_map/ppermute | solution.py:370
  9.5 1.9 %copy-start = (bf16[4,1024,384]{2,1,0:T(8,128)(2,1)S(1)}, bf16[4,1024,384]{2,1,0:T(8,128)(2,1)}, u32[]{:S(2)}) copy-start(bf16[4,1024,384]{2,1,0:T(8,128)(2,1)} %refs_3_.9) | copy-start | bytes 9437188
  11.4 1.9 %copy-start.2 = (bf16[4,1024,384]{2,1,0:T(8,128)(2,1)S(1)}, bf16[4,1024,384]{2,1,0:T(8,128)(2,1)}, u32[]{:S(2)}) copy-start(bf16[4,1024,384]{2,1,0:T(8,128)(2,1)} %refs_4_.15) | copy-start | bytes 9437188
  13.3 1.9 %copy-start.4 = (bf16[4,384,1024]{2,1,0:T(8,128)(2,1)S(1)}, bf16[4,384,1024]{2,1,0:T(8,128)(2,1)}, u32[]{:S(2)}) copy-start(bf16[4,384,1024]{2,1,0:T(8,128)(2,1)} %refs_6_.7) | copy-start | bytes 9437188
  15.2 6.0 %copy-start.1 = (bf16[4,1024,384]{2,1,0:T(8,128)(2,1)S(1)}, bf16[4,1024,384]{2,1,0:T(8,128)(2,1)}, u32[]{:S(2)}) copy-start(bf16[4,1024,384]{2,1,0:T(8,128)(2,1)} %refs_3_.9) | copy-start | bytes 9437188
  15.2 6.0 %copy-start.3 = (bf16[4,1024,384]{2,1,0:T(8,128)(2,1)S(1)}, bf16[4,1024,384]{2,1,0:T(8,128)(2,1)}, u32[]{:S(2)}) copy-start(bf16[4,1024,384]{2,1,0:T(8,128)(2,1)} %refs_4_.15) | copy-start | bytes 9437188
  15.2 6.0 %copy-start.5 = (bf16[4,384,1024]{2,1,0:T(8,128)(2,1)S(1)}, bf16[4,384,1024]{2,1,0:T(8,128)(2,1)}, u32[]{:S(2)}) copy-start(bf16[4,384,1024]{2,1,0:T(8,128)(2,1)} %refs_6_.7) | copy-start | bytes 9437188
  18.4 10.9 %collective-permute-start.5 = (bf16[3,160,384]{2,1,0:T(8,128)(2,1)S(1)}, bf16[3,160,384]{2,1,0:T(8,128)(2,1)S(1)}, u32[]{:S(2)}, u32[]{:S(2)}) collective-permute-start(bf16[3,160,384]{2,1,0:T(8,128)(2,1)S(1)} %get-tuple-element.69.refs_2_), channel_id=1, source_target_pairs={{0,2},{2,0},{1,3},{3,1},{4,6},{6,4},{5,7},{7,5},{8,10},{10,8},{9,1... | collective-permute-start | bytes 1105928 | tf_op jit(solution)/shard_map/ppermute | solution.py:370
  19.1 2.1 %collective-permute-start.3 = (bf16[144,1024]{1,0:T(8,128)(2,1)S(1)}, bf16[144,1024]{1,0:T(8,128)(2,1)S(1)}, u32[]{:S(2)}, u32[]{:S(2)}) collective-permute-start(bf16[144,1024]{1,0:T(8,128)(2,1)S(1)} %collective-permute-done.2.refs_0_), channel_id=1, source_target_pairs={{0,1},{1,0},{2,3},{3,2},{4,5},{5,4},{6,7},{7,6},{8,9},{9,8},{10,11... | collective-permute-start | bytes 884744 | tf_op jit(solution)/shard_map/ppermute | solution.py:370
  19.1 2.1 %collective-permute-start.1 = (bf16[144,1024]{1,0:T(8,128)(2,1)S(1)}, bf16[144,1024]{1,0:T(8,128)(2,1)S(1)}, u32[]{:S(2)}, u32[]{:S(2)}) collective-permute-start(bf16[144,1024]{1,0:T(8,128)(2,1)S(1)} %collective-permute-done.refs_0_), channel_id=1, source_target_pairs={{0,1},{1,0},{2,3},{3,2},{4,5},{5,4},{6,7},{7,6},{8,9},{9,8},{10,11... | collective-permute-start | bytes 884744 | tf_op jit(solution)/shard_map/ppermute | solution.py:370
  19.6 10.8 %collective-permute-start.6 = (bf16[144,1024]{1,0:T(8,128)(2,1)S(1)}, bf16[144,1024]{1,0:T(8,128)(2,1)S(1)}, u32[]{:S(2)}, u32[]{:S(2)}) collective-permute-start(bf16[144,1024]{1,0:T(8,128)(2,1)S(1)} %collective-permute-done.refs_0_), channel_id=1, source_target_pairs={{0,4},{4,8},{8,12},{12,0},{1,5},{5,9},{9,13},{13,1},{2,6},{6,10},{... | collective-permute-start | bytes 884744 | tf_op jit(solution)/shard_map/ppermute | solution.py:370
  24.4 11.9 %collective-permute-start.4 = (bf16[3,160,384]{2,1,0:T(8,128)(2,1)S(1)}, bf16[3,160,384]{2,1,0:T(8,128)(2,1)S(1)}, u32[]{:S(2)}, u32[]{:S(2)}) collective-permute-start(bf16[3,160,384]{2,1,0:T(8,128)(2,1)S(1)} %get-tuple-element.70.refs_4_), channel_id=1, source_target_pairs={{0,2},{2,0},{1,3},{3,1},{4,6},{6,4},{5,7},{7,5},{8,10},{10,8},{9,1... | collective-permute-start | bytes 1105928 | tf_op jit(solution)/shard_map/ppermute | solution.py:370
  30.3 2.2 %collective-permute-start.7 = (bf16[144,1024]{1,0:T(8,128)(2,1)S(1)}, bf16[144,1024]{1,0:T(8,128)(2,1)S(1)}, u32[]{:S(2)}, u32[]{:S(2)}) collective-permute-start(bf16[144,1024]{1,0:T(8,128)(2,1)S(1)} %collective-permute-done.6.refs_1_), channel_id=1, source_target_pairs={{0,1},{1,0},{2,3},{3,2},{4,5},{5,4},{6,7},{7,6},{8,9},{9,8},{10,11... | collective-permute-start | bytes 884744 | tf_op jit(solution)/shard_map/ppermute | solution.py:370
  30.4 11.6 %collective-permute-start.9 = (bf16[144,1024]{1,0:T(8,128)(2,1)S(1)}, bf16[144,1024]{1,0:T(8,128)(2,1)S(1)}, u32[]{:S(2)}, u32[]{:S(2)}) collective-permute-start(bf16[144,1024]{1,0:T(8,128)(2,1)S(1)} %collective-permute-done.2.refs_0_), channel_id=1, source_target_pairs={{0,4},{4,8},{8,12},{12,0},{1,5},{5,9},{9,13},{13,1},{2,6},{6,10},{... | collective-permute-start | bytes 884744 | tf_op jit(solution)/shard_map/ppermute | solution.py:370
  30.9 16.9 %collective-permute-start.10 = (bf16[144,1024]{1,0:T(8,128)(2,1)S(1)}, bf16[144,1024]{1,0:T(8,128)(2,1)S(1)}, u32[]{:S(2)}, u32[]{:S(2)}) collective-permute-start(bf16[144,1024]{1,0:T(8,128)(2,1)S(1)} %collective-permute-done.6.refs_1_), channel_id=1, source_target_pairs={{0,4},{4,8},{8,12},{12,0},{1,5},{5,9},{9,13},{13,1},{2,6},{6,10},{... | collective-permute-start | bytes 884744 | tf_op jit(solution)/shard_map/ppermute | solution.py:370
  36.4 18.5 %collective-permute-start.8 = (bf16[3,288,384]{2,1,0:T(8,128)(2,1)S(1)}, bf16[3,288,384]{2,1,0:T(8,128)(2,1)S(1)}, u32[]{:S(2)}, u32[]{:S(2)}) collective-permute-start(bf16[3,288,384]{2,1,0:T(8,128)(2,1)S(1)} %get-tuple-element.75.refs_1_), channel_id=1, source_target_pairs={{0,2},{2,0},{1,3},{3,1},{4,6},{6,4},{5,7},{7,5},{8,10},{10,8},{9,1... | collective-permute-start | bytes 1990664 | tf_op jit(solution)/shard_map/ppermute | solution.py:370
  47.9 1.6 %collective-permute-start.11 = (bf16[144,1024]{1,0:T(8,128)(2,1)S(1)}, bf16[144,1024]{1,0:T(8,128)(2,1)S(1)}, u32[]{:S(2)}, u32[]{:S(2)}) collective-permute-start(bf16[144,1024]{1,0:T(8,128)(2,1)S(1)} %collective-permute-done.9.refs_0_), channel_id=1, source_target_pairs={{0,1},{1,0},{2,3},{3,2},{4,5},{5,4},{6,7},{7,6},{8,9},{9,8},{10,11... | collective-permute-start | bytes 884744 | tf_op jit(solution)/shard_map/ppermute | solution.py:370
  49.5 1.6 %collective-permute-start.12 = (bf16[144,1024]{1,0:T(8,128)(2,1)S(1)}, bf16[144,1024]{1,0:T(8,128)(2,1)S(1)}, u32[]{:S(2)}, u32[]{:S(2)}) collective-permute-start(bf16[144,1024]{1,0:T(8,128)(2,1)S(1)} %collective-permute-done.10.refs_1_), channel_id=1, source_target_pairs={{0,1},{1,0},{2,3},{3,2},{4,5},{5,4},{6,7},{7,6},{8,9},{9,8},{10,11... | collective-permute-start | bytes 884744 | tf_op jit(solution)/shard_map/ppermute | solution.py:370
  49.6 11.7 %collective-permute-start.14 = (bf16[144,1024]{1,0:T(8,128)(2,1)S(1)}, bf16[144,1024]{1,0:T(8,128)(2,1)S(1)}, u32[]{:S(2)}, u32[]{:S(2)}) collective-permute-start(bf16[144,1024]{1,0:T(8,128)(2,1)S(1)} %collective-permute-done.9.refs_0_), channel_id=1, source_target_pairs={{0,4},{4,8},{8,12},{12,0},{1,5},{5,9},{9,13},{13,1},{2,6},{6,10},{... | collective-permute-start | bytes 884744 | tf_op jit(solution)/shard_map/ppermute | solution.py:370
  49.6 17.4 %collective-permute-start.15 = (bf16[144,1024]{1,0:T(8,128)(2,1)S(1)}, bf16[144,1024]{1,0:T(8,128)(2,1)S(1)}, u32[]{:S(2)}, u32[]{:S(2)}) collective-permute-start(bf16[144,1024]{1,0:T(8,128)(2,1)S(1)} %collective-permute-done.10.refs_1_), channel_id=1, source_target_pairs={{0,4},{4,8},{8,12},{12,0},{1,5},{5,9},{9,13},{13,1},{2,6},{6,10},{... | collective-permute-start | bytes 884744 | tf_op jit(solution)/shard_map/ppermute | solution.py:370
  54.9 19.1 %collective-permute-start.13 = (bf16[3,288,384]{2,1,0:T(8,128)(2,1)S(1)}, bf16[3,288,384]{2,1,0:T(8,128)(2,1)S(1)}, u32[]{:S(2)}, u32[]{:S(2)}) collective-permute-start(bf16[3,288,384]{2,1,0:T(8,128)(2,1)S(1)} %get-tuple-element.81.refs_1_), channel_id=1, source_target_pairs={{0,2},{2,0},{1,3},{3,1},{4,6},{6,4},{5,7},{7,5},{8,10},{10,8},{9,1... | collective-permute-start | bytes 1990664 | tf_op jit(solution)/shard_map/ppermute | solution.py:370
  67.0 1.6 %collective-permute-start.16 = (bf16[144,1024]{1,0:T(8,128)(2,1)S(1)}, bf16[144,1024]{1,0:T(8,128)(2,1)S(1)}, u32[]{:S(2)}, u32[]{:S(2)}) collective-permute-start(bf16[144,1024]{1,0:T(8,128)(2,1)S(1)} %collective-permute-done.14.refs_0_), channel_id=1, source_target_pairs={{0,1},{1,0},{2,3},{3,2},{4,5},{5,4},{6,7},{7,6},{8,9},{9,8},{10,11... | collective-permute-start | bytes 884744 | tf_op jit(solution)/shard_map/ppermute | solution.py:370
  68.6 1.6 %collective-permute-start.17 = (bf16[144,1024]{1,0:T(8,128)(2,1)S(1)}, bf16[144,1024]{1,0:T(8,128)(2,1)S(1)}, u32[]{:S(2)}, u32[]{:S(2)}) collective-permute-start(bf16[144,1024]{1,0:T(8,128)(2,1)S(1)} %collective-permute-done.15.refs_1_), channel_id=1, source_target_pairs={{0,1},{1,0},{2,3},{3,2},{4,5},{5,4},{6,7},{7,6},{8,9},{9,8},{10,11... | collective-permute-start | bytes 884744 | tf_op jit(solution)/shard_map/ppermute | solution.py:370
  74.0 19.1 %collective-permute-start.18 = (bf16[3,288,384]{2,1,0:T(8,128)(2,1)S(1)}, bf16[3,288,384]{2,1,0:T(8,128)(2,1)S(1)}, u32[]{:S(2)}, u32[]{:S(2)}) collective-permute-start(bf16[3,288,384]{2,1,0:T(8,128)(2,1)S(1)} %get-tuple-element.87.refs_1_), channel_id=1, source_target_pairs={{0,2},{2,0},{1,3},{3,1},{4,6},{6,4},{5,7},{7,5},{8,10},{10,8},{9,1... | collective-permute-start | bytes 1990664 | tf_op jit(solution)/shard_map/ppermute | solution.py:370
  79.3 1.6 %collective-permute-start.19 = (bf16[256,512]{1,0:T(8,128)(2,1)S(1)}, bf16[256,512]{1,0:T(8,128)(2,1)S(1)}, u32[]{:S(2)}, u32[]{:S(2)}) collective-permute-start(bf16[256,512]{1,0:T(8,128)(2,1)S(1)} %get-tuple-element.89), channel_id=1, source_target_pairs={{0,1},{1,0},{2,3},{3,2},{4,5},{5,4},{6,7},{7,6},{8,9},{9,8},{10,11... | collective-permute-start | bytes 786440 | tf_op jit(solution)/shard_map/ppermute | solution.py:370
  79.4 5.8 %collective-permute-start.24 = (bf16[256,512]{1,0:T(8,128)(2,1)S(1)}, bf16[256,512]{1,0:T(8,128)(2,1)S(1)}, u32[]{:S(2)}, u32[]{:S(2)}) collective-permute-start(bf16[256,512]{1,0:T(8,128)(2,1)S(1)} %get-tuple-element.109), channel_id=1, source_target_pairs={{0,1},{1,0},{2,3},{3,2},{4,5},{5,4},{6,7},{7,6},{8,9},{9,8},{10,11... | collective-permute-start | bytes 786440 | tf_op jit(solution)/shard_map/ppermute | solution.py:370
  81.6 15.3 %collective-permute-start.20 = (bf16[128,512]{1,0:T(8,128)(2,1)S(1)}, bf16[128,512]{1,0:T(8,128)(2,1)S(1)}, u32[]{:S(2)}, u32[]{:S(2)}) collective-permute-start(bf16[128,512]{1,0:T(8,128)(2,1)S(1)} %get-tuple-element.90), channel_id=1, source_target_pairs={{0,8},{1,10},{2,9},{3,11},{4,12},{5,14},{6,13},{7,15},{8,0},{9,2},... | collective-permute-start | bytes 393224 | tf_op jit(solution)/shard_map/ppermute | solution.py:454
  82.1 14.8 %collective-permute-start.21 = (bf16[128,512]{1,0:T(8,128)(2,1)S(1)}, bf16[128,512]{1,0:T(8,128)(2,1)S(1)}, u32[]{:S(2)}, u32[]{:S(2)}) collective-permute-start(bf16[128,512]{1,0:T(8,128)(2,1)S(1)} %get-tuple-element.91), channel_id=1, source_target_pairs={{0,10},{1,8},{2,11},{3,9},{4,14},{5,12},{6,15},{7,13},{8,2},{9,0},... | collective-permute-start | bytes 393224 | tf_op jit(solution)/shard_map/ppermute | solution.py:454
  85.2 11.8 %collective-permute-start.23 = (bf16[256,512]{1,0:T(8,128)(2,1)S(1)}, bf16[256,512]{1,0:T(8,128)(2,1)S(1)}, u32[]{:S(2)}, u32[]{:S(2)}) collective-permute-start(bf16[256,512]{1,0:T(8,128)(2,1)S(1)} %get-tuple-element.107), channel_id=1, source_target_pairs={{0,1},{1,0},{2,3},{3,2},{4,5},{5,4},{6,7},{7,6},{8,9},{9,8},{10,11... | collective-permute-start | bytes 786440 | tf_op jit(solution)/shard_map/ppermute | solution.py:370
  85.9 14.5 %collective-permute-start.25 = (bf16[256,512]{1,0:T(8,128)(2,1)S(1)}, bf16[256,512]{1,0:T(8,128)(2,1)S(1)}, u32[]{:S(2)}, u32[]{:S(2)}) collective-permute-start(bf16[256,512]{1,0:T(8,128)(2,1)S(1)} %shard_map.100), channel_id=1, source_target_pairs={{0,12},{4,0},{8,4},{12,8},{1,13},{5,1},{9,5},{13,9},{2,14},{6,2},{... | collective-permute-start | bytes 786440 | tf_op jit(solution)/shard_map/ppermute | solution.py:370
  97.0 4.2 %collective-permute-start.22 = (bf16[256,512]{1,0:T(8,128)(2,1)S(1)}, bf16[256,512]{1,0:T(8,128)(2,1)S(1)}, u32[]{:S(2)}, u32[]{:S(2)}) collective-permute-start(bf16[256,512]{1,0:T(8,128)(2,1)S(1)} %get-tuple-element.96), channel_id=1, source_target_pairs={{0,1},{1,0},{2,3},{3,2},{4,5},{5,4},{6,7},{7,6},{8,9},{9,8},{10,11... | collective-permute-start | bytes 786440 | tf_op jit(solution)/shard_map/ppermute | solution.py:370
  100.9 5.5 %collective-permute-start.26 = (bf16[128,512]{1,0:T(8,128)(2,1)S(1)}, bf16[128,512]{1,0:T(8,128)(2,1)S(1)}, u32[]{:S(2)}, u32[]{:S(2)}) collective-permute-start(bf16[128,512]{1,0:T(8,128)(2,1)S(1)} %get-tuple-element.112), channel_id=1, source_target_pairs={{0,2},{2,0},{1,3},{3,1},{4,6},{6,4},{5,7},{7,5},{8,10},{10,8},{9,1... | collective-permute-start | bytes 393224 | tf_op jit(solution)/shard_map/ppermute | solution.py:370
  101.8 8.9 %collective-permute-start.28 = (bf16[128,512]{1,0:T(8,128)(2,1)S(1)}, bf16[128,512]{1,0:T(8,128)(2,1)S(1)}, u32[]{:S(2)}, u32[]{:S(2)}) collective-permute-start(bf16[128,512]{1,0:T(8,128)(2,1)S(1)} %get-tuple-element.118), channel_id=1, source_target_pairs={{0,4},{1,6},{2,5},{3,7},{4,8},{5,10},{6,9},{7,11},{8,12},{9,14},{1... | collective-permute-start | bytes 393224 | tf_op jit(solution)/shard_map/ppermute | solution.py:454
  102.7 10.5 %collective-permute-start.29 = (bf16[128,512]{1,0:T(8,128)(2,1)S(1)}, bf16[128,512]{1,0:T(8,128)(2,1)S(1)}, u32[]{:S(2)}, u32[]{:S(2)}) collective-permute-start(bf16[128,512]{1,0:T(8,128)(2,1)S(1)} %get-tuple-element.120), channel_id=1, source_target_pairs={{0,6},{1,4},{2,7},{3,5},{4,10},{5,8},{6,11},{7,9},{8,14},{9,12},{1... | collective-permute-start | bytes 393224 | tf_op jit(solution)/shard_map/ppermute | solution.py:454
  107.0 6.2 %collective-permute-start.27 = (bf16[128,512]{1,0:T(8,128)(2,1)S(1)}, bf16[128,512]{1,0:T(8,128)(2,1)S(1)}, u32[]{:S(2)}, u32[]{:S(2)}) collective-permute-start(bf16[128,512]{1,0:T(8,128)(2,1)S(1)} %get-tuple-element.114), channel_id=1, source_target_pairs={{0,1},{1,0},{2,3},{3,2},{4,5},{5,4},{6,7},{7,6},{8,9},{9,8},{10,11... | collective-permute-start | bytes 393224 | tf_op jit(solution)/shard_map/ppermute | solution.py:370

commit v4 on v3

--- a/solution.py
+++ b/solution.py
@@ -396,8 +396,11 @@
     received = [shift(one, "dp", by) for by, one in enumerate(sends, 1)]
     parts = [ahead([own], [own_other], place)]
     blocks, swapped = [[own] + received], [[]]
-    for _ in range(1, owners):
-        blocks.append([shift(one, "expert", 1) for one in blocks[-1]])
+    for by in range(1, owners):
+        blocks.append([])
+        for one in blocks[-2]:
+            one = after(one, *blocks[-1]) if by == 2 else one
+            blocks[-1].append(shift(one, "expert", 1))
     blocks.append([])
     swapped.append([shift(blocks[1][0], "sub", 1)])
     for one in received:

time: 115 us -> 114 us (level)
  waiting for transfers between devices: 39.4 us -> 34.5 us
  starting transfers between devices: 22.8 us -> 26.7 us
    ppermute x26, waiting for transfers between devices: 36.9 us -> 30.1 us  [shift(): lax.ppermute(array, axis, [(i, (i + by) % size) for i in range(size)])]
    ppermute x26, starting transfers between devices: 17.1 us -> 19.4 us  [shift(): lax.ppermute(array, axis, [(i, (i + by) % size) for i in range(size)])]
    ppermute x4, waiting for transfers between devices: 2.49 us -> 4.34 us  [sent_straight(): far.append(lax.ppermute(piece, ('expert', 'dp', 'sub'), pairs))]
    ppermute x4, starting transfers between devices: 5.65 us -> 7.39 us  [sent_straight(): far.append(lax.ppermute(piece, ('expert', 'dp', 'sub'), pairs))]
  transfers between devices with their start and end apart: 30 -> 30, of which waited for: 15 -> 17; matrix products, arithmetic and copies ran while one was open for 0% -> 0% of each run, Pallas kernels for 35% -> 35%
where the time goes in v4:
time: 114 us
  Pallas kernels  42.3 us (37%)
  waiting for transfers between devices  34.5 us (30%)
  starting transfers between devices  26.7 us (23%)
  local copies, waits for them, and re-layouts  9.12 us (8%)
    ppermute x26, waiting for transfers between devices, shift(): lax.ppermute(array, axis, [(i, (i + by) % size) for i in range(size)])  30.1 us
    ppermute x26, starting transfers between devices, shift(): lax.ppermute(array, axis, [(i, (i + by) % size) for i in range(size)])  19.4 us
    pallas_call x5, Pallas kernels, forward(): pl.pallas_call(functools.partial(forward_kernel, shards, token_rows, chos...  18 us
    pallas_call x4, Pallas kernels, backward(): pl.pallas_call(functools.partial(backward_kernel, capacity, parts, wide),...  14.9 us
    unnamed x20, local copies, waits for them, and re-layouts  9.12 us
    ppermute x4, starting transfers between devices, sent_straight(): far.append(lax.ppermute(piece, ('expert', 'dp', 'sub'), pairs))  7.39 us
    pallas_call x7, Pallas kernels, small(): pl.pallas_call(kernel, in_specs=[SMEM] + [WHOLE] * (len(arrays) - 1), out...  5.07 us
    ppermute x4, waiting for transfers between devices, sent_straight(): far.append(lax.ppermute(piece, ('expert', 'dp', 'sub'), pairs))  4.34 us
  transfers between devices with their start and end apart: 30, of which 17 were waited for; matrix products, arithmetic and copies ran while one was open for 0% of the time, Pallas kernels for 35%

profile of v4, /device:TPU:0, one launch (start us, length us, event | category | flops | bytes accessed | tf_op | source)
XLA Modules:
  0.0 113.6 jit_solution(10146079052690884981)
XLA Ops:
  0.7 1.0 copy-done.6
  1.8 1.0 copy-done.7
  2.8 0.7 copy-done.8
  3.5 0.7 copy-done.9
  4.2 0.8 shard_map.86
  4.9 3.1 %collective-permute-start.2 = (bf16[144,1024]{1,0:T(8,128)(2,1)S(1)}, bf16[144,1024]{1,0:T(8,128)(2,1)S(1)}, u32[]{:S(2)}, u32[]{:S(2)}) collective-permute-start(bf16[144,1024]{1,0:T(8,128)(2,1)S(1)} %get-tuple-element.63.refs_0_), channel_id=1, source_target_pairs={{0,4},{4,8},{8,12},{12,0},{1,5},{5,9},{9,13},{13,1},{2,6},{6,10},{... | collective-permute-start | bytes 884744 | tf_op jit(solution)/shard_map/ppermute | solution.py:370
  8.0 1.5 %collective-permute-start = (bf16[144,1024]{1,0:T(8,128)(2,1)S(1)}, bf16[144,1024]{1,0:T(8,128)(2,1)S(1)}, u32[]{:S(2)}, u32[]{:S(2)}) collective-permute-start(bf16[144,1024]{1,0:T(8,128)(2,1)S(1)} %get-tuple-element.66), channel_id=1, source_target_pairs={{0,2},{2,0},{1,3},{3,1},{4,6},{6,4},{5,7},{7,5},{8,10},{10,8},{9,1... | collective-permute-start | bytes 884744 | tf_op jit(solution)/shard_map/ppermute | solution.py:370
  9.5 1.9 %copy-done = bf16[4,1024,384]{2,1,0:T(8,128)(2,1)S(1)} copy-done((bf16[4,1024,384]{2,1,0:T(8,128)(2,1)S(1)}, bf16[4,1024,384]{2,1,0:T(8,128)(2,1)}, u32[]{:S(2)}) %copy-start) | copy-done | bytes 3145752
  11.4 1.9 %copy-done.2 = bf16[4,1024,384]{2,1,0:T(8,128)(2,1)S(1)} copy-done((bf16[4,1024,384]{2,1,0:T(8,128)(2,1)S(1)}, bf16[4,1024,384]{2,1,0:T(8,128)(2,1)}, u32[]{:S(2)}) %copy-start.2) | copy-done | bytes 3145752
  13.3 1.9 %copy-done.4 = bf16[4,384,1024]{2,1,0:T(8,128)(2,1)S(1)} copy-done((bf16[4,384,1024]{2,1,0:T(8,128)(2,1)S(1)}, bf16[4,384,1024]{2,1,0:T(8,128)(2,1)}, u32[]{:S(2)}) %copy-start.4) | copy-done | bytes 3145752
  15.2 3.3 %shard_map.87 = (bf16[3,160,384]{2,1,0:T(8,128)(2,1)S(1)}, bf16[4,48,1024]{2,1,0:T(8,128)(2,1)S(1)}, f32[16,128]{1,0:T(8,128)S(1)}) custom-call(s32[3]{0:T(128)S(1)} %pad_add_fusion.place.refs_5_, bf16[144,1024]{1,0:T(8,128)(2,1)S(1)} %get-tuple-element.63.refs_0_, bf16[144,1024]{1,0:T(8,128)(2,1)S(1)} %get-tuple-element.64.refs_1_, ...), custom_call_target="tpu_custom_call" | custom-call | flops 1 | bytes 1 | tf_op jit(solution)/shard_map/pallas_call | solution.py:239
  19.6 1.6 %collective-permute-start.6 = (bf16[144,1024]{1,0:T(8,128)(2,1)S(1)}, bf16[144,1024]{1,0:T(8,128)(2,1)S(1)}, u32[]{:S(2)}, u32[]{:S(2)}) collective-permute-start(bf16[144,1024]{1,0:T(8,128)(2,1)S(1)} %collective-permute-done.refs_0_), channel_id=1, source_target_pairs={{0,4},{4,8},{8,12},{12,0},{1,5},{5,9},{9,13},{13,1},{2,6},{6,10},{... | collective-permute-start | bytes 884744 | tf_op jit(solution)/shard_map/ppermute | solution.py:370
  21.1 1.6 %collective-permute-start.9 = (bf16[144,1024]{1,0:T(8,128)(2,1)S(1)}, bf16[144,1024]{1,0:T(8,128)(2,1)S(1)}, u32[]{:S(2)}, u32[]{:S(2)}) collective-permute-start(bf16[144,1024]{1,0:T(8,128)(2,1)S(1)} %collective-permute-done.2.refs_0_), channel_id=1, source_target_pairs={{0,4},{4,8},{8,12},{12,0},{1,5},{5,9},{9,13},{13,1},{2,6},{6,10},{... | collective-permute-start | bytes 884744 | tf_op jit(solution)/shard_map/ppermute | solution.py:370
  22.8 3.3 %shard_map.88 = (bf16[3,160,384]{2,1,0:T(8,128)(2,1)S(1)}, bf16[4,48,1024]{2,1,0:T(8,128)(2,1)S(1)}, f32[16,128]{1,0:T(8,128)S(1)}) custom-call(s32[3]{0:T(128)S(1)} %pad_add_fusion.place.refs_5_, bf16[144,1024]{1,0:T(8,128)(2,1)S(1)} %collective-permute-done.refs_0_, bf16[144,1024]{1,0:T(8,128)(2,1)S(1)} %collective-permute-done.1.refs_1_, ...), custom_call_target="tpu_custom_call" | custom-call | flops 1 | bytes 1 | tf_op jit(solution)/shard_map/pallas_call | solution.py:239
  26.0 1.6 %collective-permute-start.4 = (bf16[3,160,384]{2,1,0:T(8,128)(2,1)S(1)}, bf16[3,160,384]{2,1,0:T(8,128)(2,1)S(1)}, u32[]{:S(2)}, u32[]{:S(2)}) collective-permute-start(bf16[3,160,384]{2,1,0:T(8,128)(2,1)S(1)} %get-tuple-element.71.refs_4_), channel_id=1, source_target_pairs={{0,2},{2,0},{1,3},{3,1},{4,6},{6,4},{5,7},{7,5},{8,10},{10,8},{9,1... | collective-permute-start | bytes 1105928 | tf_op jit(solution)/shard_map/ppermute | solution.py:370
  27.6 0.7 collective-permute-done.5.refs_5_
  28.3 2.9 %collective-permute-done.6.refs_1_ = bf16[144,1024]{1,0:T(8,128)(2,1)S(1)} collective-permute-done((bf16[144,1024]{1,0:T(8,128)(2,1)S(1)}, bf16[144,1024]{1,0:T(8,128)(2,1)S(1)}, u32[]{:S(2)}, u32[]{:S(2)}) %collective-permute-start.6) | collective-permute-done | bytes 294944 | tf_op jit(solution)/shard_map/ppermute | solution.py:370
  31.2 5.4 %collective-permute-done.9.refs_0_ = bf16[144,1024]{1,0:T(8,128)(2,1)S(1)} collective-permute-done((bf16[144,1024]{1,0:T(8,128)(2,1)S(1)}, bf16[144,1024]{1,0:T(8,128)(2,1)S(1)}, u32[]{:S(2)}, u32[]{:S(2)}) %collective-permute-start.9) | collective-permute-done | bytes 294944 | tf_op jit(solution)/shard_map/ppermute | solution.py:370
  36.7 3.8 %shard_map.89 = (bf16[3,288,384]{2,1,0:T(8,128)(2,1)S(1)}, bf16[4,80,1024]{2,1,0:T(8,128)(2,1)S(1)}, f32[16,256]{1,0:T(8,128)S(1)}) custom-call(s32[3]{0:T(128)S(1)} %pad_add_fusion.place.refs_5_, bf16[144,1024]{1,0:T(8,128)(2,1)S(1)} %collective-permute-done.2.refs_0_, bf16[144,1024]{1,0:T(8,128)(2,1)S(1)} %collective-permute-done.6.refs_1_, ...), custom_call_target="tpu_custom_call" | custom-call | flops 1 | bytes 1 | tf_op jit(solution)/shard_map/pallas_call | solution.py:239
  40.5 1.6 %collective-permute-start.8 = (bf16[3,288,384]{2,1,0:T(8,128)(2,1)S(1)}, bf16[3,288,384]{2,1,0:T(8,128)(2,1)S(1)}, u32[]{:S(2)}, u32[]{:S(2)}) collective-permute-start(bf16[3,288,384]{2,1,0:T(8,128)(2,1)S(1)} %get-tuple-element.76.refs_1_), channel_id=1, source_target_pairs={{0,2},{2,0},{1,3},{3,1},{4,6},{6,4},{5,7},{7,5},{8,10},{10,8},{9,1... | collective-permute-start | bytes 1990664 | tf_op jit(solution)/shard_map/ppermute | solution.py:370
  42.1 3.7 %shard_map.90 = (bf16[4,96,384]{2,1,0:T(8,128)(2,1)S(1)}, bf16[256,512]{1,0:T(8,128)(2,1)S(1)}, bf16[256,512]{1,0:T(8,128)(2,1)S(1)}) custom-call(s32[3]{0:T(128)S(1)} %pad_add_fusion.place.refs_5_, f32[16,128]{1,0:T(8,128)S(1)} %get-tuple-element.68.refs_5_.refs_0_, f32[16,128]{1,0:T(8,128)S(1)} %get-tuple-element.69.refs_7_.refs_1_, ...), custom_call_target="tpu_custom_call" | custom-call | flops 1 | bytes 1 | tf_op jit(solution)/shard_map/pallas_call | solution.py:263
  45.7 0.9 collective-permute-done.10.refs_1_
  46.6 1.6 %collective-permute-done.11.refs_2_ = bf16[144,1024]{1,0:T(8,128)(2,1)S(1)} collective-permute-done((bf16[144,1024]{1,0:T(8,128)(2,1)S(1)}, bf16[144,1024]{1,0:T(8,128)(2,1)S(1)}, u32[]{:S(2)}, u32[]{:S(2)}) %collective-permute-start.11) | collective-permute-done | bytes 294944 | tf_op jit(solution)/shard_map/ppermute | solution.py:370
  49.8 3.8 %shard_map.91 = (bf16[3,288,384]{2,1,0:T(8,128)(2,1)S(1)}, bf16[4,80,1024]{2,1,0:T(8,128)(2,1)S(1)}, f32[16,256]{1,0:T(8,128)S(1)}) custom-call(s32[3]{0:T(128)S(1)} %pad_add_fusion.place.refs_5_, bf16[144,1024]{1,0:T(8,128)(2,1)S(1)} %collective-permute-done.9.refs_0_, bf16[144,1024]{1,0:T(8,128)(2,1)S(1)} %collective-permute-done.10.refs_1_, ...), custom_call_target="tpu_custom_call" | custom-call | flops 1 | bytes 1 | tf_op jit(solution)/shard_map/pallas_call | solution.py:239
  53.6 3.0 %collective-permute-done.8.refs_2_ = bf16[3,288,384]{2,1,0:T(8,128)(2,1)S(1)} collective-permute-done((bf16[3,288,384]{2,1,0:T(8,128)(2,1)S(1)}, bf16[3,288,384]{2,1,0:T(8,128)(2,1)S(1)}, u32[]{:S(2)}, u32[]{:S(2)}) %collective-permute-start.8) | collective-permute-done | bytes 663584 | tf_op jit(solution)/shard_map/ppermute | solution.py:370
  56.6 1.5 %collective-permute-start.13 = (bf16[3,288,384]{2,1,0:T(8,128)(2,1)S(1)}, bf16[3,288,384]{2,1,0:T(8,128)(2,1)S(1)}, u32[]{:S(2)}, u32[]{:S(2)}) collective-permute-start(bf16[3,288,384]{2,1,0:T(8,128)(2,1)S(1)} %get-tuple-element.83.refs_1_), channel_id=1, source_target_pairs={{0,2},{2,0},{1,3},{3,1},{4,6},{6,4},{5,7},{7,5},{8,10},{10,8},{9,1... | collective-permute-start | bytes 1990664 | tf_op jit(solution)/shard_map/ppermute | solution.py:370
  58.1 3.8 %shard_map.92 = (bf16[4,80,384]{2,1,0:T(8,128)(2,1)S(1)}, bf16[256,512]{1,0:T(8,128)(2,1)S(1)}, bf16[256,512]{1,0:T(8,128)(2,1)S(1)}) custom-call(s32[3]{0:T(128)S(1)} %pad_add_fusion.place.refs_5_, f32[16,256]{1,0:T(8,128)S(1)} %get-tuple-element.73.refs_8_.refs_0_, bf16[3,288,384]{2,1,0:T(8,128)(2,1)S(1)} %get-tuple-element.76.refs_1_, ...), custom_call_target="tpu_custom_call" | custom-call | flops 1 | bytes 1 | tf_op jit(solution)/shard_map/pallas_call | solution.py:263
  61.9 3.9 %collective-permute-done.15.refs_1_ = bf16[144,1024]{1,0:T(8,128)(2,1)S(1)} collective-permute-done((bf16[144,1024]{1,0:T(8,128)(2,1)S(1)}, bf16[144,1024]{1,0:T(8,128)(2,1)S(1)}, u32[]{:S(2)}, u32[]{:S(2)}) %collective-permute-start.15) | collective-permute-done | bytes 294944 | tf_op jit(solution)/shard_map/ppermute | solution.py:370
  65.7 1.6 %collective-permute-done.16.refs_2_ = bf16[144,1024]{1,0:T(8,128)(2,1)S(1)} collective-permute-done((bf16[144,1024]{1,0:T(8,128)(2,1)S(1)}, bf16[144,1024]{1,0:T(8,128)(2,1)S(1)}, u32[]{:S(2)}, u32[]{:S(2)}) %collective-permute-start.16) | collective-permute-done | bytes 294944 | tf_op jit(solution)/shard_map/ppermute | solution.py:370
  67.5 1.4 %collective-permute-done.17.refs_3_ = bf16[144,1024]{1,0:T(8,128)(2,1)S(1)} collective-permute-done((bf16[144,1024]{1,0:T(8,128)(2,1)S(1)}, bf16[144,1024]{1,0:T(8,128)(2,1)S(1)}, u32[]{:S(2)}, u32[]{:S(2)}) %collective-permute-start.17) | collective-permute-done | bytes 294944 | tf_op jit(solution)/shard_map/ppermute | solution.py:370
  68.9 3.8 %shard_map.93 = (bf16[3,288,384]{2,1,0:T(8,128)(2,1)S(1)}, bf16[4,80,1024]{2,1,0:T(8,128)(2,1)S(1)}, f32[16,256]{1,0:T(8,128)S(1)}) custom-call(s32[3]{0:T(128)S(1)} %pad_add_fusion.place.refs_5_, bf16[144,1024]{1,0:T(8,128)(2,1)S(1)} %collective-permute-done.14.refs_0_, bf16[144,1024]{1,0:T(8,128)(2,1)S(1)} %collective-permute-done.15.refs_1_, ...), custom_call_target="tpu_custom_call" | custom-call | flops 1 | bytes 1 | tf_op jit(solution)/shard_map/pallas_call | solution.py:239
  72.7 1.6 %collective-permute-start.18 = (bf16[3,288,384]{2,1,0:T(8,128)(2,1)S(1)}, bf16[3,288,384]{2,1,0:T(8,128)(2,1)S(1)}, u32[]{:S(2)}, u32[]{:S(2)}) collective-permute-start(bf16[3,288,384]{2,1,0:T(8,128)(2,1)S(1)} %get-tuple-element.89.refs_1_), channel_id=1, source_target_pairs={{0,2},{2,0},{1,3},{3,1},{4,6},{6,4},{5,7},{7,5},{8,10},{10,8},{9,1... | collective-permute-start | bytes 1990664 | tf_op jit(solution)/shard_map/ppermute | solution.py:370
  74.3 3.8 %shard_map.94 = (bf16[4,80,384]{2,1,0:T(8,128)(2,1)S(1)}, bf16[256,512]{1,0:T(8,128)(2,1)S(1)}, bf16[256,512]{1,0:T(8,128)(2,1)S(1)}) custom-call(s32[3]{0:T(128)S(1)} %pad_add_fusion.place.refs_5_, f32[16,256]{1,0:T(8,128)S(1)} %get-tuple-element.80.refs_5_.refs_0_, bf16[3,288,384]{2,1,0:T(8,128)(2,1)S(1)} %get-tuple-element.83.refs_1_, ...), custom_call_target="tpu_custom_call" | custom-call | flops 1 | bytes 1 | tf_op jit(solution)/shard_map/pallas_call | solution.py:263
  78.6 1.0 collective-permute-done.19.refs_1_
  79.7 0.7 shard_map.95
  80.8 3.1 %collective-permute-start.21 = (bf16[128,512]{1,0:T(8,128)(2,1)S(1)}, bf16[128,512]{1,0:T(8,128)(2,1)S(1)}, u32[]{:S(2)}, u32[]{:S(2)}) collective-permute-start(bf16[128,512]{1,0:T(8,128)(2,1)S(1)} %get-tuple-element.93), channel_id=1, source_target_pairs={{0,10},{1,8},{2,11},{3,9},{4,14},{5,12},{6,15},{7,13},{8,2},{9,0},... | collective-permute-start | bytes 393224 | tf_op jit(solution)/shard_map/ppermute | solution.py:457
  84.6 2.5 %collective-permute-start.25 = (bf16[256,512]{1,0:T(8,128)(2,1)S(1)}, bf16[256,512]{1,0:T(8,128)(2,1)S(1)}, u32[]{:S(2)}, u32[]{:S(2)}) collective-permute-start(bf16[256,512]{1,0:T(8,128)(2,1)S(1)} %shard_map.100), channel_id=1, source_target_pairs={{0,12},{4,0},{8,4},{12,8},{1,13},{5,1},{9,5},{13,9},{2,14},{6,2},{... | collective-permute-start | bytes 786440 | tf_op jit(solution)/shard_map/ppermute | solution.py:370
  87.0 3.1 %collective-permute-done.18.refs_2_ = bf16[3,288,384]{2,1,0:T(8,128)(2,1)S(1)} collective-permute-done((bf16[3,288,384]{2,1,0:T(8,128)(2,1)S(1)}, bf16[3,288,384]{2,1,0:T(8,128)(2,1)S(1)}, u32[]{:S(2)}, u32[]{:S(2)}) %collective-permute-start.18) | collective-permute-done | bytes 663584 | tf_op jit(solution)/shard_map/ppermute | solution.py:370
  90.1 3.8 %shard_map.96 = (bf16[4,80,384]{2,1,0:T(8,128)(2,1)S(1)}, bf16[256,512]{1,0:T(8,128)(2,1)S(1)}, bf16[256,512]{1,0:T(8,128)(2,1)S(1)}) custom-call(s32[3]{0:T(128)S(1)} %pad_add_fusion.place.refs_5_, f32[16,256]{1,0:T(8,128)S(1)} %get-tuple-element.86.refs_5_.refs_0_, bf16[3,288,384]{2,1,0:T(8,128)(2,1)S(1)} %get-tuple-element.89.refs_1_, ...), custom_call_target="tpu_custom_call" | custom-call | flops 1 | bytes 1 | tf_op jit(solution)/shard_map/pallas_call | solution.py:263
  93.9 1.3 %collective-permute-done.21.refs_1_ = bf16[128,512]{1,0:T(8,128)(2,1)S(1)} collective-permute-done((bf16[128,512]{1,0:T(8,128)(2,1)S(1)}, bf16[128,512]{1,0:T(8,128)(2,1)S(1)}, u32[]{:S(2)}, u32[]{:S(2)}) %collective-permute-start.21) | collective-permute-done | bytes 131104 | tf_op jit(solution)/shard_map/ppermute | solution.py:457
  95.8 3.3 %collective-permute-done.25.refs_1_ = bf16[256,512]{1,0:T(8,128)(2,1)S(1)} collective-permute-done((bf16[256,512]{1,0:T(8,128)(2,1)S(1)}, bf16[256,512]{1,0:T(8,128)(2,1)S(1)}, u32[]{:S(2)}, u32[]{:S(2)}) %collective-permute-start.25) | collective-permute-done | bytes 262176 | tf_op jit(solution)/shard_map/ppermute | solution.py:370
  99.8 0.7 shard_map.97
  100.5 2.5 %collective-permute-start.28 = (bf16[128,512]{1,0:T(8,128)(2,1)S(1)}, bf16[128,512]{1,0:T(8,128)(2,1)S(1)}, u32[]{:S(2)}, u32[]{:S(2)}) collective-permute-start(bf16[128,512]{1,0:T(8,128)(2,1)S(1)} %get-tuple-element.120), channel_id=1, source_target_pairs={{0,4},{1,6},{2,5},{3,7},{4,8},{5,10},{6,9},{7,11},{8,12},{9,14},{1... | collective-permute-start | bytes 393224 | tf_op jit(solution)/shard_map/ppermute | solution.py:457
  103.0 1.2 %collective-permute-start.29 = (bf16[128,512]{1,0:T(8,128)(2,1)S(1)}, bf16[128,512]{1,0:T(8,128)(2,1)S(1)}, u32[]{:S(2)}, u32[]{:S(2)}) collective-permute-start(bf16[128,512]{1,0:T(8,128)(2,1)S(1)} %get-tuple-element.122), channel_id=1, source_target_pairs={{0,6},{1,4},{2,7},{3,5},{4,10},{5,8},{6,11},{7,9},{8,14},{9,12},{1... | collective-permute-start | bytes 393224 | tf_op jit(solution)/shard_map/ppermute | solution.py:457
  105.5 3.6 %shard_map.98 = (bf16[4,384,1024]{2,1,0:T(8,128)(2,1)}, f32[8,128]{1,0:T(8,128)}) custom-call(bf16[4,96,384]{2,1,0:T(8,128)(2,1)S(1)} %get-tuple-element.74.refs_7_.refs_0_, bf16[4,80,384]{2,1,0:T(8,128)(2,1)S(1)} %get-tuple-element.81.refs_7_.refs_1_, bf16[4,80,384]{2,1,0:T(8,128)(2,1)S(1)} %get-tuple-element.94.refs_5_.refs_2_, ...), custom_call_target="tpu_custom_call" | custom-call | flops 1 | bytes 1 | tf_op jit(solution)/shard_map/pallas_call | solution.py:285
  109.1 1.0 collective-permute-done.28.refs_2_
  110.2 2.0 %collective-permute-done.29.refs_3_ = bf16[128,512]{1,0:T(8,128)(2,1)S(1)} collective-permute-done((bf16[128,512]{1,0:T(8,128)(2,1)S(1)}, bf16[128,512]{1,0:T(8,128)(2,1)S(1)}, u32[]{:S(2)}, u32[]{:S(2)}) %collective-permute-start.29) | collective-permute-done | bytes 131104 | tf_op jit(solution)/shard_map/ppermute | solution.py:457
  112.2 1.4 %shard_map.103 = bf16[128,1024]{1,0:T(8,128)(2,1)} custom-call(s32[3]{0:T(128)S(1)} %pad_add_fusion.place.refs_5_, bf16[128,512]{1,0:T(8,128)(2,1)S(1)} %get-tuple-element.115.stay, bf16[128,512]{1,0:T(8,128)(2,1)S(1)} %collective-permute-done.27.come, bf16[128,512]{1,0:T(8,128)(2,1)S(1)} %collective-permute-done.20.refs_0_, ...), custom_call_target="tpu_custom_call" | custom-call | flops 1 | bytes 1 | tf_op jit(solution)/shard_map/pallas_call | solution.py:300
  (51 shorter events, 7.2 us)
Async XLA Ops:
  0.7 1.0 copy-start.6
  1.8 1.0 copy-start.7
  2.8 0.7 copy-start.8
  3.5 0.7 copy-start.9
  4.9 14.1 %collective-permute-start.2 = (bf16[144,1024]{1,0:T(8,128)(2,1)S(1)}, bf16[144,1024]{1,0:T(8,128)(2,1)S(1)}, u32[]{:S(2)}, u32[]{:S(2)}) collective-permute-start(bf16[144,1024]{1,0:T(8,128)(2,1)S(1)} %get-tuple-element.63.refs_0_), channel_id=1, source_target_pairs={{0,4},{4,8},{8,12},{12,0},{1,5},{5,9},{9,13},{13,1},{2,6},{6,10},{... | collective-permute-start | bytes 884744 | tf_op jit(solution)/shard_map/ppermute | solution.py:370
  8.0 11.0 %collective-permute-start = (bf16[144,1024]{1,0:T(8,128)(2,1)S(1)}, bf16[144,1024]{1,0:T(8,128)(2,1)S(1)}, u32[]{:S(2)}, u32[]{:S(2)}) collective-permute-start(bf16[144,1024]{1,0:T(8,128)(2,1)S(1)} %get-tuple-element.66), channel_id=1, source_target_pairs={{0,2},{2,0},{1,3},{3,1},{4,6},{6,4},{5,7},{7,5},{8,10},{10,8},{9,1... | collective-permute-start | bytes 884744 | tf_op jit(solution)/shard_map/ppermute | solution.py:370
  9.5 1.9 %copy-start = (bf16[4,1024,384]{2,1,0:T(8,128)(2,1)S(1)}, bf16[4,1024,384]{2,1,0:T(8,128)(2,1)}, u32[]{:S(2)}) copy-start(bf16[4,1024,384]{2,1,0:T(8,128)(2,1)} %refs_3_.9) | copy-start | bytes 9437188
  11.4 1.9 %copy-start.2 = (bf16[4,1024,384]{2,1,0:T(8,128)(2,1)S(1)}, bf16[4,1024,384]{2,1,0:T(8,128)(2,1)}, u32[]{:S(2)}) copy-start(bf16[4,1024,384]{2,1,0:T(8,128)(2,1)} %refs_4_.15) | copy-start | bytes 9437188
  13.3 1.9 %copy-start.4 = (bf16[4,384,1024]{2,1,0:T(8,128)(2,1)S(1)}, bf16[4,384,1024]{2,1,0:T(8,128)(2,1)}, u32[]{:S(2)}) copy-start(bf16[4,384,1024]{2,1,0:T(8,128)(2,1)} %refs_6_.7) | copy-start | bytes 9437188
  15.2 7.6 %copy-start.1 = (bf16[4,1024,384]{2,1,0:T(8,128)(2,1)S(1)}, bf16[4,1024,384]{2,1,0:T(8,128)(2,1)}, u32[]{:S(2)}) copy-start(bf16[4,1024,384]{2,1,0:T(8,128)(2,1)} %refs_3_.9) | copy-start | bytes 9437188
  15.2 7.6 %copy-start.3 = (bf16[4,1024,384]{2,1,0:T(8,128)(2,1)S(1)}, bf16[4,1024,384]{2,1,0:T(8,128)(2,1)}, u32[]{:S(2)}) copy-start(bf16[4,1024,384]{2,1,0:T(8,128)(2,1)} %refs_4_.15) | copy-start | bytes 9437188
  15.2 7.6 %copy-start.5 = (bf16[4,384,1024]{2,1,0:T(8,128)(2,1)S(1)}, bf16[4,384,1024]{2,1,0:T(8,128)(2,1)}, u32[]{:S(2)}) copy-start(bf16[4,384,1024]{2,1,0:T(8,128)(2,1)} %refs_6_.7) | copy-start | bytes 9437188
  18.4 9.9 %collective-permute-start.5 = (bf16[3,160,384]{2,1,0:T(8,128)(2,1)S(1)}, bf16[3,160,384]{2,1,0:T(8,128)(2,1)S(1)}, u32[]{:S(2)}, u32[]{:S(2)}) collective-permute-start(bf16[3,160,384]{2,1,0:T(8,128)(2,1)S(1)} %get-tuple-element.70.refs_2_), channel_id=1, source_target_pairs={{0,2},{2,0},{1,3},{3,1},{4,6},{6,4},{5,7},{7,5},{8,10},{10,8},{9,1... | collective-permute-start | bytes 1105928 | tf_op jit(solution)/shard_map/ppermute | solution.py:370
  19.1 3.7 %collective-permute-start.3 = (bf16[144,1024]{1,0:T(8,128)(2,1)S(1)}, bf16[144,1024]{1,0:T(8,128)(2,1)S(1)}, u32[]{:S(2)}, u32[]{:S(2)}) collective-permute-start(bf16[144,1024]{1,0:T(8,128)(2,1)S(1)} %collective-permute-done.2.refs_0_), channel_id=1, source_target_pairs={{0,1},{1,0},{2,3},{3,2},{4,5},{5,4},{6,7},{7,6},{8,9},{9,8},{10,11... | collective-permute-start | bytes 884744 | tf_op jit(solution)/shard_map/ppermute | solution.py:370
  19.1 3.7 %collective-permute-start.1 = (bf16[144,1024]{1,0:T(8,128)(2,1)S(1)}, bf16[144,1024]{1,0:T(8,128)(2,1)S(1)}, u32[]{:S(2)}, u32[]{:S(2)}) collective-permute-start(bf16[144,1024]{1,0:T(8,128)(2,1)S(1)} %collective-permute-done.refs_0_), channel_id=1, source_target_pairs={{0,1},{1,0},{2,3},{3,2},{4,5},{5,4},{6,7},{7,6},{8,9},{9,8},{10,11... | collective-permute-start | bytes 884744 | tf_op jit(solution)/shard_map/ppermute | solution.py:370
  19.6 11.7 %collective-permute-start.6 = (bf16[144,1024]{1,0:T(8,128)(2,1)S(1)}, bf16[144,1024]{1,0:T(8,128)(2,1)S(1)}, u32[]{:S(2)}, u32[]{:S(2)}) collective-permute-start(bf16[144,1024]{1,0:T(8,128)(2,1)S(1)} %collective-permute-done.refs_0_), channel_id=1, source_target_pairs={{0,4},{4,8},{8,12},{12,0},{1,5},{5,9},{9,13},{13,1},{2,6},{6,10},{... | collective-permute-start | bytes 884744 | tf_op jit(solution)/shard_map/ppermute | solution.py:370
  21.1 15.5 %collective-permute-start.9 = (bf16[144,1024]{1,0:T(8,128)(2,1)S(1)}, bf16[144,1024]{1,0:T(8,128)(2,1)S(1)}, u32[]{:S(2)}, u32[]{:S(2)}) collective-permute-start(bf16[144,1024]{1,0:T(8,128)(2,1)S(1)} %collective-permute-done.2.refs_0_), channel_id=1, source_target_pairs={{0,4},{4,8},{8,12},{12,0},{1,5},{5,9},{9,13},{13,1},{2,6},{6,10},{... | collective-permute-start | bytes 884744 | tf_op jit(solution)/shard_map/ppermute | solution.py:370
  26.0 14.5 %collective-permute-start.4 = (bf16[3,160,384]{2,1,0:T(8,128)(2,1)S(1)}, bf16[3,160,384]{2,1,0:T(8,128)(2,1)S(1)}, u32[]{:S(2)}, u32[]{:S(2)}) collective-permute-start(bf16[3,160,384]{2,1,0:T(8,128)(2,1)S(1)} %get-tuple-element.71.refs_4_), channel_id=1, source_target_pairs={{0,2},{2,0},{1,3},{3,1},{4,6},{6,4},{5,7},{7,5},{8,10},{10,8},{9,1... | collective-permute-start | bytes 1105928 | tf_op jit(solution)/shard_map/ppermute | solution.py:370
  31.2 5.4 %collective-permute-start.7 = (bf16[144,1024]{1,0:T(8,128)(2,1)S(1)}, bf16[144,1024]{1,0:T(8,128)(2,1)S(1)}, u32[]{:S(2)}, u32[]{:S(2)}) collective-permute-start(bf16[144,1024]{1,0:T(8,128)(2,1)S(1)} %collective-permute-done.6.refs_1_), channel_id=1, source_target_pairs={{0,1},{1,0},{2,3},{3,2},{4,5},{5,4},{6,7},{7,6},{8,9},{9,8},{10,11... | collective-permute-start | bytes 884744 | tf_op jit(solution)/shard_map/ppermute | solution.py:370
  36.7 9.9 %collective-permute-start.10 = (bf16[144,1024]{1,0:T(8,128)(2,1)S(1)}, bf16[144,1024]{1,0:T(8,128)(2,1)S(1)}, u32[]{:S(2)}, u32[]{:S(2)}) collective-permute-start(bf16[144,1024]{1,0:T(8,128)(2,1)S(1)} %collective-permute-done.6.refs_1_), channel_id=1, source_target_pairs={{0,4},{4,8},{8,12},{12,0},{1,5},{5,9},{9,13},{13,1},{2,6},{6,10},{... | collective-permute-start | bytes 884744 | tf_op jit(solution)/shard_map/ppermute | solution.py:370
  40.5 16.1 %collective-permute-start.8 = (bf16[3,288,384]{2,1,0:T(8,128)(2,1)S(1)}, bf16[3,288,384]{2,1,0:T(8,128)(2,1)S(1)}, u32[]{:S(2)}, u32[]{:S(2)}) collective-permute-start(bf16[3,288,384]{2,1,0:T(8,128)(2,1)S(1)} %get-tuple-element.76.refs_1_), channel_id=1, source_target_pairs={{0,2},{2,0},{1,3},{3,1},{4,6},{6,4},{5,7},{7,5},{8,10},{10,8},{9,1... | collective-permute-start | bytes 1990664 | tf_op jit(solution)/shard_map/ppermute | solution.py:370
  46.6 1.6 %collective-permute-start.11 = (bf16[144,1024]{1,0:T(8,128)(2,1)S(1)}, bf16[144,1024]{1,0:T(8,128)(2,1)S(1)}, u32[]{:S(2)}, u32[]{:S(2)}) collective-permute-start(bf16[144,1024]{1,0:T(8,128)(2,1)S(1)} %collective-permute-done.9.refs_0_), channel_id=1, source_target_pairs={{0,1},{1,0},{2,3},{3,2},{4,5},{5,4},{6,7},{7,6},{8,9},{9,8},{10,11... | collective-permute-start | bytes 884744 | tf_op jit(solution)/shard_map/ppermute | solution.py:370
  48.2 1.6 %collective-permute-start.12 = (bf16[144,1024]{1,0:T(8,128)(2,1)S(1)}, bf16[144,1024]{1,0:T(8,128)(2,1)S(1)}, u32[]{:S(2)}, u32[]{:S(2)}) collective-permute-start(bf16[144,1024]{1,0:T(8,128)(2,1)S(1)} %collective-permute-done.10.refs_1_), channel_id=1, source_target_pairs={{0,1},{1,0},{2,3},{3,2},{4,5},{5,4},{6,7},{7,6},{8,9},{9,8},{10,11... | collective-permute-start | bytes 884744 | tf_op jit(solution)/shard_map/ppermute | solution.py:370
  48.3 13.5 %collective-permute-start.14 = (bf16[144,1024]{1,0:T(8,128)(2,1)S(1)}, bf16[144,1024]{1,0:T(8,128)(2,1)S(1)}, u32[]{:S(2)}, u32[]{:S(2)}) collective-permute-start(bf16[144,1024]{1,0:T(8,128)(2,1)S(1)} %collective-permute-done.9.refs_0_), channel_id=1, source_target_pairs={{0,4},{4,8},{8,12},{12,0},{1,5},{5,9},{9,13},{13,1},{2,6},{6,10},{... | collective-permute-start | bytes 884744 | tf_op jit(solution)/shard_map/ppermute | solution.py:370
  48.9 16.8 %collective-permute-start.15 = (bf16[144,1024]{1,0:T(8,128)(2,1)S(1)}, bf16[144,1024]{1,0:T(8,128)(2,1)S(1)}, u32[]{:S(2)}, u32[]{:S(2)}) collective-permute-start(bf16[144,1024]{1,0:T(8,128)(2,1)S(1)} %collective-permute-done.10.refs_1_), channel_id=1, source_target_pairs={{0,4},{4,8},{8,12},{12,0},{1,5},{5,9},{9,13},{13,1},{2,6},{6,10},{... | collective-permute-start | bytes 884744 | tf_op jit(solution)/shard_map/ppermute | solution.py:370
  56.6 16.1 %collective-permute-start.13 = (bf16[3,288,384]{2,1,0:T(8,128)(2,1)S(1)}, bf16[3,288,384]{2,1,0:T(8,128)(2,1)S(1)}, u32[]{:S(2)}, u32[]{:S(2)}) collective-permute-start(bf16[3,288,384]{2,1,0:T(8,128)(2,1)S(1)} %get-tuple-element.83.refs_1_), channel_id=1, source_target_pairs={{0,2},{2,0},{1,3},{3,1},{4,6},{6,4},{5,7},{7,5},{8,10},{10,8},{9,1... | collective-permute-start | bytes 1990664 | tf_op jit(solution)/shard_map/ppermute | solution.py:370
  65.7 1.6 %collective-permute-start.16 = (bf16[144,1024]{1,0:T(8,128)(2,1)S(1)}, bf16[144,1024]{1,0:T(8,128)(2,1)S(1)}, u32[]{:S(2)}, u32[]{:S(2)}) collective-permute-start(bf16[144,1024]{1,0:T(8,128)(2,1)S(1)} %collective-permute-done.14.refs_0_), channel_id=1, source_target_pairs={{0,1},{1,0},{2,3},{3,2},{4,5},{5,4},{6,7},{7,6},{8,9},{9,8},{10,11... | collective-permute-start | bytes 884744 | tf_op jit(solution)/shard_map/ppermute | solution.py:370
  67.3 1.6 %collective-permute-start.17 = (bf16[144,1024]{1,0:T(8,128)(2,1)S(1)}, bf16[144,1024]{1,0:T(8,128)(2,1)S(1)}, u32[]{:S(2)}, u32[]{:S(2)}) collective-permute-start(bf16[144,1024]{1,0:T(8,128)(2,1)S(1)} %collective-permute-done.15.refs_1_), channel_id=1, source_target_pairs={{0,1},{1,0},{2,3},{3,2},{4,5},{5,4},{6,7},{7,6},{8,9},{9,8},{10,11... | collective-permute-start | bytes 884744 | tf_op jit(solution)/shard_map/ppermute | solution.py:370
  72.7 17.4 %collective-permute-start.18 = (bf16[3,288,384]{2,1,0:T(8,128)(2,1)S(1)}, bf16[3,288,384]{2,1,0:T(8,128)(2,1)S(1)}, u32[]{:S(2)}, u32[]{:S(2)}) collective-permute-start(bf16[3,288,384]{2,1,0:T(8,128)(2,1)S(1)} %get-tuple-element.89.refs_1_), channel_id=1, source_target_pairs={{0,2},{2,0},{1,3},{3,1},{4,6},{6,4},{5,7},{7,5},{8,10},{10,8},{9,1... | collective-permute-start | bytes 1990664 | tf_op jit(solution)/shard_map/ppermute | solution.py:370
  78.1 1.6 %collective-permute-start.19 = (bf16[256,512]{1,0:T(8,128)(2,1)S(1)}, bf16[256,512]{1,0:T(8,128)(2,1)S(1)}, u32[]{:S(2)}, u32[]{:S(2)}) collective-permute-start(bf16[256,512]{1,0:T(8,128)(2,1)S(1)} %get-tuple-element.91), channel_id=1, source_target_pairs={{0,1},{1,0},{2,3},{3,2},{4,5},{5,4},{6,7},{7,6},{8,9},{9,8},{10,11... | collective-permute-start | bytes 786440 | tf_op jit(solution)/shard_map/ppermute | solution.py:370
  78.1 5.8 %collective-permute-start.24 = (bf16[256,512]{1,0:T(8,128)(2,1)S(1)}, bf16[256,512]{1,0:T(8,128)(2,1)S(1)}, u32[]{:S(2)}, u32[]{:S(2)}) collective-permute-start(bf16[256,512]{1,0:T(8,128)(2,1)S(1)} %get-tuple-element.111), channel_id=1, source_target_pairs={{0,1},{1,0},{2,3},{3,2},{4,5},{5,4},{6,7},{7,6},{8,9},{9,8},{10,11... | collective-permute-start | bytes 786440 | tf_op jit(solution)/shard_map/ppermute | solution.py:370
  80.3 13.5 %collective-permute-start.20 = (bf16[128,512]{1,0:T(8,128)(2,1)S(1)}, bf16[128,512]{1,0:T(8,128)(2,1)S(1)}, u32[]{:S(2)}, u32[]{:S(2)}) collective-permute-start(bf16[128,512]{1,0:T(8,128)(2,1)S(1)} %get-tuple-element.92), channel_id=1, source_target_pairs={{0,8},{1,10},{2,9},{3,11},{4,12},{5,14},{6,13},{7,15},{8,0},{9,2},... | collective-permute-start | bytes 393224 | tf_op jit(solution)/shard_map/ppermute | solution.py:457
  80.8 14.3 %collective-permute-start.21 = (bf16[128,512]{1,0:T(8,128)(2,1)S(1)}, bf16[128,512]{1,0:T(8,128)(2,1)S(1)}, u32[]{:S(2)}, u32[]{:S(2)}) collective-permute-start(bf16[128,512]{1,0:T(8,128)(2,1)S(1)} %get-tuple-element.93), channel_id=1, source_target_pairs={{0,10},{1,8},{2,11},{3,9},{4,14},{5,12},{6,15},{7,13},{8,2},{9,0},... | collective-permute-start | bytes 393224 | tf_op jit(solution)/shard_map/ppermute | solution.py:457
  84.0 11.2 %collective-permute-start.23 = (bf16[256,512]{1,0:T(8,128)(2,1)S(1)}, bf16[256,512]{1,0:T(8,128)(2,1)S(1)}, u32[]{:S(2)}, u32[]{:S(2)}) collective-permute-start(bf16[256,512]{1,0:T(8,128)(2,1)S(1)} %get-tuple-element.109), channel_id=1, source_target_pairs={{0,1},{1,0},{2,3},{3,2},{4,5},{5,4},{6,7},{7,6},{8,9},{9,8},{10,11... | collective-permute-start | bytes 786440 | tf_op jit(solution)/shard_map/ppermute | solution.py:370
  84.6 14.5 %collective-permute-start.25 = (bf16[256,512]{1,0:T(8,128)(2,1)S(1)}, bf16[256,512]{1,0:T(8,128)(2,1)S(1)}, u32[]{:S(2)}, u32[]{:S(2)}) collective-permute-start(bf16[256,512]{1,0:T(8,128)(2,1)S(1)} %shard_map.100), channel_id=1, source_target_pairs={{0,12},{4,0},{8,4},{12,8},{1,13},{5,1},{9,5},{13,9},{2,14},{6,2},{... | collective-permute-start | bytes 786440 | tf_op jit(solution)/shard_map/ppermute | solution.py:370
  95.1 4.7 %collective-permute-start.22 = (bf16[256,512]{1,0:T(8,128)(2,1)S(1)}, bf16[256,512]{1,0:T(8,128)(2,1)S(1)}, u32[]{:S(2)}, u32[]{:S(2)}) collective-permute-start(bf16[256,512]{1,0:T(8,128)(2,1)S(1)} %get-tuple-element.98), channel_id=1, source_target_pairs={{0,1},{1,0},{2,3},{3,2},{4,5},{5,4},{6,7},{7,6},{8,9},{9,8},{10,11... | collective-permute-start | bytes 786440 | tf_op jit(solution)/shard_map/ppermute | solution.py:370
  99.7 5.2 %collective-permute-start.26 = (bf16[128,512]{1,0:T(8,128)(2,1)S(1)}, bf16[128,512]{1,0:T(8,128)(2,1)S(1)}, u32[]{:S(2)}, u32[]{:S(2)}) collective-permute-start(bf16[128,512]{1,0:T(8,128)(2,1)S(1)} %get-tuple-element.114), channel_id=1, source_target_pairs={{0,2},{2,0},{1,3},{3,1},{4,6},{6,4},{5,7},{7,5},{8,10},{10,8},{9,1... | collective-permute-start | bytes 393224 | tf_op jit(solution)/shard_map/ppermute | solution.py:370
  100.5 9.7 %collective-permute-start.28 = (bf16[128,512]{1,0:T(8,128)(2,1)S(1)}, bf16[128,512]{1,0:T(8,128)(2,1)S(1)}, u32[]{:S(2)}, u32[]{:S(2)}) collective-permute-start(bf16[128,512]{1,0:T(8,128)(2,1)S(1)} %get-tuple-element.120), channel_id=1, source_target_pairs={{0,4},{1,6},{2,5},{3,7},{4,8},{5,10},{6,9},{7,11},{8,12},{9,14},{1... | collective-permute-start | bytes 393224 | tf_op jit(solution)/shard_map/ppermute | solution.py:457
  103.0 9.2 %collective-permute-start.29 = (bf16[128,512]{1,0:T(8,128)(2,1)S(1)}, bf16[128,512]{1,0:T(8,128)(2,1)S(1)}, u32[]{:S(2)}, u32[]{:S(2)}) collective-permute-start(bf16[128,512]{1,0:T(8,128)(2,1)S(1)} %get-tuple-element.122), channel_id=1, source_target_pairs={{0,6},{1,4},{2,7},{3,5},{4,10},{5,8},{6,11},{7,9},{8,14},{9,12},{1... | collective-permute-start | bytes 393224 | tf_op jit(solution)/shard_map/ppermute | solution.py:457
  105.5 6.8 %collective-permute-start.27 = (bf16[128,512]{1,0:T(8,128)(2,1)S(1)}, bf16[128,512]{1,0:T(8,128)(2,1)S(1)}, u32[]{:S(2)}, u32[]{:S(2)}) collective-permute-start(bf16[128,512]{1,0:T(8,128)(2,1)S(1)} %get-tuple-element.116), channel_id=1, source_target_pairs={{0,1},{1,0},{2,3},{3,2},{4,5},{5,4},{6,7},{7,6},{8,9},{9,8},{10,11... | collective-permute-start | bytes 393224 | tf_op jit(solution)/shard_map/ppermute | solution.py:370

commit v5 on v4

--- a/solution.py
+++ b/solution.py
@@ -28,16 +28,13 @@
     return pl.BlockSpec((1,) + shape, lambda j: (j,) + (0,) * len(shape))
 
 
-def pack_kernel(place, tokens, cotangent, route_ids, route_weights, *refs):
-    *outs, ids, weights, sems = refs
-    chosen, rows = ids.shape
+def pack_kernel(place, tokens, cotangent, routes, *refs):
+    *outs, sems = refs
+    chosen, rows = routes.shape[0] // 2, routes.shape[1]
     quarter = outs[0].shape[1] // 2
     wide = len(outs) - 1
     dp, sub = place[2], place[0]
-    copies = [
-        pltpu.make_async_copy(route_ids, ids, sems.at[0]),
-        pltpu.make_async_copy(route_weights, weights, sems.at[1]),
-    ]
+    copies = []
     wanted = [((dp + by) % wide, sub) for by in range(1, wide)] + [(dp, sub), (dp, 1 - sub)]
     for out, (half, which) in zip(outs, wanted):
         columns = pl.ds(pl.multiple_of((half * 2 + which) * quarter, LANES), quarter)
@@ -48,9 +45,7 @@
             )
     for copy in copies:
         copy.start()
-    copies[0].wait()
-    copies[1].wait()
-    parts, rest = [ids[...].astype(F32)], weights[...]
+    parts, rest = [routes[:chosen]], routes[chosen:]
     for _ in range(3):
         part = rest.astype(BF).astype(F32)
         parts.append(part)
@@ -65,26 +60,23 @@
     lines = jnp.concatenate(lines, axis=0).astype(BF)
     for out in outs:
         out[rows:, :] = lines
-    for copy in copies[2:]:
+    for copy in copies:
         copy.wait()
 
 
 def pack(place, tokens, cotangent, route_ids, route_weights, wide, quarter):
-    rows, chosen = route_ids.shape
+    rows = route_ids.shape[0]
     shape = (rows + ROUTE_ROWS, 2 * quarter)
+    routes = jnp.concatenate([route_ids.T.astype(F32), route_weights.T], axis=0)
     return pl.pallas_call(
         pack_kernel,
-        in_specs=[SMEM] + [pl.BlockSpec(memory_space=pltpu.HBM)] * 4,
+        in_specs=[SMEM] + [pl.BlockSpec(memory_space=pltpu.HBM)] * 2 + [WHOLE],
         out_specs=[WHOLE] * (wide + 1),
         out_shape=[jax.ShapeDtypeStruct(shape, BF)] * (wide + 1),
-        scratch_shapes=[
-            pltpu.VMEM((chosen, rows), jnp.int32),
-            pltpu.VMEM((chosen, rows), F32),
-            pltpu.SemaphoreType.DMA((2 * wide + 4,)),
-        ],
+        scratch_shapes=[pltpu.SemaphoreType.DMA((2 * wide + 2,))],
         compiler_params=pltpu.CompilerParams(vmem_limit_bytes=LIMIT),
         cost_estimate=PACK_COST,
-    )(place, tokens, cotangent, route_ids.T, route_weights.T)
+    )(place, tokens, cotangent, routes)
 
 
 def route_tables(payloads, token_rows, chosen, first_expert, dp, local_experts, tables):

time: 114 us -> 114 us (level)
  other arithmetic: 0.08 us -> 1.45 us
  local copies, waits for them, and re-layouts: 9.12 us -> 7.76 us
    unnamed x20 -> x16, local copies, waits for them, and re-layouts: 9.12 us -> 7.76 us
where the time goes in v5:
time: 114 us
  Pallas kernels  42.3 us (37%)
  waiting for transfers between devices  34.4 us (30%)
  starting transfers between devices  26.7 us (23%)
  local copies, waits for them, and re-layouts  7.76 us (7%)
  other arithmetic  1.45 us (1%)
    ppermute x26, waiting for transfers between devices, shift(): lax.ppermute(array, axis, [(i, (i + by) % size) for i in range(size)])  30.1 us
    ppermute x26, starting transfers between devices, shift(): lax.ppermute(array, axis, [(i, (i + by) % size) for i in range(size)])  19.4 us
    pallas_call x5, Pallas kernels, forward(): pl.pallas_call(functools.partial(forward_kernel, shards, token_rows, chos...  18 us
    pallas_call x4, Pallas kernels, backward(): pl.pallas_call(functools.partial(backward_kernel, capacity, parts, wide),...  14.9 us
    unnamed x16, local copies, waits for them, and re-layouts  7.76 us
    ppermute x4, starting transfers between devices, sent_straight(): far.append(lax.ppermute(piece, ('expert', 'dp', 'sub'), pairs))  7.38 us
    pallas_call x7, Pallas kernels, small(): pl.pallas_call(kernel, in_specs=[SMEM] + [WHOLE] * (len(arrays) - 1), out...  5.07 us
    ppermute x4, waiting for transfers between devices, sent_straight(): far.append(lax.ppermute(piece, ('expert', 'dp', 'sub'), pairs))  4.34 us
  transfers between devices with their start and end apart: 30, of which 17 were waited for; matrix products, arithmetic and copies ran while one was open for 0% of the time, Pallas kernels for 35%

profile of v5, /device:TPU:0, one launch (start us, length us, event | category | flops | bytes accessed | tf_op | source)
XLA Modules:
  0.0 113.6 jit_solution(13509743093388885955)
XLA Ops:
  0.6 0.7 convert_bitcast_fusion
  1.3 0.7 pad_maximum_fusion.routes
  2.1 1.0 copy-done.6
  3.1 1.0 copy-done.7
  4.2 0.8 shard_map.86
  4.9 3.1 %collective-permute-start.2 = (bf16[144,1024]{1,0:T(8,128)(2,1)S(1)}, bf16[144,1024]{1,0:T(8,128)(2,1)S(1)}, u32[]{:S(2)}, u32[]{:S(2)}) collective-permute-start(bf16[144,1024]{1,0:T(8,128)(2,1)S(1)} %get-tuple-element.63.refs_0_), channel_id=1, source_target_pairs={{0,4},{4,8},{8,12},{12,0},{1,5},{5,9},{9,13},{13,1},{2,6},{6,10},{... | collective-permute-start | bytes 884744 | tf_op jit(solution)/shard_map/ppermute | solution.py:362
  8.0 1.5 %collective-permute-start = (bf16[144,1024]{1,0:T(8,128)(2,1)S(1)}, bf16[144,1024]{1,0:T(8,128)(2,1)S(1)}, u32[]{:S(2)}, u32[]{:S(2)}) collective-permute-start(bf16[144,1024]{1,0:T(8,128)(2,1)S(1)} %get-tuple-element.66), channel_id=1, source_target_pairs={{0,2},{2,0},{1,3},{3,1},{4,6},{6,4},{5,7},{7,5},{8,10},{10,8},{9,1... | collective-permute-start | bytes 884744 | tf_op jit(solution)/shard_map/ppermute | solution.py:362
  9.5 1.9 %copy-done = bf16[4,1024,384]{2,1,0:T(8,128)(2,1)S(1)} copy-done((bf16[4,1024,384]{2,1,0:T(8,128)(2,1)S(1)}, bf16[4,1024,384]{2,1,0:T(8,128)(2,1)}, u32[]{:S(2)}) %copy-start) | copy-done | bytes 3145752
  11.4 1.9 %copy-done.2 = bf16[4,1024,384]{2,1,0:T(8,128)(2,1)S(1)} copy-done((bf16[4,1024,384]{2,1,0:T(8,128)(2,1)S(1)}, bf16[4,1024,384]{2,1,0:T(8,128)(2,1)}, u32[]{:S(2)}) %copy-start.2) | copy-done | bytes 3145752
  13.3 1.9 %copy-done.4 = bf16[4,384,1024]{2,1,0:T(8,128)(2,1)S(1)} copy-done((bf16[4,384,1024]{2,1,0:T(8,128)(2,1)S(1)}, bf16[4,384,1024]{2,1,0:T(8,128)(2,1)}, u32[]{:S(2)}) %copy-start.4) | copy-done | bytes 3145752
  15.2 3.3 %shard_map.87 = (bf16[3,160,384]{2,1,0:T(8,128)(2,1)S(1)}, bf16[4,48,1024]{2,1,0:T(8,128)(2,1)S(1)}, f32[16,128]{1,0:T(8,128)S(1)}) custom-call(s32[3]{0:T(128)S(1)} %pad_add_fusion.place.refs_5_, bf16[144,1024]{1,0:T(8,128)(2,1)S(1)} %get-tuple-element.63.refs_0_, bf16[144,1024]{1,0:T(8,128)(2,1)S(1)} %get-tuple-element.64.refs_1_, ...), custom_call_target="tpu_custom_call" | custom-call | flops 1 | bytes 1 | tf_op jit(solution)/shard_map/pallas_call | solution.py:231
  19.6 1.6 %collective-permute-start.6 = (bf16[144,1024]{1,0:T(8,128)(2,1)S(1)}, bf16[144,1024]{1,0:T(8,128)(2,1)S(1)}, u32[]{:S(2)}, u32[]{:S(2)}) collective-permute-start(bf16[144,1024]{1,0:T(8,128)(2,1)S(1)} %collective-permute-done.refs_0_), channel_id=1, source_target_pairs={{0,4},{4,8},{8,12},{12,0},{1,5},{5,9},{9,13},{13,1},{2,6},{6,10},{... | collective-permute-start | bytes 884744 | tf_op jit(solution)/shard_map/ppermute | solution.py:362
  21.1 1.6 %collective-permute-start.9 = (bf16[144,1024]{1,0:T(8,128)(2,1)S(1)}, bf16[144,1024]{1,0:T(8,128)(2,1)S(1)}, u32[]{:S(2)}, u32[]{:S(2)}) collective-permute-start(bf16[144,1024]{1,0:T(8,128)(2,1)S(1)} %collective-permute-done.2.refs_0_), channel_id=1, source_target_pairs={{0,4},{4,8},{8,12},{12,0},{1,5},{5,9},{9,13},{13,1},{2,6},{6,10},{... | collective-permute-start | bytes 884744 | tf_op jit(solution)/shard_map/ppermute | solution.py:362
  22.7 3.3 %shard_map.88 = (bf16[3,160,384]{2,1,0:T(8,128)(2,1)S(1)}, bf16[4,48,1024]{2,1,0:T(8,128)(2,1)S(1)}, f32[16,128]{1,0:T(8,128)S(1)}) custom-call(s32[3]{0:T(128)S(1)} %pad_add_fusion.place.refs_5_, bf16[144,1024]{1,0:T(8,128)(2,1)S(1)} %collective-permute-done.refs_0_, bf16[144,1024]{1,0:T(8,128)(2,1)S(1)} %collective-permute-done.1.refs_1_, ...), custom_call_target="tpu_custom_call" | custom-call | flops 1 | bytes 1 | tf_op jit(solution)/shard_map/pallas_call | solution.py:231
  26.0 1.6 %collective-permute-start.4 = (bf16[3,160,384]{2,1,0:T(8,128)(2,1)S(1)}, bf16[3,160,384]{2,1,0:T(8,128)(2,1)S(1)}, u32[]{:S(2)}, u32[]{:S(2)}) collective-permute-start(bf16[3,160,384]{2,1,0:T(8,128)(2,1)S(1)} %get-tuple-element.71.refs_4_), channel_id=1, source_target_pairs={{0,2},{2,0},{1,3},{3,1},{4,6},{6,4},{5,7},{7,5},{8,10},{10,8},{9,1... | collective-permute-start | bytes 1105928 | tf_op jit(solution)/shard_map/ppermute | solution.py:362
  27.6 0.7 collective-permute-done.5.refs_5_
  28.3 2.9 %collective-permute-done.6.refs_1_ = bf16[144,1024]{1,0:T(8,128)(2,1)S(1)} collective-permute-done((bf16[144,1024]{1,0:T(8,128)(2,1)S(1)}, bf16[144,1024]{1,0:T(8,128)(2,1)S(1)}, u32[]{:S(2)}, u32[]{:S(2)}) %collective-permute-start.6) | collective-permute-done | bytes 294944 | tf_op jit(solution)/shard_map/ppermute | solution.py:362
  31.2 5.4 %collective-permute-done.9.refs_0_ = bf16[144,1024]{1,0:T(8,128)(2,1)S(1)} collective-permute-done((bf16[144,1024]{1,0:T(8,128)(2,1)S(1)}, bf16[144,1024]{1,0:T(8,128)(2,1)S(1)}, u32[]{:S(2)}, u32[]{:S(2)}) %collective-permute-start.9) | collective-permute-done | bytes 294944 | tf_op jit(solution)/shard_map/ppermute | solution.py:362
  36.7 3.8 %shard_map.89 = (bf16[3,288,384]{2,1,0:T(8,128)(2,1)S(1)}, bf16[4,80,1024]{2,1,0:T(8,128)(2,1)S(1)}, f32[16,256]{1,0:T(8,128)S(1)}) custom-call(s32[3]{0:T(128)S(1)} %pad_add_fusion.place.refs_5_, bf16[144,1024]{1,0:T(8,128)(2,1)S(1)} %collective-permute-done.2.refs_0_, bf16[144,1024]{1,0:T(8,128)(2,1)S(1)} %collective-permute-done.6.refs_1_, ...), custom_call_target="tpu_custom_call" | custom-call | flops 1 | bytes 1 | tf_op jit(solution)/shard_map/pallas_call | solution.py:231
  40.5 1.6 %collective-permute-start.8 = (bf16[3,288,384]{2,1,0:T(8,128)(2,1)S(1)}, bf16[3,288,384]{2,1,0:T(8,128)(2,1)S(1)}, u32[]{:S(2)}, u32[]{:S(2)}) collective-permute-start(bf16[3,288,384]{2,1,0:T(8,128)(2,1)S(1)} %get-tuple-element.76.refs_1_), channel_id=1, source_target_pairs={{0,2},{2,0},{1,3},{3,1},{4,6},{6,4},{5,7},{7,5},{8,10},{10,8},{9,1... | collective-permute-start | bytes 1990664 | tf_op jit(solution)/shard_map/ppermute | solution.py:362
  42.1 3.7 %shard_map.90 = (bf16[4,96,384]{2,1,0:T(8,128)(2,1)S(1)}, bf16[256,512]{1,0:T(8,128)(2,1)S(1)}, bf16[256,512]{1,0:T(8,128)(2,1)S(1)}) custom-call(s32[3]{0:T(128)S(1)} %pad_add_fusion.place.refs_5_, f32[16,128]{1,0:T(8,128)S(1)} %get-tuple-element.68.refs_5_.refs_0_, f32[16,128]{1,0:T(8,128)S(1)} %get-tuple-element.69.refs_7_.refs_1_, ...), custom_call_target="tpu_custom_call" | custom-call | flops 1 | bytes 1 | tf_op jit(solution)/shard_map/pallas_call | solution.py:255
  45.7 0.9 collective-permute-done.10.refs_1_
  46.6 1.6 %collective-permute-done.11.refs_2_ = bf16[144,1024]{1,0:T(8,128)(2,1)S(1)} collective-permute-done((bf16[144,1024]{1,0:T(8,128)(2,1)S(1)}, bf16[144,1024]{1,0:T(8,128)(2,1)S(1)}, u32[]{:S(2)}, u32[]{:S(2)}) %collective-permute-start.11) | collective-permute-done | bytes 294944 | tf_op jit(solution)/shard_map/ppermute | solution.py:362
  49.8 3.8 %shard_map.91 = (bf16[3,288,384]{2,1,0:T(8,128)(2,1)S(1)}, bf16[4,80,1024]{2,1,0:T(8,128)(2,1)S(1)}, f32[16,256]{1,0:T(8,128)S(1)}) custom-call(s32[3]{0:T(128)S(1)} %pad_add_fusion.place.refs_5_, bf16[144,1024]{1,0:T(8,128)(2,1)S(1)} %collective-permute-done.9.refs_0_, bf16[144,1024]{1,0:T(8,128)(2,1)S(1)} %collective-permute-done.10.refs_1_, ...), custom_call_target="tpu_custom_call" | custom-call | flops 1 | bytes 1 | tf_op jit(solution)/shard_map/pallas_call | solution.py:231
  53.6 3.0 %collective-permute-done.8.refs_2_ = bf16[3,288,384]{2,1,0:T(8,128)(2,1)S(1)} collective-permute-done((bf16[3,288,384]{2,1,0:T(8,128)(2,1)S(1)}, bf16[3,288,384]{2,1,0:T(8,128)(2,1)S(1)}, u32[]{:S(2)}, u32[]{:S(2)}) %collective-permute-start.8) | collective-permute-done | bytes 663584 | tf_op jit(solution)/shard_map/ppermute | solution.py:362
  56.6 1.5 %collective-permute-start.13 = (bf16[3,288,384]{2,1,0:T(8,128)(2,1)S(1)}, bf16[3,288,384]{2,1,0:T(8,128)(2,1)S(1)}, u32[]{:S(2)}, u32[]{:S(2)}) collective-permute-start(bf16[3,288,384]{2,1,0:T(8,128)(2,1)S(1)} %get-tuple-element.83.refs_1_), channel_id=1, source_target_pairs={{0,2},{2,0},{1,3},{3,1},{4,6},{6,4},{5,7},{7,5},{8,10},{10,8},{9,1... | collective-permute-start | bytes 1990664 | tf_op jit(solution)/shard_map/ppermute | solution.py:362
  58.1 3.8 %shard_map.92 = (bf16[4,80,384]{2,1,0:T(8,128)(2,1)S(1)}, bf16[256,512]{1,0:T(8,128)(2,1)S(1)}, bf16[256,512]{1,0:T(8,128)(2,1)S(1)}) custom-call(s32[3]{0:T(128)S(1)} %pad_add_fusion.place.refs_5_, f32[16,256]{1,0:T(8,128)S(1)} %get-tuple-element.73.refs_8_.refs_0_, bf16[3,288,384]{2,1,0:T(8,128)(2,1)S(1)} %get-tuple-element.76.refs_1_, ...), custom_call_target="tpu_custom_call" | custom-call | flops 1 | bytes 1 | tf_op jit(solution)/shard_map/pallas_call | solution.py:255
  61.9 3.9 %collective-permute-done.15.refs_1_ = bf16[144,1024]{1,0:T(8,128)(2,1)S(1)} collective-permute-done((bf16[144,1024]{1,0:T(8,128)(2,1)S(1)}, bf16[144,1024]{1,0:T(8,128)(2,1)S(1)}, u32[]{:S(2)}, u32[]{:S(2)}) %collective-permute-start.15) | collective-permute-done | bytes 294944 | tf_op jit(solution)/shard_map/ppermute | solution.py:362
  65.7 1.6 %collective-permute-done.16.refs_2_ = bf16[144,1024]{1,0:T(8,128)(2,1)S(1)} collective-permute-done((bf16[144,1024]{1,0:T(8,128)(2,1)S(1)}, bf16[144,1024]{1,0:T(8,128)(2,1)S(1)}, u32[]{:S(2)}, u32[]{:S(2)}) %collective-permute-start.16) | collective-permute-done | bytes 294944 | tf_op jit(solution)/shard_map/ppermute | solution.py:362
  67.4 1.4 %collective-permute-done.17.refs_3_ = bf16[144,1024]{1,0:T(8,128)(2,1)S(1)} collective-permute-done((bf16[144,1024]{1,0:T(8,128)(2,1)S(1)}, bf16[144,1024]{1,0:T(8,128)(2,1)S(1)}, u32[]{:S(2)}, u32[]{:S(2)}) %collective-permute-start.17) | collective-permute-done | bytes 294944 | tf_op jit(solution)/shard_map/ppermute | solution.py:362
  68.9 3.8 %shard_map.93 = (bf16[3,288,384]{2,1,0:T(8,128)(2,1)S(1)}, bf16[4,80,1024]{2,1,0:T(8,128)(2,1)S(1)}, f32[16,256]{1,0:T(8,128)S(1)}) custom-call(s32[3]{0:T(128)S(1)} %pad_add_fusion.place.refs_5_, bf16[144,1024]{1,0:T(8,128)(2,1)S(1)} %collective-permute-done.14.refs_0_, bf16[144,1024]{1,0:T(8,128)(2,1)S(1)} %collective-permute-done.15.refs_1_, ...), custom_call_target="tpu_custom_call" | custom-call | flops 1 | bytes 1 | tf_op jit(solution)/shard_map/pallas_call | solution.py:231
  72.7 1.6 %collective-permute-start.18 = (bf16[3,288,384]{2,1,0:T(8,128)(2,1)S(1)}, bf16[3,288,384]{2,1,0:T(8,128)(2,1)S(1)}, u32[]{:S(2)}, u32[]{:S(2)}) collective-permute-start(bf16[3,288,384]{2,1,0:T(8,128)(2,1)S(1)} %get-tuple-element.89.refs_1_), channel_id=1, source_target_pairs={{0,2},{2,0},{1,3},{3,1},{4,6},{6,4},{5,7},{7,5},{8,10},{10,8},{9,1... | collective-permute-start | bytes 1990664 | tf_op jit(solution)/shard_map/ppermute | solution.py:362
  74.3 3.8 %shard_map.94 = (bf16[4,80,384]{2,1,0:T(8,128)(2,1)S(1)}, bf16[256,512]{1,0:T(8,128)(2,1)S(1)}, bf16[256,512]{1,0:T(8,128)(2,1)S(1)}) custom-call(s32[3]{0:T(128)S(1)} %pad_add_fusion.place.refs_5_, f32[16,256]{1,0:T(8,128)S(1)} %get-tuple-element.80.refs_5_.refs_0_, bf16[3,288,384]{2,1,0:T(8,128)(2,1)S(1)} %get-tuple-element.83.refs_1_, ...), custom_call_target="tpu_custom_call" | custom-call | flops 1 | bytes 1 | tf_op jit(solution)/shard_map/pallas_call | solution.py:255
  78.6 1.0 collective-permute-done.19.refs_1_
  79.7 0.7 shard_map.95
  80.8 3.1 %collective-permute-start.21 = (bf16[128,512]{1,0:T(8,128)(2,1)S(1)}, bf16[128,512]{1,0:T(8,128)(2,1)S(1)}, u32[]{:S(2)}, u32[]{:S(2)}) collective-permute-start(bf16[128,512]{1,0:T(8,128)(2,1)S(1)} %get-tuple-element.93), channel_id=1, source_target_pairs={{0,10},{1,8},{2,11},{3,9},{4,14},{5,12},{6,15},{7,13},{8,2},{9,0},... | collective-permute-start | bytes 393224 | tf_op jit(solution)/shard_map/ppermute | solution.py:449
  84.6 2.5 %collective-permute-start.25 = (bf16[256,512]{1,0:T(8,128)(2,1)S(1)}, bf16[256,512]{1,0:T(8,128)(2,1)S(1)}, u32[]{:S(2)}, u32[]{:S(2)}) collective-permute-start(bf16[256,512]{1,0:T(8,128)(2,1)S(1)} %shard_map.100), channel_id=1, source_target_pairs={{0,12},{4,0},{8,4},{12,8},{1,13},{5,1},{9,5},{13,9},{2,14},{6,2},{... | collective-permute-start | bytes 786440 | tf_op jit(solution)/shard_map/ppermute | solution.py:362
  87.0 3.1 %collective-permute-done.18.refs_2_ = bf16[3,288,384]{2,1,0:T(8,128)(2,1)S(1)} collective-permute-done((bf16[3,288,384]{2,1,0:T(8,128)(2,1)S(1)}, bf16[3,288,384]{2,1,0:T(8,128)(2,1)S(1)}, u32[]{:S(2)}, u32[]{:S(2)}) %collective-permute-start.18) | collective-permute-done | bytes 663584 | tf_op jit(solution)/shard_map/ppermute | solution.py:362
  90.1 3.8 %shard_map.96 = (bf16[4,80,384]{2,1,0:T(8,128)(2,1)S(1)}, bf16[256,512]{1,0:T(8,128)(2,1)S(1)}, bf16[256,512]{1,0:T(8,128)(2,1)S(1)}) custom-call(s32[3]{0:T(128)S(1)} %pad_add_fusion.place.refs_5_, f32[16,256]{1,0:T(8,128)S(1)} %get-tuple-element.86.refs_5_.refs_0_, bf16[3,288,384]{2,1,0:T(8,128)(2,1)S(1)} %get-tuple-element.89.refs_1_, ...), custom_call_target="tpu_custom_call" | custom-call | flops 1 | bytes 1 | tf_op jit(solution)/shard_map/pallas_call | solution.py:255
  93.9 1.3 %collective-permute-done.21.refs_1_ = bf16[128,512]{1,0:T(8,128)(2,1)S(1)} collective-permute-done((bf16[128,512]{1,0:T(8,128)(2,1)S(1)}, bf16[128,512]{1,0:T(8,128)(2,1)S(1)}, u32[]{:S(2)}, u32[]{:S(2)}) %collective-permute-start.21) | collective-permute-done | bytes 131104 | tf_op jit(solution)/shard_map/ppermute | solution.py:449
  95.8 3.3 %collective-permute-done.25.refs_1_ = bf16[256,512]{1,0:T(8,128)(2,1)S(1)} collective-permute-done((bf16[256,512]{1,0:T(8,128)(2,1)S(1)}, bf16[256,512]{1,0:T(8,128)(2,1)S(1)}, u32[]{:S(2)}, u32[]{:S(2)}) %collective-permute-start.25) | collective-permute-done | bytes 262176 | tf_op jit(solution)/shard_map/ppermute | solution.py:362
  99.8 0.7 shard_map.97
  100.5 2.5 %collective-permute-start.28 = (bf16[128,512]{1,0:T(8,128)(2,1)S(1)}, bf16[128,512]{1,0:T(8,128)(2,1)S(1)}, u32[]{:S(2)}, u32[]{:S(2)}) collective-permute-start(bf16[128,512]{1,0:T(8,128)(2,1)S(1)} %get-tuple-element.120), channel_id=1, source_target_pairs={{0,4},{1,6},{2,5},{3,7},{4,8},{5,10},{6,9},{7,11},{8,12},{9,14},{1... | collective-permute-start | bytes 393224 | tf_op jit(solution)/shard_map/ppermute | solution.py:449
  103.0 1.2 %collective-permute-start.29 = (bf16[128,512]{1,0:T(8,128)(2,1)S(1)}, bf16[128,512]{1,0:T(8,128)(2,1)S(1)}, u32[]{:S(2)}, u32[]{:S(2)}) collective-permute-start(bf16[128,512]{1,0:T(8,128)(2,1)S(1)} %get-tuple-element.122), channel_id=1, source_target_pairs={{0,6},{1,4},{2,7},{3,5},{4,10},{5,8},{6,11},{7,9},{8,14},{9,12},{1... | collective-permute-start | bytes 393224 | tf_op jit(solution)/shard_map/ppermute | solution.py:449
  105.5 3.6 %shard_map.98 = (bf16[4,384,1024]{2,1,0:T(8,128)(2,1)}, f32[8,128]{1,0:T(8,128)}) custom-call(bf16[4,96,384]{2,1,0:T(8,128)(2,1)S(1)} %get-tuple-element.74.refs_7_.refs_0_, bf16[4,80,384]{2,1,0:T(8,128)(2,1)S(1)} %get-tuple-element.81.refs_7_.refs_1_, bf16[4,80,384]{2,1,0:T(8,128)(2,1)S(1)} %get-tuple-element.94.refs_5_.refs_2_, ...), custom_call_target="tpu_custom_call" | custom-call | flops 1 | bytes 1 | tf_op jit(solution)/shard_map/pallas_call | solution.py:277
  109.1 1.0 collective-permute-done.28.refs_2_
  110.2 2.0 %collective-permute-done.29.refs_3_ = bf16[128,512]{1,0:T(8,128)(2,1)S(1)} collective-permute-done((bf16[128,512]{1,0:T(8,128)(2,1)S(1)}, bf16[128,512]{1,0:T(8,128)(2,1)S(1)}, u32[]{:S(2)}, u32[]{:S(2)}) %collective-permute-start.29) | collective-permute-done | bytes 131104 | tf_op jit(solution)/shard_map/ppermute | solution.py:449
  112.2 1.4 %shard_map.103 = bf16[128,1024]{1,0:T(8,128)(2,1)} custom-call(s32[3]{0:T(128)S(1)} %pad_add_fusion.place.refs_5_, bf16[128,512]{1,0:T(8,128)(2,1)S(1)} %get-tuple-element.115.stay, bf16[128,512]{1,0:T(8,128)(2,1)S(1)} %collective-permute-done.27.come, bf16[128,512]{1,0:T(8,128)(2,1)S(1)} %collective-permute-done.20.refs_0_, ...), custom_call_target="tpu_custom_call" | custom-call | flops 1 | bytes 1 | tf_op jit(solution)/shard_map/pallas_call | solution.py:292
  (49 shorter events, 7.2 us)
Async XLA Ops:
  2.1 1.0 copy-start.6
  3.1 1.0 copy-start.7
  4.9 14.1 %collective-permute-start.2 = (bf16[144,1024]{1,0:T(8,128)(2,1)S(1)}, bf16[144,1024]{1,0:T(8,128)(2,1)S(1)}, u32[]{:S(2)}, u32[]{:S(2)}) collective-permute-start(bf16[144,1024]{1,0:T(8,128)(2,1)S(1)} %get-tuple-element.63.refs_0_), channel_id=1, source_target_pairs={{0,4},{4,8},{8,12},{12,0},{1,5},{5,9},{9,13},{13,1},{2,6},{6,10},{... | collective-permute-start | bytes 884744 | tf_op jit(solution)/shard_map/ppermute | solution.py:362
  8.0 11.0 %collective-permute-start = (bf16[144,1024]{1,0:T(8,128)(2,1)S(1)}, bf16[144,1024]{1,0:T(8,128)(2,1)S(1)}, u32[]{:S(2)}, u32[]{:S(2)}) collective-permute-start(bf16[144,1024]{1,0:T(8,128)(2,1)S(1)} %get-tuple-element.66), channel_id=1, source_target_pairs={{0,2},{2,0},{1,3},{3,1},{4,6},{6,4},{5,7},{7,5},{8,10},{10,8},{9,1... | collective-permute-start | bytes 884744 | tf_op jit(solution)/shard_map/ppermute | solution.py:362
  9.5 1.9 %copy-start = (bf16[4,1024,384]{2,1,0:T(8,128)(2,1)S(1)}, bf16[4,1024,384]{2,1,0:T(8,128)(2,1)}, u32[]{:S(2)}) copy-start(bf16[4,1024,384]{2,1,0:T(8,128)(2,1)} %refs_3_.9) | copy-start | bytes 9437188
  11.4 1.9 %copy-start.2 = (bf16[4,1024,384]{2,1,0:T(8,128)(2,1)S(1)}, bf16[4,1024,384]{2,1,0:T(8,128)(2,1)}, u32[]{:S(2)}) copy-start(bf16[4,1024,384]{2,1,0:T(8,128)(2,1)} %refs_4_.15) | copy-start | bytes 9437188
  13.3 1.9 %copy-start.4 = (bf16[4,384,1024]{2,1,0:T(8,128)(2,1)S(1)}, bf16[4,384,1024]{2,1,0:T(8,128)(2,1)}, u32[]{:S(2)}) copy-start(bf16[4,384,1024]{2,1,0:T(8,128)(2,1)} %refs_6_.7) | copy-start | bytes 9437188
  15.2 7.6 %copy-start.1 = (bf16[4,1024,384]{2,1,0:T(8,128)(2,1)S(1)}, bf16[4,1024,384]{2,1,0:T(8,128)(2,1)}, u32[]{:S(2)}) copy-start(bf16[4,1024,384]{2,1,0:T(8,128)(2,1)} %refs_3_.9) | copy-start | bytes 9437188
  15.2 7.6 %copy-start.3 = (bf16[4,1024,384]{2,1,0:T(8,128)(2,1)S(1)}, bf16[4,1024,384]{2,1,0:T(8,128)(2,1)}, u32[]{:S(2)}) copy-start(bf16[4,1024,384]{2,1,0:T(8,128)(2,1)} %refs_4_.15) | copy-start | bytes 9437188
  15.2 7.6 %copy-start.5 = (bf16[4,384,1024]{2,1,0:T(8,128)(2,1)S(1)}, bf16[4,384,1024]{2,1,0:T(8,128)(2,1)}, u32[]{:S(2)}) copy-start(bf16[4,384,1024]{2,1,0:T(8,128)(2,1)} %refs_6_.7) | copy-start | bytes 9437188
  18.4 9.9 %collective-permute-start.5 = (bf16[3,160,384]{2,1,0:T(8,128)(2,1)S(1)}, bf16[3,160,384]{2,1,0:T(8,128)(2,1)S(1)}, u32[]{:S(2)}, u32[]{:S(2)}) collective-permute-start(bf16[3,160,384]{2,1,0:T(8,128)(2,1)S(1)} %get-tuple-element.70.refs_2_), channel_id=1, source_target_pairs={{0,2},{2,0},{1,3},{3,1},{4,6},{6,4},{5,7},{7,5},{8,10},{10,8},{9,1... | collective-permute-start | bytes 1105928 | tf_op jit(solution)/shard_map/ppermute | solution.py:362
  19.0 3.7 %collective-permute-start.3 = (bf16[144,1024]{1,0:T(8,128)(2,1)S(1)}, bf16[144,1024]{1,0:T(8,128)(2,1)S(1)}, u32[]{:S(2)}, u32[]{:S(2)}) collective-permute-start(bf16[144,1024]{1,0:T(8,128)(2,1)S(1)} %collective-permute-done.2.refs_0_), channel_id=1, source_target_pairs={{0,1},{1,0},{2,3},{3,2},{4,5},{5,4},{6,7},{7,6},{8,9},{9,8},{10,11... | collective-permute-start | bytes 884744 | tf_op jit(solution)/shard_map/ppermute | solution.py:362
  19.1 3.7 %collective-permute-start.1 = (bf16[144,1024]{1,0:T(8,128)(2,1)S(1)}, bf16[144,1024]{1,0:T(8,128)(2,1)S(1)}, u32[]{:S(2)}, u32[]{:S(2)}) collective-permute-start(bf16[144,1024]{1,0:T(8,128)(2,1)S(1)} %collective-permute-done.refs_0_), channel_id=1, source_target_pairs={{0,1},{1,0},{2,3},{3,2},{4,5},{5,4},{6,7},{7,6},{8,9},{9,8},{10,11... | collective-permute-start | bytes 884744 | tf_op jit(solution)/shard_map/ppermute | solution.py:362
  19.6 11.7 %collective-permute-start.6 = (bf16[144,1024]{1,0:T(8,128)(2,1)S(1)}, bf16[144,1024]{1,0:T(8,128)(2,1)S(1)}, u32[]{:S(2)}, u32[]{:S(2)}) collective-permute-start(bf16[144,1024]{1,0:T(8,128)(2,1)S(1)} %collective-permute-done.refs_0_), channel_id=1, source_target_pairs={{0,4},{4,8},{8,12},{12,0},{1,5},{5,9},{9,13},{13,1},{2,6},{6,10},{... | collective-permute-start | bytes 884744 | tf_op jit(solution)/shard_map/ppermute | solution.py:362
  21.1 15.5 %collective-permute-start.9 = (bf16[144,1024]{1,0:T(8,128)(2,1)S(1)}, bf16[144,1024]{1,0:T(8,128)(2,1)S(1)}, u32[]{:S(2)}, u32[]{:S(2)}) collective-permute-start(bf16[144,1024]{1,0:T(8,128)(2,1)S(1)} %collective-permute-done.2.refs_0_), channel_id=1, source_target_pairs={{0,4},{4,8},{8,12},{12,0},{1,5},{5,9},{9,13},{13,1},{2,6},{6,10},{... | collective-permute-start | bytes 884744 | tf_op jit(solution)/shard_map/ppermute | solution.py:362
  26.0 14.5 %collective-permute-start.4 = (bf16[3,160,384]{2,1,0:T(8,128)(2,1)S(1)}, bf16[3,160,384]{2,1,0:T(8,128)(2,1)S(1)}, u32[]{:S(2)}, u32[]{:S(2)}) collective-permute-start(bf16[3,160,384]{2,1,0:T(8,128)(2,1)S(1)} %get-tuple-element.71.refs_4_), channel_id=1, source_target_pairs={{0,2},{2,0},{1,3},{3,1},{4,6},{6,4},{5,7},{7,5},{8,10},{10,8},{9,1... | collective-permute-start | bytes 1105928 | tf_op jit(solution)/shard_map/ppermute | solution.py:362
  31.2 5.4 %collective-permute-start.7 = (bf16[144,1024]{1,0:T(8,128)(2,1)S(1)}, bf16[144,1024]{1,0:T(8,128)(2,1)S(1)}, u32[]{:S(2)}, u32[]{:S(2)}) collective-permute-start(bf16[144,1024]{1,0:T(8,128)(2,1)S(1)} %collective-permute-done.6.refs_1_), channel_id=1, source_target_pairs={{0,1},{1,0},{2,3},{3,2},{4,5},{5,4},{6,7},{7,6},{8,9},{9,8},{10,11... | collective-permute-start | bytes 884744 | tf_op jit(solution)/shard_map/ppermute | solution.py:362
  36.7 9.9 %collective-permute-start.10 = (bf16[144,1024]{1,0:T(8,128)(2,1)S(1)}, bf16[144,1024]{1,0:T(8,128)(2,1)S(1)}, u32[]{:S(2)}, u32[]{:S(2)}) collective-permute-start(bf16[144,1024]{1,0:T(8,128)(2,1)S(1)} %collective-permute-done.6.refs_1_), channel_id=1, source_target_pairs={{0,4},{4,8},{8,12},{12,0},{1,5},{5,9},{9,13},{13,1},{2,6},{6,10},{... | collective-permute-start | bytes 884744 | tf_op jit(solution)/shard_map/ppermute | solution.py:362
  40.5 16.1 %collective-permute-start.8 = (bf16[3,288,384]{2,1,0:T(8,128)(2,1)S(1)}, bf16[3,288,384]{2,1,0:T(8,128)(2,1)S(1)}, u32[]{:S(2)}, u32[]{:S(2)}) collective-permute-start(bf16[3,288,384]{2,1,0:T(8,128)(2,1)S(1)} %get-tuple-element.76.refs_1_), channel_id=1, source_target_pairs={{0,2},{2,0},{1,3},{3,1},{4,6},{6,4},{5,7},{7,5},{8,10},{10,8},{9,1... | collective-permute-start | bytes 1990664 | tf_op jit(solution)/shard_map/ppermute | solution.py:362
  46.6 1.6 %collective-permute-start.11 = (bf16[144,1024]{1,0:T(8,128)(2,1)S(1)}, bf16[144,1024]{1,0:T(8,128)(2,1)S(1)}, u32[]{:S(2)}, u32[]{:S(2)}) collective-permute-start(bf16[144,1024]{1,0:T(8,128)(2,1)S(1)} %collective-permute-done.9.refs_0_), channel_id=1, source_target_pairs={{0,1},{1,0},{2,3},{3,2},{4,5},{5,4},{6,7},{7,6},{8,9},{9,8},{10,11... | collective-permute-start | bytes 884744 | tf_op jit(solution)/shard_map/ppermute | solution.py:362
  48.2 1.6 %collective-permute-start.12 = (bf16[144,1024]{1,0:T(8,128)(2,1)S(1)}, bf16[144,1024]{1,0:T(8,128)(2,1)S(1)}, u32[]{:S(2)}, u32[]{:S(2)}) collective-permute-start(bf16[144,1024]{1,0:T(8,128)(2,1)S(1)} %collective-permute-done.10.refs_1_), channel_id=1, source_target_pairs={{0,1},{1,0},{2,3},{3,2},{4,5},{5,4},{6,7},{7,6},{8,9},{9,8},{10,11... | collective-permute-start | bytes 884744 | tf_op jit(solution)/shard_map/ppermute | solution.py:362
  48.3 13.5 %collective-permute-start.14 = (bf16[144,1024]{1,0:T(8,128)(2,1)S(1)}, bf16[144,1024]{1,0:T(8,128)(2,1)S(1)}, u32[]{:S(2)}, u32[]{:S(2)}) collective-permute-start(bf16[144,1024]{1,0:T(8,128)(2,1)S(1)} %collective-permute-done.9.refs_0_), channel_id=1, source_target_pairs={{0,4},{4,8},{8,12},{12,0},{1,5},{5,9},{9,13},{13,1},{2,6},{6,10},{... | collective-permute-start | bytes 884744 | tf_op jit(solution)/shard_map/ppermute | solution.py:362
  48.9 16.8 %collective-permute-start.15 = (bf16[144,1024]{1,0:T(8,128)(2,1)S(1)}, bf16[144,1024]{1,0:T(8,128)(2,1)S(1)}, u32[]{:S(2)}, u32[]{:S(2)}) collective-permute-start(bf16[144,1024]{1,0:T(8,128)(2,1)S(1)} %collective-permute-done.10.refs_1_), channel_id=1, source_target_pairs={{0,4},{4,8},{8,12},{12,0},{1,5},{5,9},{9,13},{13,1},{2,6},{6,10},{... | collective-permute-start | bytes 884744 | tf_op jit(solution)/shard_map/ppermute | solution.py:362
  56.6 16.1 %collective-permute-start.13 = (bf16[3,288,384]{2,1,0:T(8,128)(2,1)S(1)}, bf16[3,288,384]{2,1,0:T(8,128)(2,1)S(1)}, u32[]{:S(2)}, u32[]{:S(2)}) collective-permute-start(bf16[3,288,384]{2,1,0:T(8,128)(2,1)S(1)} %get-tuple-element.83.refs_1_), channel_id=1, source_target_pairs={{0,2},{2,0},{1,3},{3,1},{4,6},{6,4},{5,7},{7,5},{8,10},{10,8},{9,1... | collective-permute-start | bytes 1990664 | tf_op jit(solution)/shard_map/ppermute | solution.py:362
  65.7 1.6 %collective-permute-start.16 = (bf16[144,1024]{1,0:T(8,128)(2,1)S(1)}, bf16[144,1024]{1,0:T(8,128)(2,1)S(1)}, u32[]{:S(2)}, u32[]{:S(2)}) collective-permute-start(bf16[144,1024]{1,0:T(8,128)(2,1)S(1)} %collective-permute-done.14.refs_0_), channel_id=1, source_target_pairs={{0,1},{1,0},{2,3},{3,2},{4,5},{5,4},{6,7},{7,6},{8,9},{9,8},{10,11... | collective-permute-start | bytes 884744 | tf_op jit(solution)/shard_map/ppermute | solution.py:362
  67.3 1.6 %collective-permute-start.17 = (bf16[144,1024]{1,0:T(8,128)(2,1)S(1)}, bf16[144,1024]{1,0:T(8,128)(2,1)S(1)}, u32[]{:S(2)}, u32[]{:S(2)}) collective-permute-start(bf16[144,1024]{1,0:T(8,128)(2,1)S(1)} %collective-permute-done.15.refs_1_), channel_id=1, source_target_pairs={{0,1},{1,0},{2,3},{3,2},{4,5},{5,4},{6,7},{7,6},{8,9},{9,8},{10,11... | collective-permute-start | bytes 884744 | tf_op jit(solution)/shard_map/ppermute | solution.py:362
  72.7 17.4 %collective-permute-start.18 = (bf16[3,288,384]{2,1,0:T(8,128)(2,1)S(1)}, bf16[3,288,384]{2,1,0:T(8,128)(2,1)S(1)}, u32[]{:S(2)}, u32[]{:S(2)}) collective-permute-start(bf16[3,288,384]{2,1,0:T(8,128)(2,1)S(1)} %get-tuple-element.89.refs_1_), channel_id=1, source_target_pairs={{0,2},{2,0},{1,3},{3,1},{4,6},{6,4},{5,7},{7,5},{8,10},{10,8},{9,1... | collective-permute-start | bytes 1990664 | tf_op jit(solution)/shard_map/ppermute | solution.py:362
  78.0 1.6 %collective-permute-start.19 = (bf16[256,512]{1,0:T(8,128)(2,1)S(1)}, bf16[256,512]{1,0:T(8,128)(2,1)S(1)}, u32[]{:S(2)}, u32[]{:S(2)}) collective-permute-start(bf16[256,512]{1,0:T(8,128)(2,1)S(1)} %get-tuple-element.91), channel_id=1, source_target_pairs={{0,1},{1,0},{2,3},{3,2},{4,5},{5,4},{6,7},{7,6},{8,9},{9,8},{10,11... | collective-permute-start | bytes 786440 | tf_op jit(solution)/shard_map/ppermute | solution.py:362
  78.1 5.8 %collective-permute-start.24 = (bf16[256,512]{1,0:T(8,128)(2,1)S(1)}, bf16[256,512]{1,0:T(8,128)(2,1)S(1)}, u32[]{:S(2)}, u32[]{:S(2)}) collective-permute-start(bf16[256,512]{1,0:T(8,128)(2,1)S(1)} %get-tuple-element.111), channel_id=1, source_target_pairs={{0,1},{1,0},{2,3},{3,2},{4,5},{5,4},{6,7},{7,6},{8,9},{9,8},{10,11... | collective-permute-start | bytes 786440 | tf_op jit(solution)/shard_map/ppermute | solution.py:362
  80.3 13.5 %collective-permute-start.20 = (bf16[128,512]{1,0:T(8,128)(2,1)S(1)}, bf16[128,512]{1,0:T(8,128)(2,1)S(1)}, u32[]{:S(2)}, u32[]{:S(2)}) collective-permute-start(bf16[128,512]{1,0:T(8,128)(2,1)S(1)} %get-tuple-element.92), channel_id=1, source_target_pairs={{0,8},{1,10},{2,9},{3,11},{4,12},{5,14},{6,13},{7,15},{8,0},{9,2},... | collective-permute-start | bytes 393224 | tf_op jit(solution)/shard_map/ppermute | solution.py:449
  80.8 14.3 %collective-permute-start.21 = (bf16[128,512]{1,0:T(8,128)(2,1)S(1)}, bf16[128,512]{1,0:T(8,128)(2,1)S(1)}, u32[]{:S(2)}, u32[]{:S(2)}) collective-permute-start(bf16[128,512]{1,0:T(8,128)(2,1)S(1)} %get-tuple-element.93), channel_id=1, source_target_pairs={{0,10},{1,8},{2,11},{3,9},{4,14},{5,12},{6,15},{7,13},{8,2},{9,0},... | collective-permute-start | bytes 393224 | tf_op jit(solution)/shard_map/ppermute | solution.py:449
  83.9 11.2 %collective-permute-start.23 = (bf16[256,512]{1,0:T(8,128)(2,1)S(1)}, bf16[256,512]{1,0:T(8,128)(2,1)S(1)}, u32[]{:S(2)}, u32[]{:S(2)}) collective-permute-start(bf16[256,512]{1,0:T(8,128)(2,1)S(1)} %get-tuple-element.109), channel_id=1, source_target_pairs={{0,1},{1,0},{2,3},{3,2},{4,5},{5,4},{6,7},{7,6},{8,9},{9,8},{10,11... | collective-permute-start | bytes 786440 | tf_op jit(solution)/shard_map/ppermute | solution.py:362
  84.6 14.5 %collective-permute-start.25 = (bf16[256,512]{1,0:T(8,128)(2,1)S(1)}, bf16[256,512]{1,0:T(8,128)(2,1)S(1)}, u32[]{:S(2)}, u32[]{:S(2)}) collective-permute-start(bf16[256,512]{1,0:T(8,128)(2,1)S(1)} %shard_map.100), channel_id=1, source_target_pairs={{0,12},{4,0},{8,4},{12,8},{1,13},{5,1},{9,5},{13,9},{2,14},{6,2},{... | collective-permute-start | bytes 786440 | tf_op jit(solution)/shard_map/ppermute | solution.py:362
  95.1 4.7 %collective-permute-start.22 = (bf16[256,512]{1,0:T(8,128)(2,1)S(1)}, bf16[256,512]{1,0:T(8,128)(2,1)S(1)}, u32[]{:S(2)}, u32[]{:S(2)}) collective-permute-start(bf16[256,512]{1,0:T(8,128)(2,1)S(1)} %get-tuple-element.98), channel_id=1, source_target_pairs={{0,1},{1,0},{2,3},{3,2},{4,5},{5,4},{6,7},{7,6},{8,9},{9,8},{10,11... | collective-permute-start | bytes 786440 | tf_op jit(solution)/shard_map/ppermute | solution.py:362
  99.7 5.2 %collective-permute-start.26 = (bf16[128,512]{1,0:T(8,128)(2,1)S(1)}, bf16[128,512]{1,0:T(8,128)(2,1)S(1)}, u32[]{:S(2)}, u32[]{:S(2)}) collective-permute-start(bf16[128,512]{1,0:T(8,128)(2,1)S(1)} %get-tuple-element.114), channel_id=1, source_target_pairs={{0,2},{2,0},{1,3},{3,1},{4,6},{6,4},{5,7},{7,5},{8,10},{10,8},{9,1... | collective-permute-start | bytes 393224 | tf_op jit(solution)/shard_map/ppermute | solution.py:362
  100.5 9.7 %collective-permute-start.28 = (bf16[128,512]{1,0:T(8,128)(2,1)S(1)}, bf16[128,512]{1,0:T(8,128)(2,1)S(1)}, u32[]{:S(2)}, u32[]{:S(2)}) collective-permute-start(bf16[128,512]{1,0:T(8,128)(2,1)S(1)} %get-tuple-element.120), channel_id=1, source_target_pairs={{0,4},{1,6},{2,5},{3,7},{4,8},{5,10},{6,9},{7,11},{8,12},{9,14},{1... | collective-permute-start | bytes 393224 | tf_op jit(solution)/shard_map/ppermute | solution.py:449
  103.0 9.2 %collective-permute-start.29 = (bf16[128,512]{1,0:T(8,128)(2,1)S(1)}, bf16[128,512]{1,0:T(8,128)(2,1)S(1)}, u32[]{:S(2)}, u32[]{:S(2)}) collective-permute-start(bf16[128,512]{1,0:T(8,128)(2,1)S(1)} %get-tuple-element.122), channel_id=1, source_target_pairs={{0,6},{1,4},{2,7},{3,5},{4,10},{5,8},{6,11},{7,9},{8,14},{9,12},{1... | collective-permute-start | bytes 393224 | tf_op jit(solution)/shard_map/ppermute | solution.py:449
  105.5 6.8 %collective-permute-start.27 = (bf16[128,512]{1,0:T(8,128)(2,1)S(1)}, bf16[128,512]{1,0:T(8,128)(2,1)S(1)}, u32[]{:S(2)}, u32[]{:S(2)}) collective-permute-start(bf16[128,512]{1,0:T(8,128)(2,1)S(1)} %get-tuple-element.116), channel_id=1, source_target_pairs={{0,1},{1,0},{2,3},{3,2},{4,5},{5,4},{6,7},{7,6},{8,9},{9,8},{10,11... | collective-permute-start | bytes 393224 | tf_op jit(solution)/shard_map/ppermute | solution.py:362
